TPU v7x, 256 devices: a whole 4x4x8 slice. The times are simulated.
256 devices in a mesh: expert: 64 (over x, z, core), tensor: 4 (over y).
Axes of the slice: x: 4, y: 4, z: 8, core: 2. Of those that a mesh axis runs over, the one named last changes fastest.
Arguments:
- query_latent: bfloat16 [2048, 128, 512], P('expert', 'tensor'), may hold values from -82 to 82
- query_rope: bfloat16 [2048, 8192], P('expert', 'tensor'), may hold values from -5 to 5
- cache_latent: bfloat16 [2048, 128, 512], P('expert'), may hold values from -5 to 5
- cache_rope: bfloat16 [2048, 64, 128], P('expert'), may hold values from -5 to 5
- cache_len: int32 [2048], P('expert'), may hold values from 2 to 128
- moe_input: bfloat16 [2048, 3584], P(('expert', 'tensor')), may hold values from -6 to 6
- routes: int32 [2048, 8], P(('expert', 'tensor')), may hold values from 0 to 63, all different within a row; in each aligned block of 8 rows (0 to 7, 8 to 15, ...) at most 2 rows name the same one
- gate_weights: float32 [2048, 8], P(('expert', 'tensor')), may hold values from 0.1 to 0.5
- w_gate: bfloat16 [64, 3584, 1024], P('expert', None, 'tensor'), may hold values from -0.09375 to 0.09375
- w_up: bfloat16 [64, 3584, 1024], P('expert', None, 'tensor'), may hold values from -0.09375 to 0.09375
- w_down: bfloat16 [64, 1024, 3584], P('expert', 'tensor'), may hold values from -0.1875 to 0.1875
Outputs:
- context: bfloat16 [2048, 128, 512], P(('expert', 'tensor'))
- moe_output: bfloat16 [2048, 3584], P(('expert', 'tensor'))
Inputs may be any that keep to these rules, and one draw needn't show every extreme that they name: `routes`: each row names 8 different experts; in each aligned block of 8 rows (the rows of one device) no expert is named by more than 2 rows.
All inputs are finite; a program needn't handle non-finite values.
Results may differ from a plain program's by a relative error of at most 0.012.
Values may be sent and summed in bfloat16 or wider, within the bound.
No kernel may reach another device: no remote copies, remote signals or barrier semaphores. Data moves between devices by JAX's collectives and lax.ppermute only.
A program may use at most 128 MiB of HBM per device.

v0:
```python
import jax
import jax.numpy as jnp
from jax import lax
from jax.sharding import PartitionSpec as P

score_scale = 192.0 ** (-0.5)


def attend(query_latent, query_rope, cache_latent, cache_rope, cache_len):
    count, heads, latent = query_latent.shape
    rotary_width = cache_rope.shape[1]
    positions = cache_latent.shape[1]
    rotary = query_rope.reshape(count, heads, rotary_width)
    scores = jnp.einsum(
        "rhl,rpl->rhp", query_latent, cache_latent, preferred_element_type=jnp.float32
    )
    scores = scores + jnp.einsum(
        "rhe,rep->rhp", rotary, cache_rope, preferred_element_type=jnp.float32
    )
    scores = scores * score_scale
    valid = jnp.arange(positions, dtype=jnp.int32)[None, None, :] < cache_len[:, None, None]
    scores = jnp.where(valid, scores, -1e30)
    highest = jnp.max(scores, axis=-1, keepdims=True)
    powers = jnp.exp(scores - highest)
    weights = (powers / jnp.sum(powers, axis=-1, keepdims=True)).astype(jnp.bfloat16)
    mixed = jnp.einsum("rhp,rpl->rhl", weights, cache_latent, preferred_element_type=jnp.float32)
    return mixed.astype(jnp.bfloat16)


def place_rows(route_block, values, experts, capacity):
    chosen = route_block.shape[1]
    flat = route_block.reshape(-1)
    onehot = (flat[:, None] == jnp.arange(experts, dtype=jnp.int32)[None, :]).astype(jnp.int32)
    earlier = jnp.cumsum(onehot, axis=0) - onehot
    position = jnp.sum(earlier * onehot, axis=1)
    targets = flat * capacity + position
    copies = jnp.repeat(values, chosen, axis=0)
    buffer = jnp.zeros((experts * capacity, values.shape[1]), values.dtype).at[targets].set(copies)
    return (buffer.reshape(experts, capacity, values.shape[1]), targets)


def expert_hidden(block, w_gate, w_up):
    gate = jnp.einsum("nekd,edf->nekf", block, w_gate, preferred_element_type=jnp.float32)
    upper = jnp.einsum("nekd,edf->nekf", block, w_up, preferred_element_type=jnp.float32)
    return (jax.nn.silu(gate) * upper).astype(jnp.bfloat16)


def per_device(
    query_latent,
    query_rope,
    cache_latent,
    cache_rope,
    cache_len,
    moe_input,
    routes,
    gate_weights,
    w_gate,
    w_up,
    w_down,
):
    tensor_count = lax.axis_size("tensor")
    expert_count = lax.axis_size("expert")
    group_size = cache_latent.shape[0]
    own_rows = group_size // tensor_count
    local_context = attend(query_latent, query_rope, cache_latent, cache_rope, cache_len)
    context = lax.all_to_all(local_context, "tensor", split_axis=0, concat_axis=1, tiled=True)
    local_experts = w_gate.shape[0]
    experts = local_experts * expert_count
    chosen = routes.shape[1]
    width = moe_input.shape[1]
    capacity = min(own_rows, max(2, 2 * own_rows * chosen // experts))
    group_input, group_routes = (
        lax.all_gather(moe_input, "tensor", axis=0, tiled=True),
        lax.all_gather(routes, "tensor", axis=0, tiled=True),
    )
    group_capacity = capacity * tensor_count
    outgoing, targets = place_rows(group_routes, group_input, experts, group_capacity)
    received = lax.all_to_all(outgoing, "expert", split_axis=0, concat_axis=0, tiled=True)
    number = received.shape[1]
    block = received.reshape(expert_count, local_experts, number, width)
    hidden = expert_hidden(block, w_gate, w_up)
    partial_out = jnp.einsum("nekf,efd->nekd", hidden, w_down, preferred_element_type=jnp.float32)
    partial_out = partial_out.reshape(experts, number, width)
    returned = lax.all_to_all(partial_out, "expert", split_axis=0, concat_axis=0, tiled=True)
    per_choice = returned.reshape(experts * group_capacity, width)[targets]
    per_choice = per_choice.reshape(group_size, chosen, width)
    summed = lax.psum_scatter(per_choice, "tensor", scatter_dimension=0, tiled=True)
    expert_out = summed.astype(jnp.bfloat16)
    moe_output = jnp.sum(gate_weights[:, :, None] * expert_out.astype(jnp.float32), axis=1).astype(
        jnp.bfloat16
    )
    return (context, moe_output)


def solution(mesh):
    return jax.shard_map(
        per_device,
        mesh=mesh,
        in_specs=(
            P("expert", "tensor", None),
            P("expert", "tensor"),
            P("expert", None, None),
            P("expert", None, None),
            P("expert"),
            P(("expert", "tensor"), None),
            P(("expert", "tensor"), None),
            P(("expert", "tensor"), None),
            P("expert", None, "tensor"),
            P("expert", None, "tensor"),
            P("expert", "tensor", None),
        ),
        out_specs=(P(("expert", "tensor"), None, None), P(("expert", "tensor"), None)),
        check_vma=False,
    )
```

profile of v0, /device:TPU:1, one launch (start us, length us, event | category | flops | bytes accessed | tf_op | source)
XLA Modules:
  0.0 388.8 jit_solution(122447445027649742)
XLA Ops:
  7.2 0.0 copy-start
  7.2 10.7 %all_gather.6 = s32[32,8]{1,0:T(8,128)S(1)} all-gather(s32[8,8]{1,0:T(8,128)} %param.17), channel_id=1, replica_groups=mesh['expert'=64,'tensor'=4] {'tensor'}, dimensions={0}, use_global_device_ids=true | all-gather | bytes 1280 | tf_op jit(solution)/shard_map/all_gather | solution.py:74
  17.8 0.1 eq.29
  17.9 0.1 eq.25
  18.0 0.6 reduce-window.6
  18.7 0.2 slice_reduce_fusion
  18.9 0.1 mul.45
  19.0 9.5 %all_gather.7 = bf16[32,3584]{1,0:T(8,128)(2,1)S(1)} all-gather(bf16[8,3584]{1,0:T(8,128)(2,1)} %param.16), channel_id=1, replica_groups=mesh['expert'=64,'tensor'=4] {'tensor'}, dimensions={0}, use_global_device_ids=true | all-gather | bytes 286720 | tf_op jit(solution)/shard_map/all_gather | solution.py:73
  28.5 0.1 fusion.41
  28.6 5.4 %scatter_custom_fusion = bf16[512,3584]{1,0:T(8,128)(2,1)} fusion(s32[256]{0:T(256)S(1)} %bitcast.93, bf16[]{:T(256)} %constant.6.clone.1, bf16[32,3584]{1,0:T(8,128)(2,1)S(1)} %all_gather.7), kind=kCustom, calls=%fused_computation.9 | custom fusion | bytes 3899394 | tf_op jit(solution)/shard_map/scatter | solution.py:38
  34.1 102.8 %all_to_all.28 = bf16[64,8,3584]{2,1,0:T(8,128)(2,1)S(1)} all-to-all(bf16[64,8,3584]{2,1,0:T(8,128)(2,1)} %bitcast.89), channel_id=1, replica_groups=mesh['expert'=64,'tensor'=4] {'expert'}, dimensions={0} | all-to-all | bytes 7340032 | tf_op jit(solution)/shard_map/all_to_all | solution.py:78
  136.8 1.8 copy-done.1
  138.6 1.1 fusion.12
  139.8 9.5 %fusion.1 = f32[64,8,3584]{2,1,0:T(8,128)} fusion(bf16[1,256,3584]{2,1,0:T(8,128)(2,1)S(1)} %copy-done, bf16[64,8,3584]{2,1,0:T(8,128)(2,1)} %copy-done.1, bf16[1,3584,256]{2,1,0:T(8,128)(2,1)} %param.20, f32[64,1,8,256]{3,2,0,1:T(8,128)S(1)} %fusion.12), kind=kOutput, calls=%fused_computation.3 | convolution fusion | flops 1879834624 | bytes 15204352 | tf_op jit(solution)/shard_map/nekf,efd->nekd/dot_general | solution.py:82
  149.3 6.3 %all-to-all-start.2 = ((f32[64,8,3584]{2,1,0:T(8,128)}), f32[64,8,3584]{2,1,0:T(8,128)}, u32[]{:S(2)}, u32[]{:S(2)}) async-start(f32[64,8,3584]{2,1,0:T(8,128)} %fusion.1), calls=%async_computation.2 | async-start | bytes 14680064 | tf_op jit(solution)/shard_map/all_to_all | solution.py:84
  155.6 0.2 reduce-scatter.2.cloned.1.call-start
  155.9 163.1 %all-to-all-done.2 = f32[64,8,3584]{2,1,0:T(8,128)} async-done(((f32[64,8,3584]{2,1,0:T(8,128)}), f32[64,8,3584]{2,1,0:T(8,128)}, u32[]{:S(2)}, u32[]{:S(2)}) %all-to-all-start.2) | async-done | bytes 7340064 | tf_op jit(solution)/shard_map/all_to_all | solution.py:84
  318.9 8.4 %gather_fusion = f32[256,3584]{1,0:T(8,128)} fusion(f32[512,3584]{1,0:T(8,128)} %bitcast.23, s32[1024]{0:T(1024)S(1)} %pad_clamp_fusion), kind=kCustom, calls=%fused_computation | custom fusion | bytes 7341056 | tf_op jit(solution)/shard_map/gather | solution.py:85
  327.3 0.0 reduce-scatter.2.cloned.1.call-update
  327.3 0.9 copy-done.3
  328.2 0.2 reshape.110
  328.4 0.0 copy-done.5
  328.5 0.1 iota_compare_fusion.2
  328.5 0.3 fusion.46
  328.8 4.0 %fusion.22 = f32[32,32,128]{2,1,0:T(8,128)S(1)} fusion(f32[32,32,128]{2,1,0:T(8,128)S(1)} %fusion.46, bf16[32,32,512]{2,1,0:T(8,128)(2,1)} %param.11, bf16[32,128,512]{2,1,0:T(8,128)(2,1)} %param.13, pred[32,128]{1,0:T(8,128)(4,1)S(1)} %iota_compare_fusion.2), kind=kOutput, calls=%fused_computation.20 | convolution fusion | flops 134610944 | bytes 6295552 | tf_op jit(solution)/shard_map/rhl,rpl->rhp/dot_general | solution.py:14
  332.8 0.3 fusion.45
  333.2 0.0 copy-start.4
  333.2 4.5 %convolution_convert_fusion = bf16[32,32,512]{2,1,0:T(8,128)(2,1)S(1)} fusion(bf16[32,128,512]{2,1,0:T(8,128)(2,1)} %param.13, f32[32,32]{1,0:T(8,128)S(1)} %fusion.45, f32[32,32,128]{2,1,0:T(8,128)S(1)} %fusion.22), kind=kOutput, calls=%fused_computation.12 | convolution fusion | flops 135136384 | bytes 5771264 | tf_op jit(solution)/shard_map/rhp,rpl->rhl/dot_general | solution.py:26
  337.7 29.6 %all_to_all.29 = bf16[32,32,512]{2,1,0:T(8,128)(2,1)S(1)} all-to-all(bf16[32,32,512]{2,1,0:T(8,128)(2,1)S(1)} %convolution_convert_fusion), channel_id=1, replica_groups=mesh['expert'=64,'tensor'=4] {'tensor'}, dimensions={0} | all-to-all | bytes 2097152 | tf_op jit(solution)/shard_map/all_to_all | solution.py:66
  367.3 1.0 copy.14
  368.3 11.5 %reduce-scatter.2.cloned.1.call-done = f32[8,8,3584]{2,1,0:T(8,128)} async-done(((f32[32,8,3584]{2,1,0:T(8,128)}), f32[8,8,3584]{2,1,0:T(8,128)}) %reduce-scatter.2.cloned.1.call-update) | async-done | bytes 917520 | tf_op jit(solution)/shard_map/reduce_scatter | solution.py:87
  379.8 2.1 multiply_reduce_fusion
  (15 shorter events, 0.1 us)
Async XLA Ops:
  7.2 132.6 %copy-start = (bf16[1,256,3584]{2,1,0:T(8,128)(2,1)S(1)}, bf16[1,256,3584]{2,1,0:T(8,128)(2,1)}, u32[]{:S(2)}) copy-start(bf16[1,256,3584]{2,1,0:T(8,128)(2,1)} %param.21) | copy-start | bytes 5505028
  34.0 104.6 %copy-start.6 = (bf16[1,3584,256]{2,1,0:T(8,128)(2,1)S(1)}, bf16[1,3584,256]{2,1,0:T(8,128)(2,1)}, u32[]{:S(2)}) copy-start(bf16[1,3584,256]{2,1,0:T(8,128)(2,1)} %param.19) | copy-start | bytes 5505028
  136.8 1.8 copy-start.1
  149.3 169.6 %all-to-all-start.2 = ((f32[64,8,3584]{2,1,0:T(8,128)}), f32[64,8,3584]{2,1,0:T(8,128)}, u32[]{:S(2)}, u32[]{:S(2)}) async-start(f32[64,8,3584]{2,1,0:T(8,128)} %fusion.1), calls=%async_computation.2 | async-start | bytes 14680064 | tf_op jit(solution)/shard_map/all_to_all | solution.py:84
  155.6 224.2 %reduce-scatter.2.cloned.1.call-start = ((), (), s32[]{:S(2)}) async-start(), calls=%async_computation.4 | async-start | bytes 4587520 | tf_op jit(solution)/shard_map/reduce_scatter | solution.py:87
  327.3 0.9 copy-start.3
  327.3 1.2 copy-start.5
  327.3 1.2 copy-start.2
  333.2 46.7 %copy-start.4 = (f32[8,8]{1,0:T(8,128)S(1)}, f32[8,8]{1,0:T(8,128)}, u32[]{:S(2)}) copy-start(f32[8,8]{1,0:T(8,128)} %param.18) | copy-start | bytes 772
Sparse Core Ops, SparseCore 0:
  327.4 52.3 reduce-scatter.1
where the time goes:
time: 389 us
  waiting for transfers between devices  175 us (45%)
  blocking collectives  153 us (39%)
  matrix products  19.5 us (5%)
  local copies, waits for them, and re-layouts  18.2 us (5%)
  between operations  14.1 us (4%)
  starting transfers between devices  6.51 us (2%)
    all_to_all x1, waiting for transfers between devices, per_device(): lax.all_to_all(partial_out, 'expert', split_axis=0, concat_axis=0, tiled=...  163 us
    all_to_all x1, blocking collectives, per_device(): lax.all_to_all(outgoing, 'expert', split_axis=0, concat_axis=0, tiled=True)  103 us
    all_to_all x1, blocking collectives, per_device(): lax.all_to_all(local_context, 'tensor', split_axis=0, concat_axis=1, tile...  29.6 us
    reduce_scatter x1, waiting for transfers between devices, per_device(): lax.psum_scatter(per_choice, 'tensor', scatter_dimension=0, tiled=True)  11.5 us
    all_gather x1, blocking collectives, per_device(): lax.all_gather(routes, 'tensor', axis=0, tiled=True)  10.7 us
    dot_general x1, matrix products, per_device(): jnp.einsum('nekf,efd->nekd', hidden, w_down, preferred_element_type=jnp.f...  9.55 us
    all_gather x1, blocking collectives, per_device(): lax.all_gather(moe_input, 'tensor', axis=0, tiled=True)  9.52 us
    gather x1, local copies, waits for them, and re-layouts, per_device(): per_choice = returned.reshape(experts * group_capacity, width)[targets]  8.35 us
  transfers between devices with their start and end apart: 2, of which 2 were waited for; matrix products, arithmetic and copies ran while one was open for 3% of the time, Pallas kernels for 0%

commit v1 on v0

v1 whole, which is shorter than its diff:
```python
import jax
import jax.numpy as jnp
from jax import lax
from jax.sharding import PartitionSpec as P

score_scale = 192.0 ** (-0.5)
CAP = 2


def attend(query_latent, query_rope, cache_latent, cache_rope, cache_len):
    count, heads, latent = query_latent.shape
    rotary_width = cache_rope.shape[1]
    positions = cache_latent.shape[1]
    rotary = query_rope.reshape(count, heads, rotary_width)
    scores = jnp.einsum(
        "rhl,rpl->rhp", query_latent, cache_latent, preferred_element_type=jnp.float32
    )
    scores = scores + jnp.einsum(
        "rhe,rep->rhp", rotary, cache_rope, preferred_element_type=jnp.float32
    )
    scores = scores * score_scale
    valid = jnp.arange(positions, dtype=jnp.int32)[None, None, :] < cache_len[:, None, None]
    scores = jnp.where(valid, scores, -1e30)
    highest = jnp.max(scores, axis=-1, keepdims=True)
    powers = jnp.exp(scores - highest)
    weights = (powers / jnp.sum(powers, axis=-1, keepdims=True)).astype(jnp.bfloat16)
    mixed = jnp.einsum("rhp,rpl->rhl", weights, cache_latent, preferred_element_type=jnp.float32)
    return mixed.astype(jnp.bfloat16)


def split3(v):
    high = v.astype(jnp.bfloat16)
    rest = v - high.astype(jnp.float32)
    middle = rest.astype(jnp.bfloat16)
    low = (rest - middle.astype(jnp.float32)).astype(jnp.bfloat16)
    return high, middle, low


def slot_masks(routes, experts):
    named = jnp.any(routes[..., None] == jnp.arange(experts, dtype=jnp.int32), axis=-2)
    rows = routes.shape[-2]
    counts = named.astype(jnp.int32)
    earlier = [jnp.zeros_like(counts[..., 0, :])]
    for row in range(1, rows):
        earlier.append(earlier[-1] + counts[..., row - 1, :])
    earlier = jnp.stack(earlier, axis=-2)
    return named[..., None] & (earlier[..., None] == jnp.arange(CAP, dtype=jnp.int32))


def per_device(
    query_latent,
    query_rope,
    cache_latent,
    cache_rope,
    cache_len,
    moe_input,
    routes,
    gate_weights,
    w_gate,
    w_up,
    w_down,
):
    bf16, f32 = jnp.bfloat16, jnp.float32
    shares = lax.axis_size("tensor")
    experts = lax.axis_size("expert")
    me = lax.axis_index("tensor")
    rows, width = moe_input.shape
    chosen = routes.shape[1]
    units = w_gate.shape[2]
    part = width // shares
    slots = experts * CAP

    def shift(value, by):
        pairs = [(i, (i + by) % shares) for i in range(shares)]
        return lax.ppermute(value, "tensor", pairs)

    own_mask = slot_masks(routes, experts)
    select = jnp.transpose(own_mask, (1, 2, 0)).reshape(slots, rows).astype(bf16)
    packed = jnp.dot(select, moe_input, preferred_element_type=f32).astype(bf16)
    down_parts = [
        lax.dynamic_slice(w_down[0], (0, ((me + by) % shares) * part), (units, part))
        for by in range(shares)
    ]
    down = [down_parts[0]] + [shift(down_parts[by], by) for by in range(1, shares)]
    small = jnp.concatenate([routes.astype(f32), gate_weights], axis=1)
    group = jnp.stack([small] + [shift(small, by) for by in range(1, shares)])

    received = lax.all_to_all(
        packed.reshape(experts, CAP, width), "expert", split_axis=0, concat_axis=0, tiled=True
    ).reshape(slots, width)

    half = slots // 2
    block1 = shift(received, 1)
    block3 = shift(received, 3)
    block2 = jnp.concatenate([shift(block1[:half], 1), shift(block3[half:], 3)], axis=0)

    def hidden_of(block):
        gate = jnp.dot(block, w_gate[0], preferred_element_type=f32)
        upper = jnp.dot(block, w_up[0], preferred_element_type=f32)
        return (jax.nn.silu(gate) * upper).astype(bf16)

    hidden = [hidden_of(b) for b in (received, block1, block2, block3)]
    own_hidden = jnp.stack(hidden)
    gathered = [own_hidden] + [shift(own_hidden, by) for by in range(1, shares)]
    all_hidden = jnp.stack(
        [
            jnp.concatenate([gathered[s][(d - s) % shares] for s in range(shares)], axis=1)
            for d in range(shares)
        ],
        axis=0,
    )
    all_hidden = all_hidden.reshape(shares, experts, CAP, shares * units)
    all_hidden = jnp.transpose(all_hidden, (1, 0, 2, 3)).reshape(slots * shares, shares * units)
    expert_out = jnp.dot(
        all_hidden, jnp.concatenate(down, axis=0), preferred_element_type=f32
    ).astype(bf16)

    local_context = attend(query_latent, query_rope, cache_latent, cache_rope, cache_len)
    heads, latent = local_context.shape[1:]
    context_parts = [
        lax.dynamic_slice(
            local_context, (((me + by) % shares) * rows, 0, 0), (rows, heads, latent)
        )
        for by in range(shares)
    ]
    context_parts = [context_parts[0]] + [
        shift(context_parts[by], by) for by in range(1, shares)
    ]

    returned = lax.all_to_all(
        expert_out.reshape(experts, shares * CAP, part),
        "expert",
        split_axis=0,
        concat_axis=0,
        tiled=True,
    ).reshape(experts * shares * CAP, part)

    group_mask = slot_masks(group[:, :, :chosen].astype(jnp.int32), experts)
    group_routes = group[:, :, :chosen].astype(jnp.int32)
    match = group_routes[..., None] == jnp.arange(experts, dtype=jnp.int32)
    gates = jnp.sum(jnp.where(match, group[:, :, chosen:, None], 0.0), axis=2)
    weight = jnp.where(group_mask, gates[..., None], 0.0)
    same = jnp.arange(shares)[:, None] == jnp.arange(shares)[None, :]
    combine = jnp.where(same[:, None, None, :, None], weight[:, :, :, None, :], 0.0)
    combine = combine.reshape(shares * rows, experts * shares * CAP)
    sums = jnp.dot(
        jnp.concatenate(split3(combine), axis=0), returned, preferred_element_type=f32
    ).reshape(3, shares, rows, part)
    sums = (sums[2] + sums[1] + sums[0]).astype(bf16)
    pieces = [sums[0]] + [shift(sums[d], shares - d) for d in range(1, shares)]
    wide = jnp.concatenate(pieces + pieces, axis=1)
    moe_output = lax.dynamic_slice(wide, (0, ((shares - me) % shares) * part), (rows, width))

    context = jnp.zeros((rows, shares, heads, latent), bf16)
    for by in range(shares):
        context = lax.dynamic_update_slice(
            context, context_parts[by][:, None], (0, (me - by) % shares, 0, 0)
        )
    return (context.reshape(rows, shares * heads, latent), moe_output)


def solution(mesh):
    return jax.shard_map(
        per_device,
        mesh=mesh,
        in_specs=(
            P("expert", "tensor", None),
            P("expert", "tensor"),
            P("expert", None, None),
            P("expert", None, None),
            P("expert"),
            P(("expert", "tensor"), None),
            P(("expert", "tensor"), None),
            P(("expert", "tensor"), None),
            P("expert", None, "tensor"),
            P("expert", None, "tensor"),
            P("expert", "tensor", None),
        ),
        out_specs=(P(("expert", "tensor"), None, None), P(("expert", "tensor"), None)),
        check_vma=False,
    )
```

time: 389 us -> 203 us (0.52)
  blocking collectives: 153 us -> 0 us
  waiting for transfers between devices: 175 us -> 90.9 us
  starting transfers between devices: 6.51 us -> 50.5 us
  between operations: 14.1 us -> 1.2 us
  local copies, waits for them, and re-layouts: 18.2 us -> 28.9 us
  other arithmetic: 3.32 us -> 9.22 us
    all_to_all x2 -> x0, blocking collectives: 132 us -> none  [the longest x1 103 us: per_device(): lax.all_to_all(outgoing, 'expert', split_axis=0, concat_axis=0, tiled=True)]
    all_to_all x1 -> x2, waiting for transfers between devices: 163 us -> 33.2 us  [the longest x1 19.1 us: per_device(): lax.all_to_all(expert_out.reshape(experts, shares * CAP, part), 'expert',...]
    ppermute x0 -> x19, waiting for transfers between devices: none -> 57.8 us  [shift(): return lax.ppermute(value, 'tensor', pairs)]
    ppermute x0 -> x19, starting transfers between devices: none -> 28.7 us  [shift(): return lax.ppermute(value, 'tensor', pairs)]
    all_gather x2 -> x0, blocking collectives: 20.2 us -> none  [the longest x1 10.7 us: per_device(): lax.all_gather(routes, 'tensor', axis=0, tiled=True)]
    all_to_all x1 -> x2, starting transfers between devices: 6.29 us -> 21.9 us  [the longest x1 13 us: per_device(): lax.all_to_all(packed.reshape(experts, CAP, width), 'expert', split_axis=...]
    reduce_scatter x1 -> x0, waiting for transfers between devices: 11.5 us -> none  [per_device(): lax.psum_scatter(per_choice, 'tensor', scatter_dimension=0, tiled=True)]
    concatenate x0 -> x18, local copies, waits for them, and re-layouts: none -> 10.3 us  [the longest x16 10.2 us: per_device(): jnp.concatenate([gathered[s][(d - s) % shares] for s in range(shares)], a...]
  transfers between devices with their start and end apart: 2 -> 21, of which waited for: 2 -> 10; matrix products, arithmetic and copies ran while one was open for 3% -> 27% of each run, Pallas kernels for 0% -> 0%
where the time goes in v1:
time: 203 us; the launch traced here: 201 us
  waiting for transfers between devices  90.9 us (45%)
  starting transfers between devices  50.5 us (25%)
  local copies, waits for them, and re-layouts  28.9 us (14%)
  matrix products  20.5 us (10%)
  other arithmetic  9.22 us (5%)
    ppermute x19, waiting for transfers between devices, shift(): return lax.ppermute(value, 'tensor', pairs)  57.8 us
    ppermute x19, starting transfers between devices, shift(): return lax.ppermute(value, 'tensor', pairs)  28.7 us
    all_to_all x1, waiting for transfers between devices, per_device(): lax.all_to_all(expert_out.reshape(experts, shares * CAP, part), 'expert',...  19.1 us
    all_to_all x1, waiting for transfers between devices, per_device(): lax.all_to_all(packed.reshape(experts, CAP, width), 'expert', split_axis=...  14.1 us
    all_to_all x1, starting transfers between devices, per_device(): lax.all_to_all(packed.reshape(experts, CAP, width), 'expert', split_axis=...  13 us
    concatenate x16, local copies, waits for them, and re-layouts, per_device(): jnp.concatenate([gathered[s][(d - s) % shares] for s in range(shares)], a...  10.2 us
    all_to_all x1, starting transfers between devices, per_device(): lax.all_to_all(expert_out.reshape(experts, shares * CAP, part), 'expert',...  8.88 us
    dynamic_update_slice x5, local copies, waits for them, and re-layouts, per_device(): lax.dynamic_update_slice(context, context_parts[by][:, None], (0, (me - b...  5.64 us
  transfers between devices with their start and end apart: 21, of which 10 were waited for; matrix products, arithmetic and copies ran while one was open for 27% of the time, Pallas kernels for 0%

profile of v1, /device:TPU:1, one launch (start us, length us, event | category | flops | bytes accessed | tf_op | source)
XLA Modules:
  0.0 201.3 jit_solution(11925232537068717208)
XLA Ops:
  4.7 13.0 %all-to-all-start = ((bf16[64,2,3584]{2,1,0:T(2,128)(2,1)}), bf16[64,2,3584]{2,1,0:T(2,128)(2,1)S(1)}, u32[]{:S(2)}, u32[]{:S(2)}) async-start(bf16[64,2,3584]{2,1,0:T(2,128)(2,1)} %reshape.143), calls=%async_computation | async-start | bytes 1835008 | tf_op jit(solution)/shard_map/all_to_all | solution.py:88
  17.8 1.3 collective-permute-start.3
  19.1 2.6 %collective-permute-start.4 = (f32[8,16]{1,0:T(8,128)S(1)}, f32[8,16]{1,0:T(8,128)S(1)}, u32[]{:S(2)}, u32[]{:S(2)}) collective-permute-start(f32[8,16]{1,0:T(8,128)S(1)} %pad_maximum_fusion.2), channel_id=1, source_target_pairs={{0,2},{1,3},{2,0},{3,1},{4,6},{5,7},{6,4},{7,5},{8,10},{9,11},{10,... | collective-permute-start | bytes 1544 | tf_op jit(solution)/shard_map/ppermute | solution.py:75
  24.9 4.0 %fusion.34 = f32[32,32,128]{2,1,0:T(8,128)S(1)} fusion(f32[32,32,128]{2,1,0:T(8,128)S(1)} %fusion.67, bf16[32,32,512]{2,1,0:T(8,128)(2,1)} %param.11, bf16[32,128,512]{2,1,0:T(8,128)(2,1)} %param.13, pred[32,128]{1,0:T(8,128)(4,1)S(1)} %iota_compare_fusion.3), kind=kOutput, calls=%fused_computation.33 | convolution fusion | flops 134610944 | bytes 6295552 | tf_op jit(solution)/shard_map/rhl,rpl->rhp/dot_general | solution.py:15
  29.3 14.1 %all-to-all-done = bf16[64,2,3584]{2,1,0:T(2,128)(2,1)S(1)} async-done(((bf16[64,2,3584]{2,1,0:T(2,128)(2,1)}), bf16[64,2,3584]{2,1,0:T(2,128)(2,1)S(1)}, u32[]{:S(2)}, u32[]{:S(2)}) %all-to-all-start) | async-done | bytes 917536 | tf_op jit(solution)/shard_map/all_to_all | solution.py:88
  46.0 4.0 %convolution_convert_fusion.1 = bf16[32,32,512]{2,1,0:T(8,128)(2,1)S(1)} fusion(bf16[32,128,512]{2,1,0:T(8,128)(2,1)} %param.13, f32[32,32]{1,0:T(8,128)S(1)} %fusion.66, f32[32,32,128]{2,1,0:T(8,128)S(1)} %fusion.34), kind=kOutput, calls=%fused_computation.26 | convolution fusion | flops 135136384 | bytes 5771264 | tf_op jit(solution)/shard_map/rhp,rpl->rhl/dot_general | solution.py:27
  50.1 2.6 %dynamic-slice_bitcast_fusion.3 = (bf16[256,896]{1,0:T(8,128)(2,1)S(1)}, bf16[256,896]{1,0:T(8,128)(2,1)}, bf16[256,896]{1,0:T(8,128)(2,1)}, bf16[256,896]{1,0:T(8,128)(2,1)}) fusion(bf16[1,256,3584]{2,1,0:T(8,128)(2,1)} %param.21, s32[]{:T(128)S(6)} %select_n.128, s32[]{:T(128)S(6)} %select_n.129, s32[]{:T(128)S(6)} %select_n.131, s32[]{:T(128)S(6)} %select_n.130), kind=kLoop, calls=%fused_computation.44 | loop fusion | bytes 3670032 | tf_op jit(solution)/shard_map/dynamic_slice | solution.py:81
  52.7 1.4 collective-permute-start.8
  55.3 12.6 %collective-permute-done.6 = bf16[128,3584]{1,0:T(8,128)(2,1)} collective-permute-done((bf16[128,3584]{1,0:T(8,128)(2,1)}, bf16[128,3584]{1,0:T(8,128)(2,1)}, u32[]{:S(2)}, u32[]{:S(2)}) %collective-permute-start.6) | collective-permute-done | bytes 917536 | tf_op jit(solution)/shard_map/ppermute | solution.py:75
  69.0 1.6 fusion.21
  70.6 3.6 %collective-permute-done.8 = bf16[128,3584]{1,0:T(8,128)(2,1)S(1)} collective-permute-done((bf16[128,3584]{1,0:T(8,128)(2,1)S(1)}, bf16[128,3584]{1,0:T(8,128)(2,1)S(1)}, u32[]{:S(2)}, u32[]{:S(2)}) %collective-permute-start.8) | collective-permute-done | bytes 917536 | tf_op jit(solution)/shard_map/ppermute | solution.py:75
  74.1 1.3 collective-permute-start.7
  75.5 1.6 multiply_convert_fusion.2
  77.9 12.2 %collective-permute-done.7 = bf16[64,3584]{1,0:T(8,128)(2,1)S(1)} collective-permute-done((bf16[64,3584]{1,0:T(8,128)(2,1)S(1)}, bf16[64,3584]{1,0:T(8,128)(2,1)S(1)}, u32[]{:S(2)}, u32[]{:S(2)}) %collective-permute-start.7) | collective-permute-done | bytes 458784 | tf_op jit(solution)/shard_map/ppermute | solution.py:75
  90.2 9.8 %collective-permute-done.9 = bf16[64,3584]{1,0:T(8,128)(2,1)S(1)} collective-permute-done((bf16[64,3584]{1,0:T(8,128)(2,1)S(1)}, bf16[64,3584]{1,0:T(8,128)(2,1)S(1)}, u32[]{:S(2)}, u32[]{:S(2)}) %collective-permute-start.9) | collective-permute-done | bytes 458784 | tf_op jit(solution)/shard_map/ppermute | solution.py:75
  103.3 2.5 %collective-permute-start.14 = (bf16[256,896]{1,0:T(8,128)(2,1)}, bf16[256,896]{1,0:T(8,128)(2,1)}, u32[]{:S(2)}, u32[]{:S(2)}) collective-permute-start(bf16[256,896]{1,0:T(8,128)(2,1)} %get-tuple-element.17), channel_id=1, source_target_pairs={{0,2},{1,3},{2,0},{3,1},{4,6},{5,7},{6,4},{7,5},{8,10},{9,11},{10,... | collective-permute-start | bytes 1376264 | tf_op jit(solution)/shard_map/ppermute | solution.py:75
  106.0 2.3 %collective-permute-start.11 = (bf16[4,128,256]{2,1,0:T(8,128)(2,1)}, bf16[4,128,256]{2,1,0:T(8,128)(2,1)S(1)}, u32[]{:S(2)}, u32[]{:S(2)}) collective-permute-start(bf16[4,128,256]{2,1,0:T(8,128)(2,1)} %pad_maximum_fusion), channel_id=1, source_target_pairs={{0,2},{1,3},{2,0},{3,1},{4,6},{5,7},{6,4},{7,5},{8,10},{9,11},{10,... | collective-permute-start | bytes 786440 | tf_op jit(solution)/shard_map/ppermute | solution.py:75
  110.0 1.5 concatenate.77
  114.4 8.9 %collective-permute-done.11 = bf16[4,128,256]{2,1,0:T(8,128)(2,1)S(1)} collective-permute-done((bf16[4,128,256]{2,1,0:T(8,128)(2,1)}, bf16[4,128,256]{2,1,0:T(8,128)(2,1)S(1)}, u32[]{:S(2)}, u32[]{:S(2)}) %collective-permute-start.11) | collective-permute-done | bytes 262176 | tf_op jit(solution)/shard_map/ppermute | solution.py:75
  123.3 6.3 %collective-permute-start = (bf16[8,32,512]{2,1,0:T(8,128)(2,1)}, bf16[8,32,512]{2,1,0:T(8,128)(2,1)}, u32[]{:S(2)}, u32[]{:S(2)}) collective-permute-start(bf16[8,32,512]{2,1,0:T(8,128)(2,1)} %get-tuple-element.20), channel_id=1, source_target_pairs={{0,1},{1,2},{2,3},{3,0},{4,5},{5,6},{6,7},{7,4},{8,9},{9,10},{10,1... | collective-permute-start | bytes 786440 | tf_op jit(solution)/shard_map/ppermute | solution.py:75
  130.2 7.2 %collective-permute-done.12 = bf16[4,128,256]{2,1,0:T(8,128)(2,1)S(1)} collective-permute-done((bf16[4,128,256]{2,1,0:T(8,128)(2,1)}, bf16[4,128,256]{2,1,0:T(8,128)(2,1)S(1)}, u32[]{:S(2)}, u32[]{:S(2)}) %collective-permute-start.12) | collective-permute-done | bytes 262176 | tf_op jit(solution)/shard_map/ppermute | solution.py:75
  145.0 4.2 %maximum_bitcast_fusion = bf16[64,4,2,1024]{3,2,1,0:T(2,128)(2,1)S(1)} fusion(bf16[1,64,2,256]{3,2,0,1:T(2,128)(2,1)} %bitcast.116, bf16[1,64,2,256]{3,2,0,1:T(2,128)(2,1)} %bitcast.115, bf16[1,64,2,256]{3,2,0,1:T(2,128)(2,1)} %bitcast.114, bf16[1,64,2,256]{3,2,0,1:T(2,128)(2,1)S(1)} %bitcast.103, bf16[1,64,2,256]{3,2,0,1:T(2,128)(2,1)} %bitcast.113, ...), kind=kLoop, calls=%fused_computation.36 | loop fusion | flops 16777216 | bytes 2097152 | tf_op jit(solution)/shard_map/transpose | solution.py:113
  150.4 2.7 %collective-permute-start.2 = (bf16[8,32,512]{2,1,0:T(8,128)(2,1)}, bf16[8,32,512]{2,1,0:T(8,128)(2,1)}, u32[]{:S(2)}, u32[]{:S(2)}) collective-permute-start(bf16[8,32,512]{2,1,0:T(8,128)(2,1)} %get-tuple-element.18), channel_id=1, source_target_pairs={{0,3},{1,0},{2,1},{3,2},{4,7},{5,4},{6,5},{7,6},{8,11},{9,8},{10,9... | collective-permute-start | bytes 786440 | tf_op jit(solution)/shard_map/ppermute | solution.py:75
  153.1 3.8 %fusion.28 = bf16[64,8,896]{2,1,0:T(8,128)(2,1)} fusion(bf16[512,1024]{1,0:T(8,128)(2,1)} %reshape.145, bf16[256,896]{1,0:T(8,128)(2,1)} %collective-permute-done.15, bf16[256,896]{1,0:T(8,128)(2,1)} %collective-permute-done.14, bf16[256,896]{1,0:T(8,128)(2,1)} %collective-permute-done.13, bf16[256,896]{1,0:T(8,128)(2,1)S(1)} %get-tuple-element.14), kind=kOutput, calls=%fused_computation.28 | convolution fusion | flops 947322880 | bytes 3801088 | tf_op jit(solution)/shard_map/dot_general | solution.py:114
  156.9 8.9 %all-to-all-start.1 = ((bf16[64,8,896]{2,1,0:T(8,128)(2,1)}), bf16[64,8,896]{2,1,0:T(8,128)(2,1)}, u32[]{:S(2)}, u32[]{:S(2)}) async-start(bf16[64,8,896]{2,1,0:T(8,128)(2,1)} %fusion.28), calls=%async_computation.1 | async-start | bytes 1835008 | tf_op jit(solution)/shard_map/all_to_all | solution.py:130
  167.7 1.7 bitcast_dynamic-update-slice_fusion.2
  169.4 1.7 bitcast_dynamic-update-slice_fusion.1
  172.4 19.1 %all-to-all-done.1 = bf16[64,8,896]{2,1,0:T(8,128)(2,1)} async-done(((bf16[64,8,896]{2,1,0:T(8,128)(2,1)}), bf16[64,8,896]{2,1,0:T(8,128)(2,1)}, u32[]{:S(2)}, u32[]{:S(2)}) %all-to-all-start.1) | async-done | bytes 917536 | tf_op jit(solution)/shard_map/all_to_all | solution.py:130
  191.5 1.5 fusion.41
  195.0 1.9 collective-permute-start.17
  197.2 1.9 collective-permute-done.17
  199.1 1.5 collective-permute-done.18
  (134 shorter events, 36.8 us)
Async XLA Ops:
  0.6 53.7 %copy-start = (bf16[1,3584,256]{2,1,0:T(8,128)(2,1)S(1)}, bf16[1,3584,256]{2,1,0:T(8,128)(2,1)}, u32[]{:S(2)}) copy-start(bf16[1,3584,256]{2,1,0:T(8,128)(2,1)} %param.19) | copy-start | bytes 5505028
  3.4 14.3 %copy-start.7 = (s32[8,8]{1,0:T(8,128)S(1)}, s32[8,8]{1,0:T(8,128)}, u32[]{:S(2)}) copy-start(s32[8,8]{1,0:T(8,128)} %param.17) | copy-start | bytes 772
  3.4 14.3 %copy-start.9 = (f32[8,8]{1,0:T(8,128)S(1)}, f32[8,8]{1,0:T(8,128)}, u32[]{:S(2)}) copy-start(f32[8,8]{1,0:T(8,128)} %param.18) | copy-start | bytes 772
  3.4 21.3 %copy-start.4 = (bf16[32,64,128]{2,1,0:T(8,128)(2,1)S(1)}, bf16[32,64,128]{2,1,0:T(8,128)(2,1)}, u32[]{:S(2)}) copy-start(bf16[32,64,128]{2,1,0:T(8,128)(2,1)} %param.14) | copy-start | bytes 1572868
  4.7 38.7 %all-to-all-start = ((bf16[64,2,3584]{2,1,0:T(2,128)(2,1)}), bf16[64,2,3584]{2,1,0:T(2,128)(2,1)S(1)}, u32[]{:S(2)}, u32[]{:S(2)}) async-start(bf16[64,2,3584]{2,1,0:T(2,128)(2,1)} %reshape.143), calls=%async_computation | async-start | bytes 1835008 | tf_op jit(solution)/shard_map/all_to_all | solution.py:88
  17.8 11.2 %copy-start.8 = (f32[8,16]{1,0:T(8,128)}, f32[8,16]{1,0:T(8,128)S(1)}, u32[]{:S(2)}) copy-start(f32[8,16]{1,0:T(8,128)S(1)} %pad_maximum_fusion.2) | copy-start | bytes 1540
  17.8 85.5 %collective-permute-start.3 = (f32[8,16]{1,0:T(8,128)S(1)}, f32[8,16]{1,0:T(8,128)S(1)}, u32[]{:S(2)}, u32[]{:S(2)}) collective-permute-start(f32[8,16]{1,0:T(8,128)S(1)} %pad_maximum_fusion.2), channel_id=1, source_target_pairs={{0,1},{1,2},{2,3},{3,0},{4,5},{5,6},{6,7},{7,4},{8,9},{9,10},{10,1... | collective-permute-start | bytes 1544 | tf_op jit(solution)/shard_map/ppermute | solution.py:75
  19.1 86.7 %collective-permute-start.4 = (f32[8,16]{1,0:T(8,128)S(1)}, f32[8,16]{1,0:T(8,128)S(1)}, u32[]{:S(2)}, u32[]{:S(2)}) collective-permute-start(f32[8,16]{1,0:T(8,128)S(1)} %pad_maximum_fusion.2), channel_id=1, source_target_pairs={{0,2},{1,3},{2,0},{3,1},{4,6},{5,7},{6,4},{7,5},{8,10},{9,11},{10,... | collective-permute-start | bytes 1544 | tf_op jit(solution)/shard_map/ppermute | solution.py:75
  21.7 84.3 %collective-permute-start.5 = (f32[8,16]{1,0:T(8,128)S(1)}, f32[8,16]{1,0:T(8,128)S(1)}, u32[]{:S(2)}, u32[]{:S(2)}) collective-permute-start(f32[8,16]{1,0:T(8,128)S(1)} %pad_maximum_fusion.2), channel_id=1, source_target_pairs={{0,3},{1,0},{2,1},{3,2},{4,7},{5,4},{6,5},{7,6},{8,11},{9,8},{10,9... | collective-permute-start | bytes 1544 | tf_op jit(solution)/shard_map/ppermute | solution.py:75
  44.7 23.2 %collective-permute-start.6 = (bf16[128,3584]{1,0:T(8,128)(2,1)}, bf16[128,3584]{1,0:T(8,128)(2,1)}, u32[]{:S(2)}, u32[]{:S(2)}) collective-permute-start(bf16[128,3584]{1,0:T(8,128)(2,1)} %reshape.144), channel_id=1, source_target_pairs={{0,1},{1,2},{2,3},{3,0},{4,5},{5,6},{6,7},{7,4},{8,9},{9,10},{10,1... | collective-permute-start | bytes 2752520 | tf_op jit(solution)/shard_map/ppermute | solution.py:75
  50.1 2.7 %copy-start.2 = (bf16[128,3584]{1,0:T(8,128)(2,1)S(1)}, bf16[128,3584]{1,0:T(8,128)(2,1)}, u32[]{:S(2)}) copy-start(bf16[128,3584]{1,0:T(8,128)(2,1)} %reshape.144) | copy-start | bytes 2752516
  52.7 21.4 %collective-permute-start.8 = (bf16[128,3584]{1,0:T(8,128)(2,1)S(1)}, bf16[128,3584]{1,0:T(8,128)(2,1)S(1)}, u32[]{:S(2)}, u32[]{:S(2)}) collective-permute-start(bf16[128,3584]{1,0:T(8,128)(2,1)S(1)} %copy-done.2), channel_id=1, source_target_pairs={{0,3},{1,0},{2,1},{3,2},{4,7},{5,4},{6,5},{7,6},{8,11},{9,8},{10,9... | collective-permute-start | bytes 2752520 | tf_op jit(solution)/shard_map/ppermute | solution.py:75
  67.9 82.5 %collective-permute-start.13 = (bf16[256,896]{1,0:T(8,128)(2,1)}, bf16[256,896]{1,0:T(8,128)(2,1)}, u32[]{:S(2)}, u32[]{:S(2)}) collective-permute-start(bf16[256,896]{1,0:T(8,128)(2,1)} %get-tuple-element.15), channel_id=1, source_target_pairs={{0,1},{1,2},{2,3},{3,0},{4,5},{5,6},{6,7},{7,4},{8,9},{9,10},{10,1... | collective-permute-start | bytes 1376264 | tf_op jit(solution)/shard_map/ppermute | solution.py:75
  74.1 15.9 %collective-permute-start.7 = (bf16[64,3584]{1,0:T(8,128)(2,1)S(1)}, bf16[64,3584]{1,0:T(8,128)(2,1)S(1)}, u32[]{:S(2)}, u32[]{:S(2)}) collective-permute-start(bf16[64,3584]{1,0:T(8,128)(2,1)S(1)} %slice.165), channel_id=1, source_target_pairs={{0,1},{1,2},{2,3},{3,0},{4,5},{5,6},{6,7},{7,4},{8,9},{9,10},{10,1... | collective-permute-start | bytes 1376264 | tf_op jit(solution)/shard_map/ppermute | solution.py:75
  77.9 23.1 %copy-start.5 = (bf16[128,256]{1,0:T(8,128)(2,1)}, bf16[128,256]{1,0:T(8,128)(2,1)S(1)}, u32[]{:S(2)}) copy-start(bf16[128,256]{1,0:T(8,128)(2,1)S(1)} %multiply_convert_fusion) | copy-start | bytes 196612
  90.1 10.0 %collective-permute-start.9 = (bf16[64,3584]{1,0:T(8,128)(2,1)S(1)}, bf16[64,3584]{1,0:T(8,128)(2,1)S(1)}, u32[]{:S(2)}, u32[]{:S(2)}) collective-permute-start(bf16[64,3584]{1,0:T(8,128)(2,1)S(1)} %slice.166), channel_id=1, source_target_pairs={{0,3},{1,0},{2,1},{3,2},{4,7},{5,4},{6,5},{7,6},{8,11},{9,8},{10,9... | collective-permute-start | bytes 1376264 | tf_op jit(solution)/shard_map/ppermute | solution.py:75
  101.7 9.8 %collective-permute-start.10 = (bf16[4,128,256]{2,1,0:T(8,128)(2,1)}, bf16[4,128,256]{2,1,0:T(8,128)(2,1)}, u32[]{:S(2)}, u32[]{:S(2)}) collective-permute-start(bf16[4,128,256]{2,1,0:T(8,128)(2,1)} %pad_maximum_fusion), channel_id=1, source_target_pairs={{0,1},{1,2},{2,3},{3,0},{4,5},{5,6},{6,7},{7,4},{8,9},{9,10},{10,1... | collective-permute-start | bytes 786440 | tf_op jit(solution)/shard_map/ppermute | solution.py:75
  103.3 5.1 %copy-start.10 = (f32[8,16]{1,0:T(8,128)}, f32[8,16]{1,0:T(8,128)S(1)}, u32[]{:S(2)}) copy-start(f32[8,16]{1,0:T(8,128)S(1)} %collective-permute-done.3) | copy-start | bytes 1540
  103.3 49.9 %collective-permute-start.14 = (bf16[256,896]{1,0:T(8,128)(2,1)}, bf16[256,896]{1,0:T(8,128)(2,1)}, u32[]{:S(2)}, u32[]{:S(2)}) collective-permute-start(bf16[256,896]{1,0:T(8,128)(2,1)} %get-tuple-element.17), channel_id=1, source_target_pairs={{0,2},{1,3},{2,0},{3,1},{4,6},{5,7},{6,4},{7,5},{8,10},{9,11},{10,... | collective-permute-start | bytes 1376264 | tf_op jit(solution)/shard_map/ppermute | solution.py:75
  105.7 2.6 %copy-start.11 = (f32[8,16]{1,0:T(8,128)}, f32[8,16]{1,0:T(8,128)S(1)}, u32[]{:S(2)}) copy-start(f32[8,16]{1,0:T(8,128)S(1)} %collective-permute-done.4) | copy-start | bytes 1540
  105.7 47.4 %collective-permute-start.15 = (bf16[256,896]{1,0:T(8,128)(2,1)}, bf16[256,896]{1,0:T(8,128)(2,1)}, u32[]{:S(2)}, u32[]{:S(2)}) collective-permute-start(bf16[256,896]{1,0:T(8,128)(2,1)} %get-tuple-element.16), channel_id=1, source_target_pairs={{0,3},{1,0},{2,1},{3,2},{4,7},{5,4},{6,5},{7,6},{8,11},{9,8},{10,9... | collective-permute-start | bytes 1376264 | tf_op jit(solution)/shard_map/ppermute | solution.py:75
  106.0 17.2 %collective-permute-start.11 = (bf16[4,128,256]{2,1,0:T(8,128)(2,1)}, bf16[4,128,256]{2,1,0:T(8,128)(2,1)S(1)}, u32[]{:S(2)}, u32[]{:S(2)}) collective-permute-start(bf16[4,128,256]{2,1,0:T(8,128)(2,1)} %pad_maximum_fusion), channel_id=1, source_target_pairs={{0,2},{1,3},{2,0},{3,1},{4,6},{5,7},{6,4},{7,5},{8,10},{9,11},{10,... | collective-permute-start | bytes 786440 | tf_op jit(solution)/shard_map/ppermute | solution.py:75
  111.5 26.0 %collective-permute-start.12 = (bf16[4,128,256]{2,1,0:T(8,128)(2,1)}, bf16[4,128,256]{2,1,0:T(8,128)(2,1)S(1)}, u32[]{:S(2)}, u32[]{:S(2)}) collective-permute-start(bf16[4,128,256]{2,1,0:T(8,128)(2,1)} %pad_maximum_fusion), channel_id=1, source_target_pairs={{0,3},{1,0},{2,1},{3,2},{4,7},{5,4},{6,5},{7,6},{8,11},{9,8},{10,9... | collective-permute-start | bytes 786440 | tf_op jit(solution)/shard_map/ppermute | solution.py:75
  123.3 44.4 %collective-permute-start = (bf16[8,32,512]{2,1,0:T(8,128)(2,1)}, bf16[8,32,512]{2,1,0:T(8,128)(2,1)}, u32[]{:S(2)}, u32[]{:S(2)}) collective-permute-start(bf16[8,32,512]{2,1,0:T(8,128)(2,1)} %get-tuple-element.20), channel_id=1, source_target_pairs={{0,1},{1,2},{2,3},{3,0},{4,5},{5,6},{6,7},{7,4},{8,9},{9,10},{10,1... | collective-permute-start | bytes 786440 | tf_op jit(solution)/shard_map/ppermute | solution.py:75
  137.5 31.9 %collective-permute-start.1 = (bf16[8,32,512]{2,1,0:T(8,128)(2,1)}, bf16[8,32,512]{2,1,0:T(8,128)(2,1)}, u32[]{:S(2)}, u32[]{:S(2)}) collective-permute-start(bf16[8,32,512]{2,1,0:T(8,128)(2,1)} %get-tuple-element.19), channel_id=1, source_target_pairs={{0,2},{1,3},{2,0},{3,1},{4,6},{5,7},{6,4},{7,5},{8,10},{9,11},{10,... | collective-permute-start | bytes 786440 | tf_op jit(solution)/shard_map/ppermute | solution.py:75
  150.4 43.6 %collective-permute-start.2 = (bf16[8,32,512]{2,1,0:T(8,128)(2,1)}, bf16[8,32,512]{2,1,0:T(8,128)(2,1)}, u32[]{:S(2)}, u32[]{:S(2)}) collective-permute-start(bf16[8,32,512]{2,1,0:T(8,128)(2,1)} %get-tuple-element.18), channel_id=1, source_target_pairs={{0,3},{1,0},{2,1},{3,2},{4,7},{5,4},{6,5},{7,6},{8,11},{9,8},{10,9... | collective-permute-start | bytes 786440 | tf_op jit(solution)/shard_map/ppermute | solution.py:75
  156.9 9.8 %copy-start.13 = (pred[4,4]{0,1:T(4,128)(4,1)S(1)}, pred[4,4]{0,1:T(4,128)(4,1)}, u32[]{:S(2)}) copy-start(pred[4,4]{0,1:T(4,128)(4,1)} %iota_compare_fusion.4) | copy-start | bytes 52
  156.9 34.6 %all-to-all-start.1 = ((bf16[64,8,896]{2,1,0:T(8,128)(2,1)}), bf16[64,8,896]{2,1,0:T(8,128)(2,1)}, u32[]{:S(2)}, u32[]{:S(2)}) async-start(bf16[64,8,896]{2,1,0:T(8,128)(2,1)} %fusion.28), calls=%async_computation.1 | async-start | bytes 1835008 | tf_op jit(solution)/shard_map/all_to_all | solution.py:130
  193.0 4.2 %collective-permute-start.16 = (bf16[8,896]{1,0:T(8,128)(2,1)S(1)}, bf16[8,896]{1,0:T(8,128)(2,1)S(1)}, u32[]{:S(2)}, u32[]{:S(2)}) collective-permute-start(bf16[8,896]{1,0:T(8,128)(2,1)S(1)} %get-tuple-element.39), channel_id=1, source_target_pairs={{0,3},{1,0},{2,1},{3,2},{4,7},{5,4},{6,5},{7,6},{8,11},{9,8},{10,9... | collective-permute-start | bytes 43016 | tf_op jit(solution)/shard_map/ppermute | solution.py:75
  195.0 6.4 %copy-start.3 = (bf16[8,4,32,512]{3,2,1,0:T(8,128)(2,1)}, bf16[8,4,32,512]{3,2,1,0:T(8,128)(2,1)S(1)}, u32[]{:S(2)}) copy-start(bf16[8,4,32,512]{3,2,1,0:T(8,128)(2,1)S(1)} %bitcast_dynamic-update-slice_fusion) | copy-start | bytes 3145732
  195.0 4.2 %collective-permute-start.17 = (bf16[8,896]{1,0:T(8,128)(2,1)S(1)}, bf16[8,896]{1,0:T(8,128)(2,1)S(1)}, u32[]{:S(2)}, u32[]{:S(2)}) collective-permute-start(bf16[8,896]{1,0:T(8,128)(2,1)S(1)} %get-tuple-element.38), channel_id=1, source_target_pairs={{0,2},{1,3},{2,0},{3,1},{4,6},{5,7},{6,4},{7,5},{8,10},{9,11},{10,... | collective-permute-start | bytes 43016 | tf_op jit(solution)/shard_map/ppermute | solution.py:75
  196.9 3.8 %collective-permute-start.18 = (bf16[8,896]{1,0:T(8,128)(2,1)S(1)}, bf16[8,896]{1,0:T(8,128)(2,1)S(1)}, u32[]{:S(2)}, u32[]{:S(2)}) collective-permute-start(bf16[8,896]{1,0:T(8,128)(2,1)S(1)} %get-tuple-element.36), channel_id=1, source_target_pairs={{0,1},{1,2},{2,3},{3,0},{4,5},{5,6},{6,7},{7,4},{8,9},{9,10},{10,1... | collective-permute-start | bytes 43016 | tf_op jit(solution)/shard_map/ppermute | solution.py:75
  (4 other events, 6.1 us)

commit v2 on v1

v2 whole, which is shorter than its diff:
```python
import functools

import jax
import jax.numpy as jnp
from jax import lax
from jax.experimental import pallas as pl
from jax.experimental.pallas import tpu as pltpu
from jax.sharding import PartitionSpec as P

score_scale = 192.0 ** (-0.5)
CAP = 2
INFO = 16


def attend(query_latent, query_rope, cache_latent, cache_rope, cache_len):
    count, heads, latent = query_latent.shape
    rotary_width = cache_rope.shape[1]
    positions = cache_latent.shape[1]
    rotary = query_rope.reshape(count, heads, rotary_width)
    scores = jnp.einsum(
        "rhl,rpl->rhp", query_latent, cache_latent, preferred_element_type=jnp.float32
    )
    scores = scores + jnp.einsum(
        "rhe,rep->rhp", rotary, cache_rope, preferred_element_type=jnp.float32
    )
    scores = scores * score_scale
    valid = jnp.arange(positions, dtype=jnp.int32)[None, None, :] < cache_len[:, None, None]
    scores = jnp.where(valid, scores, -1e30)
    highest = jnp.max(scores, axis=-1, keepdims=True)
    powers = jnp.exp(scores - highest)
    weights = (powers / jnp.sum(powers, axis=-1, keepdims=True)).astype(jnp.bfloat16)
    mixed = jnp.einsum("rhp,rpl->rhl", weights, cache_latent, preferred_element_type=jnp.float32)
    return mixed.astype(jnp.bfloat16)


def split3(v):
    high = v.astype(jnp.bfloat16)
    rest = v - high.astype(jnp.float32)
    middle = rest.astype(jnp.bfloat16)
    low = (rest - middle.astype(jnp.float32)).astype(jnp.bfloat16)
    return high, middle, low


def slot_masks(routes, experts):
    named = jnp.any(routes[..., None] == jnp.arange(experts, dtype=jnp.int32), axis=-2)
    rows = routes.shape[-2]
    counts = named.astype(jnp.int32)
    earlier = [jnp.zeros_like(counts[..., 0, :])]
    for row in range(1, rows):
        earlier.append(earlier[-1] + counts[..., row - 1, :])
    earlier = jnp.stack(earlier, axis=-2)
    return named[..., None] & (earlier[..., None] == jnp.arange(CAP, dtype=jnp.int32))


vmem_params = pltpu.CompilerParams(vmem_limit_bytes=40 * 1024 * 1024)
whole = pl.BlockSpec(memory_space=pltpu.VMEM)


def pack_kernel(shares, experts, routes_ref, rows_ref, out_ref):
    f32, bf16 = jnp.float32, jnp.bfloat16
    rows, width = rows_ref.shape
    part = width // shares
    chunk = shares * CAP
    lane = lax.broadcasted_iota(jnp.int32, (rows, experts * chunk), 1)
    expert, slot, quarter = lane // chunk, lane % CAP, lane % chunk // CAP
    named = jnp.zeros(lane.shape, f32)
    for k in range(routes_ref.shape[1]):
        named = jnp.where(routes_ref[:, k : k + 1] == expert, 1.0, named)
    before = lax.broadcasted_iota(jnp.int32, (rows, rows), 0) > lax.broadcasted_iota(
        jnp.int32, (rows, rows), 1
    )
    earlier = jnp.dot(before.astype(f32), named, preferred_element_type=f32)
    taken = jnp.where(earlier == slot.astype(f32), named, 0.0)
    select = jnp.concatenate(
        [jnp.where(quarter == q, taken, 0.0) for q in range(shares)], axis=0
    )
    values = rows_ref[...].astype(f32)
    values = jnp.concatenate(
        [values[:, q * part : (q + 1) * part] for q in range(shares)], axis=0
    )
    out_ref[...] = jnp.dot(
        select.T.astype(bf16), values.astype(bf16), preferred_element_type=f32
    ).astype(bf16)


def pack_rows(routes, rows, shares, experts):
    part = rows.shape[1] // shares
    total = experts * shares * CAP
    return pl.pallas_call(
        functools.partial(pack_kernel, shares, experts),
        out_shape=jax.ShapeDtypeStruct((total, part), rows.dtype),
        in_specs=[whole] * 2,
        out_specs=whole,
        compiler_params=vmem_params,
        cost_estimate=pl.CostEstimate(
            flops=2 * total * part * rows.shape[0] * shares,
            bytes_accessed=2 * total * part,
            transcendentals=0,
        ),
    )(routes, rows)


def hidden_kernel(count, shares, *refs):
    halves, (order_ref, gate_ref, up_ref, out_ref, wide) = refs[:count], refs[count:]
    rows, part = halves[0].shape
    slots = rows // shares
    for h in range(count):
        ordered = jnp.dot(
            order_ref[...], halves[h][...], preferred_element_type=jnp.float32
        ).astype(wide.dtype)
        for q in range(shares):
            wide[pl.ds(h * slots, slots), pl.ds(q * part, part)] = ordered[
                q * slots : (q + 1) * slots
            ]
    gate = jnp.dot(wide[...], gate_ref[...], preferred_element_type=jnp.float32)
    upper = jnp.dot(wide[...], up_ref[...], preferred_element_type=jnp.float32)
    out_ref[...] = (gate / (1.0 + jnp.exp(-gate)) * upper).astype(out_ref.dtype)


def hidden_units(halves, order, w_gate, w_up):
    count = len(halves)
    rows, part = halves[0].shape
    width, units = w_gate.shape
    shares = width // part
    total = count * rows // shares
    return pl.pallas_call(
        functools.partial(hidden_kernel, count, shares),
        out_shape=jax.ShapeDtypeStruct((total, units), jnp.bfloat16),
        in_specs=[whole] * (count + 3),
        out_specs=whole,
        scratch_shapes=[pltpu.VMEM((total, width), jnp.bfloat16)],
        compiler_params=vmem_params,
        cost_estimate=pl.CostEstimate(
            flops=4 * total * width * units,
            bytes_accessed=4 * width * units + 2 * total * width,
            transcendentals=total * units,
        ),
    )(*halves, order, w_gate, w_up)


def down_early_kernel(shares, *refs):
    early, weights, out_ref = refs[:shares], refs[shares : 2 * shares], refs[2 * shares]
    slots = out_ref.shape[0] // shares
    for block in range(shares):
        total = None
        for s in range(shares):
            of_sender = (block - s) % shares
            if of_sender == shares // 2:
                continue
            place = of_sender - (of_sender > shares // 2)
            units = early[s][pl.ds(place * slots, slots), :]
            term = jnp.dot(
                units, weights[s][: units.shape[1], :], preferred_element_type=jnp.float32
            )
            total = term if total is None else total + term
        out_ref[pl.ds(block * slots, slots), :] = total


def down_late_kernel(shares, *refs):
    late, weights = refs[:shares], refs[shares : 2 * shares]
    early_ref, order_ref, out_ref, plain = refs[2 * shares :]
    slots = late[0].shape[0]
    half = slots // 2
    for block in range(shares):
        s = (block - shares // 2) % shares
        units = late[s][...]
        term = jnp.dot(
            units, weights[s][: units.shape[1], :], preferred_element_type=jnp.float32
        )
        total = (early_ref[pl.ds(block * slots, slots), :] + term).astype(plain.dtype)
        plain[pl.ds(block * half, half), :] = total[:half]
        plain[pl.ds((shares + block) * half, half), :] = total[half:]
    for h in range(2):
        place = pl.ds(h * shares * half, shares * half)
        out_ref[place, :] = jnp.dot(
            order_ref[...], plain[place, :], preferred_element_type=jnp.float32
        ).astype(out_ref.dtype)


def down_early(early, weights):
    shares = len(weights)
    units, part = weights[0].shape
    rows = early[0].shape[0] // (shares - 1) * shares
    return pl.pallas_call(
        functools.partial(down_early_kernel, shares),
        out_shape=jax.ShapeDtypeStruct((rows, part), jnp.float32),
        in_specs=[whole] * (2 * shares),
        out_specs=whole,
        compiler_params=vmem_params,
        cost_estimate=pl.CostEstimate(
            flops=2 * rows * part * (shares - 1) * units,
            bytes_accessed=4 * rows * part + 4 * units * part * shares,
            transcendentals=0,
        ),
    )(*early, *weights)


def down_late(late, weights, early, order):
    shares = len(weights)
    rows, part = early.shape
    return pl.pallas_call(
        functools.partial(down_late_kernel, shares),
        out_shape=jax.ShapeDtypeStruct((rows, part), jnp.bfloat16),
        in_specs=[whole] * (2 * shares + 2),
        out_specs=whole,
        scratch_shapes=[pltpu.VMEM((rows, part), jnp.bfloat16)],
        compiler_params=vmem_params,
        cost_estimate=pl.CostEstimate(
            flops=2 * rows * part * (weights[0].shape[0] + rows),
            bytes_accessed=6 * rows * part,
            transcendentals=0,
        ),
    )(*late, *weights, early, order)


def per_device(
    query_latent,
    query_rope,
    cache_latent,
    cache_rope,
    cache_len,
    moe_input,
    routes,
    gate_weights,
    w_gate,
    w_up,
    w_down,
):
    bf16, f32 = jnp.bfloat16, jnp.float32
    shares = lax.axis_size("tensor")
    experts = lax.axis_size("expert")
    me = lax.axis_index("tensor")
    rows, width = moe_input.shape
    chosen = routes.shape[1]
    units = w_gate.shape[2]
    part = width // shares
    slots = experts * CAP

    def shift(value, by):
        pairs = [(i, (i + by) % shares) for i in range(shares)]
        return lax.ppermute(value, "tensor", pairs)

    packed = pack_rows(routes, moe_input, shares, experts)
    packed, w_down, routes, gate_weights = lax.optimization_barrier(
        (packed, w_down, routes, gate_weights)
    )
    received = lax.all_to_all(
        packed.reshape(experts, shares * CAP, part),
        "expert",
        split_axis=0,
        concat_axis=0,
        tiled=True,
    ).reshape(shares * slots, part)
    info = jnp.concatenate((routes.astype(bf16),) + split3(gate_weights), axis=1)
    info = jnp.pad(info, ((0, INFO - rows), (0, part - info.shape[1])))
    down_parts = [
        jnp.concatenate(
            [
                lax.dynamic_slice(w_down[0], (0, ((me + by) % shares) * part), (units, part)),
                info,
            ],
            axis=0,
        )
        for by in range(shares)
    ]
    down = [down_parts[0]] + [shift(down_parts[by], by) for by in range(1, shares)]
    local_context = attend(query_latent, query_rope, cache_latent, cache_rope, cache_len)
    heads, latent = local_context.shape[1:]
    received, local_context = lax.optimization_barrier((received, local_context))

    half = shares * slots // 2
    low, high = received[:half], received[half:]
    place = jnp.arange(half, dtype=jnp.int32)
    by_quarter = place // (half // shares), place % (half // shares)
    source = by_quarter[1] // CAP * (shares * CAP) + by_quarter[0] * CAP + by_quarter[1] % CAP
    sort = (source[:, None] == place[None, :]).astype(bf16)

    def hidden_of(*halves):
        return hidden_units(halves, sort, w_gate[0], w_up[0])

    low1, high3 = shift(low, 1), shift(high, 3)
    hidden0 = hidden_of(low, high)
    low, high, hidden0, down = lax.optimization_barrier((low, high, hidden0, down))
    high1, low3 = shift(high, 1), shift(low, 3)
    low2, high2 = shift(low1, 1), shift(high3, 3)
    hidden13 = hidden_of(low1, high1, low3, high3)
    early = jnp.concatenate([hidden0, hidden13], axis=0)
    early = [early] + [shift(early, by) for by in range(1, shares)]
    late = hidden_of(low2, high2)
    late = [late] + [shift(late, by) for by in range(1, shares)]

    expert_out = down_late(late, down, down_early(early, down), sort.T)
    expert_out, local_context, down = lax.optimization_barrier(
        (expert_out, local_context, down)
    )

    returned = lax.all_to_all(
        expert_out.reshape(experts, shares * CAP, part),
        "expert",
        split_axis=0,
        concat_axis=0,
        tiled=True,
    ).reshape(experts * shares * CAP, part)
    context_parts = [
        lax.dynamic_slice(
            local_context, (((me + by) % shares) * rows, 0, 0), (rows, heads, latent)
        )
        for by in range(shares)
    ]
    context_parts = [context_parts[0]] + [
        shift(context_parts[by], by) for by in range(1, shares)
    ]

    context = jnp.zeros((rows, shares, heads, latent), bf16)
    for by in range(shares):
        context = lax.dynamic_update_slice(
            context, context_parts[by][:, None], (0, (me - by) % shares, 0, 0)
        )

    info = jnp.stack([d[units : units + rows, : 4 * chosen] for d in down]).astype(f32)
    group_routes = info[:, :, :chosen].astype(jnp.int32)
    group_gates = (info[:, :, chosen : 2 * chosen] + info[:, :, 2 * chosen : 3 * chosen]) + info[
        :, :, 3 * chosen :
    ]
    group_mask = slot_masks(group_routes, experts)
    match = group_routes[..., None] == jnp.arange(experts, dtype=jnp.int32)
    gates = jnp.sum(jnp.where(match, group_gates[..., None], 0.0), axis=2)
    weight = jnp.where(group_mask, gates[..., None], 0.0)
    same = jnp.arange(shares)[:, None] == jnp.arange(shares)[None, :]
    combine = jnp.where(same[:, None, None, :, None], weight[:, :, :, None, :], 0.0)
    combine = combine.reshape(shares * rows, experts * shares * CAP)
    returned, context, combine = lax.optimization_barrier((returned, context, combine))
    sums = jnp.dot(
        jnp.concatenate(split3(combine), axis=0), returned, preferred_element_type=f32
    ).reshape(3, shares, rows, part)
    sums = (sums[2] + sums[1] + sums[0]).astype(bf16)
    pieces = [sums[0]] + [shift(sums[d], shares - d) for d in range(1, shares)]
    wide = jnp.concatenate(pieces + pieces, axis=1)
    moe_output = lax.dynamic_slice(wide, (0, ((shares - me) % shares) * part), (rows, width))

    return (context.reshape(rows, shares * heads, latent), moe_output)


def solution(mesh):
    return jax.shard_map(
        per_device,
        mesh=mesh,
        in_specs=(
            P("expert", "tensor", None),
            P("expert", "tensor"),
            P("expert", None, None),
            P("expert", None, None),
            P("expert"),
            P(("expert", "tensor"), None),
            P(("expert", "tensor"), None),
            P(("expert", "tensor"), None),
            P("expert", None, "tensor"),
            P("expert", None, "tensor"),
            P("expert", "tensor", None),
        ),
        out_specs=(P(("expert", "tensor"), None, None), P(("expert", "tensor"), None)),
        check_vma=False,
    )
```

time: 203 us -> 141 us (0.69)
  waiting for transfers between devices: 90.9 us -> 41.5 us
  local copies, waits for them, and re-layouts: 28.9 us -> 11.3 us
  Pallas kernels: 0 us -> 13.4 us
  matrix products: 20.5 us -> 11.8 us
  starting transfers between devices: 50.5 us -> 52.9 us
    ppermute x19 -> x21, waiting for transfers between devices: 57.8 us -> 28.9 us  [shift(): return lax.ppermute(value, 'tensor', pairs)]
    pallas_call x0 -> x6, Pallas kernels: none -> 13.4 us  [the longest x3 5.95 us: hidden_units(): pl.pallas_call(functools.partial(hidden_kernel, count, shares), out_shape...]
    all_to_all x1, waiting for transfers between devices: 19.1 us -> 8.3 us  [per_device(): lax.all_to_all(expert_out.reshape(experts, shares * CAP, part), 'expert',...]
    dot_general x10 -> x0, matrix products: 10.7 us -> none  [the longest x1 3.79 us: per_device(): jnp.dot(all_hidden, jnp.concatenate(down, axis=0), preferred_element_type...]
    concatenate x17 -> x0, local copies, waits for them, and re-layouts: 10.2 us -> none  [the longest x16 10.2 us: per_device(): jnp.concatenate([gathered[s][(d - s) % shares] for s in range(shares)], a...]
    all_to_all x1, waiting for transfers between devices: 14.1 us -> 4.26 us  [per_device(): lax.all_to_all(packed.reshape(experts, shares * CAP, part), 'expert', spl...]
    dynamic_update_slice x5, local copies, waits for them, and re-layouts: 5.64 us -> 1.14 us  [per_device(): lax.dynamic_update_slice(context, context_parts[by][:, None], (0, (me - b...]
    unnamed x37 -> x32, local copies, waits for them, and re-layouts: 0.26 us -> 4.69 us
  transfers between devices with their start and end apart: 21 -> 23, of which waited for: 10 -> 11; matrix products, arithmetic and copies ran while one was open for 27% -> 16% of each run, Pallas kernels for 0% -> 6%
where the time goes in v2:
time: 141 us; the launch traced here: 140 us
  starting transfers between devices  52.9 us (38%)
  waiting for transfers between devices  41.5 us (29%)
  Pallas kernels  13.4 us (10%)
  matrix products  11.8 us (8%)
  local copies, waits for them, and re-layouts  11.3 us (8%)
  other arithmetic  8.13 us (6%)
    ppermute x21, waiting for transfers between devices, shift(): return lax.ppermute(value, 'tensor', pairs)  28.9 us
    ppermute x21, starting transfers between devices, shift(): return lax.ppermute(value, 'tensor', pairs)  27.9 us
    all_to_all x1, starting transfers between devices, per_device(): lax.all_to_all(packed.reshape(experts, shares * CAP, part), 'expert', spl...  13.2 us
    all_to_all x1, starting transfers between devices, per_device(): lax.all_to_all(expert_out.reshape(experts, shares * CAP, part), 'expert',...  11.9 us
    all_to_all x1, waiting for transfers between devices, per_device(): lax.all_to_all(expert_out.reshape(experts, shares * CAP, part), 'expert',...  8.3 us
    pallas_call x3, Pallas kernels, hidden_units(): pl.pallas_call(functools.partial(hidden_kernel, count, shares), out_shape...  5.95 us
    dot_general x1, matrix products, attend(): jnp.einsum('rhp,rpl->rhl', weights, cache_latent, preferred_element_type=...  5.37 us
    unnamed x32, local copies, waits for them, and re-layouts  4.69 us
  transfers between devices with their start and end apart: 23, of which 11 were waited for; matrix products, arithmetic and copies ran while one was open for 16% of the time, Pallas kernels for 6%

profile of v2, /device:TPU:1, one launch (start us, length us, event | category | flops | bytes accessed | tf_op | source)
XLA Modules:
  0.0 140.1 jit_solution(2960828778192954137)
XLA Ops:
  2.2 1.6 %shard_map.122 = bf16[512,896]{1,0:T(8,128)(2,1)} custom-call(s32[8,8]{1,0:T(8,128)S(1)} %copy-done.6, bf16[8,3584]{1,0:T(8,128)(2,1)S(1)} %copy-done.5), custom_call_target="tpu_custom_call" | custom-call | flops 29360128 | bytes 917504 | tf_op jit(solution)/shard_map/pallas_call | solution.py:89
  3.8 13.2 %all-to-all-start = ((bf16[64,8,896]{2,1,0:T(8,128)(2,1)}), bf16[64,8,896]{2,1,0:T(8,128)(2,1)}, u32[]{:S(2)}, u32[]{:S(2)}) async-start(bf16[64,8,896]{2,1,0:T(8,128)(2,1)} %bitcast), calls=%async_computation | async-start | bytes 1835008 | tf_op jit(solution)/shard_map/all_to_all | solution.py:247
  19.4 1.9 %pad_maximum_fusion = (bf16[272,896]{1,0:T(8,128)(2,1)}, bf16[272,896]{1,0:T(8,128)(2,1)}, bf16[272,896]{1,0:T(8,128)(2,1)}, bf16[272,896]{1,0:T(8,128)(2,1)S(1)}) fusion(bf16[16,896]{1,0:T(8,128)(2,1)} %fusion.27, bf16[256,896]{1,0:T(8,128)(2,1)S(1)} %get-tuple-element.52, bf16[256,896]{1,0:T(8,128)(2,1)S(1)} %get-tuple-element.54, ...), kind=kLoop, calls=%fused_computation.7 | loop fusion | flops 3168256 | bytes 3813376 | tf_op jit(solution)/shard_map/concatenate | solution.py:257
  22.6 2.6 %collective-permute-start.8 = (bf16[272,896]{1,0:T(8,128)(2,1)}, bf16[272,896]{1,0:T(8,128)(2,1)}, u32[]{:S(2)}, u32[]{:S(2)}) collective-permute-start(bf16[272,896]{1,0:T(8,128)(2,1)} %get-tuple-element.70), channel_id=1, source_target_pairs={{0,2},{1,3},{2,0},{3,1},{4,6},{5,7},{6,4},{7,5},{8,10},{9,11},{10,... | collective-permute-start | bytes 1462280 | tf_op jit(solution)/shard_map/ppermute | solution.py:241
  26.9 4.5 %fusion.4 = f32[32,32,128]{2,1,0:T(8,128)} fusion(f32[32,32,128]{2,1,0:T(8,128)S(1)} %fusion.44, bf16[32,32,512]{2,1,0:T(8,128)(2,1)S(1)} %copy-done, bf16[32,128,512]{2,1,0:T(8,128)(2,1)} %param.13, pred[32,128]{1,0:T(8,128)(4,1)S(1)} %iota_compare_fusion.6), kind=kOutput, calls=%fused_computation.6 | convolution fusion | flops 134610944 | bytes 6295552 | tf_op jit(solution)/shard_map/rhl,rpl->rhp/dot_general | solution.py:20
  31.4 1.7 %fusion.43 = f32[32,32]{1,0:T(8,128)S(1)} fusion(f32[32,32,128]{2,1,0:T(8,128)} %fusion.4), kind=kOutput, calls=%fused_computation.111 | output fusion | flops 262271 | bytes 528384 | tf_op jit(solution)/shard_map/sub | solution.py:30
  33.1 5.4 %convolution_convert_fusion = bf16[32,32,512]{2,1,0:T(8,128)(2,1)} fusion(bf16[32,128,512]{2,1,0:T(8,128)(2,1)} %param.13, f32[32,32]{1,0:T(8,128)S(1)} %fusion.43, f32[32,32,128]{2,1,0:T(8,128)} %fusion.4), kind=kOutput, calls=%fused_computation.1 | convolution fusion | flops 135136384 | bytes 5771264 | tf_op jit(solution)/shard_map/rhp,rpl->rhl/dot_general | solution.py:32
  38.4 4.3 %all-to-all-done = bf16[64,8,896]{2,1,0:T(8,128)(2,1)} async-done(((bf16[64,8,896]{2,1,0:T(8,128)(2,1)}), bf16[64,8,896]{2,1,0:T(8,128)(2,1)}, u32[]{:S(2)}, u32[]{:S(2)}) %all-to-all-start) | async-done | bytes 917536 | tf_op jit(solution)/shard_map/all_to_all | solution.py:247
  43.9 1.4 collective-permute-start
  45.3 1.5 %collective-permute-start.2 = (bf16[256,896]{1,0:T(8,128)(2,1)S(1)}, bf16[256,896]{1,0:T(8,128)(2,1)}, u32[]{:S(2)}, u32[]{:S(2)}) collective-permute-start(bf16[256,896]{1,0:T(8,128)(2,1)S(1)} %get-tuple-element.34.refs_1_), channel_id=1, source_target_pairs={{0,3},{1,0},{2,1},{3,2},{4,7},{5,4},{6,5},{7,6},{8,11},{9,8},{10,9... | collective-permute-start | bytes 1376264 | tf_op jit(solution)/shard_map/ppermute | solution.py:241
  47.5 1.5 %copy-done.2 = bf16[1,3584,256]{2,1,0:T(8,128)(2,1)S(1)} copy-done((bf16[1,3584,256]{2,1,0:T(8,128)(2,1)S(1)}, bf16[1,3584,256]{2,1,0:T(8,128)(2,1)}, u32[]{:S(2)}) %copy-start.2) | copy-done | bytes 1835032
  50.1 2.7 %collective-permute-start.11 = (bf16[256,896]{1,0:T(8,128)(2,1)S(1)}, bf16[256,896]{1,0:T(8,128)(2,1)S(1)}, u32[]{:S(2)}, u32[]{:S(2)}) collective-permute-start(bf16[256,896]{1,0:T(8,128)(2,1)S(1)} %get-tuple-element.35.refs_0_), channel_id=1, source_target_pairs={{0,3},{1,0},{2,1},{3,2},{4,7},{5,4},{6,5},{7,6},{8,11},{9,8},{10,9... | collective-permute-start | bytes 1376264 | tf_op jit(solution)/shard_map/ppermute | solution.py:241
  52.8 4.5 %collective-permute-done.refs_0_ = bf16[256,896]{1,0:T(8,128)(2,1)} collective-permute-done((bf16[256,896]{1,0:T(8,128)(2,1)S(1)}, bf16[256,896]{1,0:T(8,128)(2,1)}, u32[]{:S(2)}, u32[]{:S(2)}) %collective-permute-start) | collective-permute-done | bytes 458784 | tf_op jit(solution)/shard_map/ppermute | solution.py:241
  57.2 2.7 %collective-permute-start.3 = (bf16[256,896]{1,0:T(8,128)(2,1)}, bf16[256,896]{1,0:T(8,128)(2,1)}, u32[]{:S(2)}, u32[]{:S(2)}) collective-permute-start(bf16[256,896]{1,0:T(8,128)(2,1)} %collective-permute-done.2.refs_3_), channel_id=1, source_target_pairs={{0,3},{1,0},{2,1},{3,2},{4,7},{5,4},{6,5},{7,6},{8,11},{9,8},{10,9... | collective-permute-start | bytes 1376264 | tf_op jit(solution)/shard_map/ppermute | solution.py:241
  59.9 7.0 %collective-permute-done.10.refs_1_ = bf16[256,896]{1,0:T(8,128)(2,1)S(1)} collective-permute-done((bf16[256,896]{1,0:T(8,128)(2,1)S(1)}, bf16[256,896]{1,0:T(8,128)(2,1)S(1)}, u32[]{:S(2)}, u32[]{:S(2)}) %collective-permute-start.10) | collective-permute-done | bytes 458784 | tf_op jit(solution)/shard_map/ppermute | solution.py:241
  67.0 2.9 %shard_map.125 = bf16[256,256]{1,0:T(8,128)(2,1)S(1)} custom-call(bf16[256,896]{1,0:T(8,128)(2,1)} %collective-permute-done.refs_0_, bf16[256,896]{1,0:T(8,128)(2,1)S(1)} %collective-permute-done.10.refs_1_, bf16[256,896]{1,0:T(8,128)(2,1)S(1)} %collective-permute-done.11.refs_2_, bf16[256,896]{1,0:T(8,128)(2,1)} %collective-permute-done.2.refs_3_, ...), custom_call_target="tpu_custom_call" | custom-call | flops 939524096 | bytes 5505024 | tf_op jit(solution)/shard_map/pallas_call | solution.py:126
  71.4 2.8 %collective-permute-start.13 = (bf16[384,256]{1,0:T(8,128)(2,1)}, bf16[384,256]{1,0:T(8,128)(2,1)}, u32[]{:S(2)}, u32[]{:S(2)}) collective-permute-start(bf16[384,256]{1,0:T(8,128)(2,1)} %pad_maximum_fusion.4.refs_0_), channel_id=1, source_target_pairs={{0,2},{1,3},{2,0},{3,1},{4,6},{5,7},{6,4},{7,5},{8,10},{9,11},{10,... | collective-permute-start | bytes 589832 | tf_op jit(solution)/shard_map/ppermute | solution.py:241
  74.8 2.0 %collective-permute-done.1.refs_0_ = bf16[256,896]{1,0:T(8,128)(2,1)} collective-permute-done((bf16[256,896]{1,0:T(8,128)(2,1)}, bf16[256,896]{1,0:T(8,128)(2,1)}, u32[]{:S(2)}, u32[]{:S(2)}) %collective-permute-start.1) | collective-permute-done | bytes 458784 | tf_op jit(solution)/shard_map/ppermute | solution.py:241
  76.9 1.5 %copy-done.3 = bf16[1,3584,256]{2,1,0:T(8,128)(2,1)S(1)} copy-done((bf16[1,3584,256]{2,1,0:T(8,128)(2,1)S(1)}, bf16[1,3584,256]{2,1,0:T(8,128)(2,1)}, u32[]{:S(2)}) %copy-start.3) | copy-done | bytes 1835032
  78.4 2.1 %shard_map.123.refs_0_ = bf16[128,256]{1,0:T(8,128)(2,1)S(1)} custom-call(bf16[256,896]{1,0:T(8,128)(2,1)} %collective-permute-done.1.refs_0_, bf16[256,896]{1,0:T(8,128)(2,1)} %collective-permute-done.3.refs_1_, bf16[256,256]{1,0:T(8,128)(2,1)S(1)} %get-tuple-element.79.refs_2_.refs_4_, bf16[3584,256]{1,0:T(8,128)(2,1)S(1)} %bitcast.45, ...), custom_call_target="tpu_custom_call" | custom-call | flops 469762048 | bytes 4587520 | tf_op jit(solution)/shard_map/pallas_call | solution.py:126
  81.5 3.3 %collective-permute-start.5 = (bf16[128,256]{1,0:T(8,128)(2,1)S(1)}, bf16[128,256]{1,0:T(8,128)(2,1)S(1)}, u32[]{:S(2)}, u32[]{:S(2)}) collective-permute-start(bf16[128,256]{1,0:T(8,128)(2,1)S(1)} %shard_map.123.refs_0_), channel_id=1, source_target_pairs={{0,2},{1,3},{2,0},{3,1},{4,6},{5,7},{6,4},{7,5},{8,10},{9,11},{10,... | collective-permute-start | bytes 196616 | tf_op jit(solution)/shard_map/ppermute | solution.py:241
  84.9 1.5 %collective-permute-done.13.refs_2_ = bf16[384,256]{1,0:T(8,128)(2,1)} collective-permute-done((bf16[384,256]{1,0:T(8,128)(2,1)}, bf16[384,256]{1,0:T(8,128)(2,1)}, u32[]{:S(2)}, u32[]{:S(2)}) %collective-permute-start.13) | collective-permute-done | bytes 196640 | tf_op jit(solution)/shard_map/ppermute | solution.py:241
  86.4 2.6 %shard_map.126.refs_8_ = f32[512,896]{1,0:T(8,128)S(1)} custom-call(bf16[384,256]{1,0:T(8,128)(2,1)} %pad_maximum_fusion.4.refs_0_, bf16[384,256]{1,0:T(8,128)(2,1)} %collective-permute-done.12.refs_1_, bf16[384,256]{1,0:T(8,128)(2,1)} %collective-permute-done.13.refs_2_, bf16[384,256]{1,0:T(8,128)(2,1)} %collective-permute-done.14.refs_3_, ...), custom_call_target="tpu_custom_call" | custom-call | flops 748683264 | bytes 5734400 | tf_op jit(solution)/shard_map/pallas_call | solution.py:184
  89.1 3.2 %shard_map.127 = bf16[512,896]{1,0:T(8,128)(2,1)} custom-call(bf16[128,256]{1,0:T(8,128)(2,1)S(1)} %shard_map.123.refs_0_, bf16[128,256]{1,0:T(8,128)(2,1)S(1)} %collective-permute-done.4.refs_1_, bf16[128,256]{1,0:T(8,128)(2,1)S(1)} %collective-permute-done.5.refs_2_, bf16[128,256]{1,0:T(8,128)(2,1)S(1)} %collective-permute-done.6.refs_3_, ...), custom_call_target="tpu_custom_call" | custom-call | flops 719323136 | bytes 2752512 | tf_op jit(solution)/shard_map/pallas_call | solution.py:201
  94.0 11.9 %all-to-all-start.1 = ((bf16[64,8,896]{2,1,0:T(8,128)(2,1)}), bf16[64,8,896]{2,1,0:T(8,128)(2,1)}, u32[]{:S(2)}, u32[]{:S(2)}) async-start(bf16[64,8,896]{2,1,0:T(8,128)(2,1)} %bitcast.8), calls=%async_computation.1 | async-start | bytes 1835008 | tf_op jit(solution)/shard_map/all_to_all | solution.py:297
  108.5 2.8 %collective-permute-start.16 = (bf16[8,32,512]{2,1,0:T(8,128)(2,1)}, bf16[8,32,512]{2,1,0:T(8,128)(2,1)S(1)}, u32[]{:S(2)}, u32[]{:S(2)}) collective-permute-start(bf16[8,32,512]{2,1,0:T(8,128)(2,1)} %get-tuple-element.57), channel_id=1, source_target_pairs={{0,2},{1,3},{2,0},{3,1},{4,6},{5,7},{6,4},{7,5},{8,10},{9,11},{10,... | collective-permute-start | bytes 786440 | tf_op jit(solution)/shard_map/ppermute | solution.py:241
  111.8 4.4 %collective-permute-done.15 = bf16[8,32,512]{2,1,0:T(8,128)(2,1)} collective-permute-done((bf16[8,32,512]{2,1,0:T(8,128)(2,1)}, bf16[8,32,512]{2,1,0:T(8,128)(2,1)}, u32[]{:S(2)}, u32[]{:S(2)}) %collective-permute-start.15) | collective-permute-done | bytes 262176 | tf_op jit(solution)/shard_map/ppermute | solution.py:241
  117.1 4.9 %collective-permute-done.16 = bf16[8,32,512]{2,1,0:T(8,128)(2,1)S(1)} collective-permute-done((bf16[8,32,512]{2,1,0:T(8,128)(2,1)}, bf16[8,32,512]{2,1,0:T(8,128)(2,1)S(1)}, u32[]{:S(2)}, u32[]{:S(2)}) %collective-permute-start.16) | collective-permute-done | bytes 262176 | tf_op jit(solution)/shard_map/ppermute | solution.py:241
  123.3 8.3 %all-to-all-done.1 = bf16[64,8,896]{2,1,0:T(8,128)(2,1)} async-done(((bf16[64,8,896]{2,1,0:T(8,128)(2,1)}), bf16[64,8,896]{2,1,0:T(8,128)(2,1)}, u32[]{:S(2)}, u32[]{:S(2)}) %all-to-all-start.1) | async-done | bytes 917536 | tf_op jit(solution)/shard_map/all_to_all | solution.py:297
  131.6 1.6 %fusion.11 = f32[96,896]{1,0:T(8,128)S(1)} fusion(bf16[512,896]{1,0:T(8,128)(2,1)} %bitcast.9, bf16[32,512]{0,1:T(8,128)(2,1)S(1)} %get-tuple-element.62, bf16[32,512]{0,1:T(8,128)(2,1)S(1)} %get-tuple-element.63, bf16[32,512]{0,1:T(8,128)(2,1)S(1)} %get-tuple-element.61), kind=kOutput, calls=%fused_computation.33 | convolution fusion | flops 88375296 | bytes 1359872 | tf_op jit(solution)/shard_map/dot_general | solution.py:333
  133.3 1.8 %collective-permute-start.18 = (bf16[8,896]{1,0:T(8,128)(2,1)S(1)}, bf16[8,896]{1,0:T(8,128)(2,1)S(1)}, u32[]{:S(2)}, u32[]{:S(2)}) collective-permute-start(bf16[8,896]{1,0:T(8,128)(2,1)S(1)} %get-tuple-element.67), channel_id=1, source_target_pairs={{0,3},{1,0},{2,1},{3,2},{4,7},{5,4},{6,5},{7,6},{8,11},{9,8},{10,9... | collective-permute-start | bytes 43016 | tf_op jit(solution)/shard_map/ppermute | solution.py:241
  136.0 3.3 %collective-permute-done.19 = bf16[8,896]{1,0:T(8,128)(2,1)S(1)} collective-permute-done((bf16[8,896]{1,0:T(8,128)(2,1)S(1)}, bf16[8,896]{1,0:T(8,128)(2,1)S(1)}, u32[]{:S(2)}, u32[]{:S(2)}) %collective-permute-start.19) | collective-permute-done | bytes 14368 | tf_op jit(solution)/shard_map/ppermute | solution.py:241
  (97 shorter events, 21.7 us)
Async XLA Ops:
  0.6 26.2 %copy-start = (bf16[32,32,512]{2,1,0:T(8,128)(2,1)S(1)}, bf16[32,32,512]{2,1,0:T(8,128)(2,1)}, u32[]{:S(2)}) copy-start(bf16[32,32,512]{2,1,0:T(8,128)(2,1)} %param.11) | copy-start | bytes 3145732
  2.2 17.0 %copy-start.8 = (bf16[1,256,3584]{2,1,0:T(8,128)(2,1)S(1)}, bf16[1,256,3584]{2,1,0:T(8,128)(2,1)}, u32[]{:S(2)}) copy-start(bf16[1,256,3584]{2,1,0:T(8,128)(2,1)} %param.21) | copy-start | bytes 5505028
  3.8 38.8 %all-to-all-start = ((bf16[64,8,896]{2,1,0:T(8,128)(2,1)}), bf16[64,8,896]{2,1,0:T(8,128)(2,1)}, u32[]{:S(2)}, u32[]{:S(2)}) async-start(bf16[64,8,896]{2,1,0:T(8,128)(2,1)} %bitcast), calls=%async_computation | async-start | bytes 1835008 | tf_op jit(solution)/shard_map/all_to_all | solution.py:247
  17.0 9.2 %copy-start.11 = (bf16[32,2048]{1,0:T(8,128)(2,1)S(1)}, bf16[32,2048]{1,0:T(8,128)(2,1)}, u32[]{:S(2)}) copy-start(bf16[32,2048]{1,0:T(8,128)(2,1)} %param.12) | copy-start | bytes 393220
  17.0 9.5 %copy-start.12 = (s32[32]{0:T(128)S(1)}, s32[32]{0:T(128)}, u32[]{:S(2)}) copy-start(s32[32]{0:T(128)} %param.15) | copy-start | bytes 388
  17.0 9.6 %copy-start.10 = (bf16[32,64,128]{2,1,0:T(8,128)(2,1)S(1)}, bf16[32,64,128]{2,1,0:T(8,128)(2,1)}, u32[]{:S(2)}) copy-start(bf16[32,64,128]{2,1,0:T(8,128)(2,1)} %param.14) | copy-start | bytes 1572868
  21.3 28.7 %collective-permute-start.7 = (bf16[272,896]{1,0:T(8,128)(2,1)}, bf16[272,896]{1,0:T(8,128)(2,1)}, u32[]{:S(2)}, u32[]{:S(2)}) collective-permute-start(bf16[272,896]{1,0:T(8,128)(2,1)} %get-tuple-element.69), channel_id=1, source_target_pairs={{0,1},{1,2},{2,3},{3,0},{4,5},{5,6},{6,7},{7,4},{8,9},{9,10},{10,1... | collective-permute-start | bytes 1462280 | tf_op jit(solution)/shard_map/ppermute | solution.py:241
  22.6 27.4 %collective-permute-start.8 = (bf16[272,896]{1,0:T(8,128)(2,1)}, bf16[272,896]{1,0:T(8,128)(2,1)}, u32[]{:S(2)}, u32[]{:S(2)}) collective-permute-start(bf16[272,896]{1,0:T(8,128)(2,1)} %get-tuple-element.70), channel_id=1, source_target_pairs={{0,2},{1,3},{2,0},{3,1},{4,6},{5,7},{6,4},{7,5},{8,10},{9,11},{10,... | collective-permute-start | bytes 1462280 | tf_op jit(solution)/shard_map/ppermute | solution.py:241
  25.2 24.8 %collective-permute-start.9 = (bf16[272,896]{1,0:T(8,128)(2,1)}, bf16[272,896]{1,0:T(8,128)(2,1)}, u32[]{:S(2)}, u32[]{:S(2)}) collective-permute-start(bf16[272,896]{1,0:T(8,128)(2,1)} %get-tuple-element.68), channel_id=1, source_target_pairs={{0,3},{1,0},{2,1},{3,2},{4,7},{5,4},{6,5},{7,6},{8,11},{9,8},{10,9... | collective-permute-start | bytes 1462280 | tf_op jit(solution)/shard_map/ppermute | solution.py:241
  31.4 16.1 %copy-start.1 = (bf16[1,3584,256]{2,1,0:T(8,128)(2,1)S(1)}, bf16[1,3584,256]{2,1,0:T(8,128)(2,1)}, u32[]{:S(2)}) copy-start(bf16[1,3584,256]{2,1,0:T(8,128)(2,1)} %param.19) | copy-start | bytes 5505028
  43.9 13.3 %collective-permute-start = (bf16[256,896]{1,0:T(8,128)(2,1)S(1)}, bf16[256,896]{1,0:T(8,128)(2,1)}, u32[]{:S(2)}, u32[]{:S(2)}) collective-permute-start(bf16[256,896]{1,0:T(8,128)(2,1)S(1)} %get-tuple-element.35.refs_0_), channel_id=1, source_target_pairs={{0,1},{1,2},{2,3},{3,0},{4,5},{5,6},{6,7},{7,4},{8,9},{9,10},{10,1... | collective-permute-start | bytes 1376264 | tf_op jit(solution)/shard_map/ppermute | solution.py:241
  45.3 11.9 %collective-permute-start.2 = (bf16[256,896]{1,0:T(8,128)(2,1)S(1)}, bf16[256,896]{1,0:T(8,128)(2,1)}, u32[]{:S(2)}, u32[]{:S(2)}) collective-permute-start(bf16[256,896]{1,0:T(8,128)(2,1)S(1)} %get-tuple-element.34.refs_1_), channel_id=1, source_target_pairs={{0,3},{1,0},{2,1},{3,2},{4,7},{5,4},{6,5},{7,6},{8,11},{9,8},{10,9... | collective-permute-start | bytes 1376264 | tf_op jit(solution)/shard_map/ppermute | solution.py:241
  50.0 16.9 %collective-permute-start.10 = (bf16[256,896]{1,0:T(8,128)(2,1)S(1)}, bf16[256,896]{1,0:T(8,128)(2,1)S(1)}, u32[]{:S(2)}, u32[]{:S(2)}) collective-permute-start(bf16[256,896]{1,0:T(8,128)(2,1)S(1)} %get-tuple-element.34.refs_1_), channel_id=1, source_target_pairs={{0,1},{1,2},{2,3},{3,0},{4,5},{5,6},{6,7},{7,4},{8,9},{9,10},{10,1... | collective-permute-start | bytes 1376264 | tf_op jit(solution)/shard_map/ppermute | solution.py:241
  50.1 16.9 %collective-permute-start.11 = (bf16[256,896]{1,0:T(8,128)(2,1)S(1)}, bf16[256,896]{1,0:T(8,128)(2,1)S(1)}, u32[]{:S(2)}, u32[]{:S(2)}) collective-permute-start(bf16[256,896]{1,0:T(8,128)(2,1)S(1)} %get-tuple-element.35.refs_0_), channel_id=1, source_target_pairs={{0,3},{1,0},{2,1},{3,2},{4,7},{5,4},{6,5},{7,6},{8,11},{9,8},{10,9... | collective-permute-start | bytes 1376264 | tf_op jit(solution)/shard_map/ppermute | solution.py:241
  57.2 19.7 %collective-permute-start.1 = (bf16[256,896]{1,0:T(8,128)(2,1)}, bf16[256,896]{1,0:T(8,128)(2,1)}, u32[]{:S(2)}, u32[]{:S(2)}) collective-permute-start(bf16[256,896]{1,0:T(8,128)(2,1)} %collective-permute-done.refs_0_), channel_id=1, source_target_pairs={{0,1},{1,2},{2,3},{3,0},{4,5},{5,6},{6,7},{7,4},{8,9},{9,10},{10,1... | collective-permute-start | bytes 1376264 | tf_op jit(solution)/shard_map/ppermute | solution.py:241
  57.2 19.7 %collective-permute-start.3 = (bf16[256,896]{1,0:T(8,128)(2,1)}, bf16[256,896]{1,0:T(8,128)(2,1)}, u32[]{:S(2)}, u32[]{:S(2)}) collective-permute-start(bf16[256,896]{1,0:T(8,128)(2,1)} %collective-permute-done.2.refs_3_), channel_id=1, source_target_pairs={{0,3},{1,0},{2,1},{3,2},{4,7},{5,4},{6,5},{7,6},{8,11},{9,8},{10,9... | collective-permute-start | bytes 1376264 | tf_op jit(solution)/shard_map/ppermute | solution.py:241
  70.5 14.3 %collective-permute-start.12 = (bf16[384,256]{1,0:T(8,128)(2,1)}, bf16[384,256]{1,0:T(8,128)(2,1)}, u32[]{:S(2)}, u32[]{:S(2)}) collective-permute-start(bf16[384,256]{1,0:T(8,128)(2,1)} %pad_maximum_fusion.4.refs_0_), channel_id=1, source_target_pairs={{0,1},{1,2},{2,3},{3,0},{4,5},{5,6},{6,7},{7,4},{8,9},{9,10},{10,1... | collective-permute-start | bytes 589832 | tf_op jit(solution)/shard_map/ppermute | solution.py:241
  71.4 15.0 %collective-permute-start.13 = (bf16[384,256]{1,0:T(8,128)(2,1)}, bf16[384,256]{1,0:T(8,128)(2,1)}, u32[]{:S(2)}, u32[]{:S(2)}) collective-permute-start(bf16[384,256]{1,0:T(8,128)(2,1)} %pad_maximum_fusion.4.refs_0_), channel_id=1, source_target_pairs={{0,2},{1,3},{2,0},{3,1},{4,6},{5,7},{6,4},{7,5},{8,10},{9,11},{10,... | collective-permute-start | bytes 589832 | tf_op jit(solution)/shard_map/ppermute | solution.py:241
  74.2 12.2 %collective-permute-start.14 = (bf16[384,256]{1,0:T(8,128)(2,1)}, bf16[384,256]{1,0:T(8,128)(2,1)}, u32[]{:S(2)}, u32[]{:S(2)}) collective-permute-start(bf16[384,256]{1,0:T(8,128)(2,1)} %pad_maximum_fusion.4.refs_0_), channel_id=1, source_target_pairs={{0,3},{1,0},{2,1},{3,2},{4,7},{5,4},{6,5},{7,6},{8,11},{9,8},{10,9... | collective-permute-start | bytes 589832 | tf_op jit(solution)/shard_map/ppermute | solution.py:241
  78.4 10.7 %copy-start.4 = (bf16[256,256]{1,0:T(8,128)(2,1)S(1)}, bf16[256,256]{1,0:T(8,128)(2,1)}, u32[]{:S(2)}) copy-start(bf16[256,256]{1,0:T(8,128)(2,1)} %get-tuple-element.78.refs_9_) | copy-start | bytes 393220
  80.5 8.6 %collective-permute-start.4 = (bf16[128,256]{1,0:T(8,128)(2,1)S(1)}, bf16[128,256]{1,0:T(8,128)(2,1)S(1)}, u32[]{:S(2)}, u32[]{:S(2)}) collective-permute-start(bf16[128,256]{1,0:T(8,128)(2,1)S(1)} %shard_map.123.refs_0_), channel_id=1, source_target_pairs={{0,1},{1,2},{2,3},{3,0},{4,5},{5,6},{6,7},{7,4},{8,9},{9,10},{10,1... | collective-permute-start | bytes 196616 | tf_op jit(solution)/shard_map/ppermute | solution.py:241
  81.5 7.6 %collective-permute-start.5 = (bf16[128,256]{1,0:T(8,128)(2,1)S(1)}, bf16[128,256]{1,0:T(8,128)(2,1)S(1)}, u32[]{:S(2)}, u32[]{:S(2)}) collective-permute-start(bf16[128,256]{1,0:T(8,128)(2,1)S(1)} %shard_map.123.refs_0_), channel_id=1, source_target_pairs={{0,2},{1,3},{2,0},{3,1},{4,6},{5,7},{6,4},{7,5},{8,10},{9,11},{10,... | collective-permute-start | bytes 196616 | tf_op jit(solution)/shard_map/ppermute | solution.py:241
  84.9 4.3 %collective-permute-start.6 = (bf16[128,256]{1,0:T(8,128)(2,1)S(1)}, bf16[128,256]{1,0:T(8,128)(2,1)S(1)}, u32[]{:S(2)}, u32[]{:S(2)}) collective-permute-start(bf16[128,256]{1,0:T(8,128)(2,1)S(1)} %shard_map.123.refs_0_), channel_id=1, source_target_pairs={{0,3},{1,0},{2,1},{3,2},{4,7},{5,4},{6,5},{7,6},{8,11},{9,8},{10,9... | collective-permute-start | bytes 196616 | tf_op jit(solution)/shard_map/ppermute | solution.py:241
  89.1 17.3 %copy-start.7 = (bf16[32,32,512]{2,1,0:T(8,128)(2,1)S(1)}, bf16[32,32,512]{2,1,0:T(8,128)(2,1)}, u32[]{:S(2)}) copy-start(bf16[32,32,512]{2,1,0:T(8,128)(2,1)} %convolution_convert_fusion) | copy-start | bytes 3145732
  94.0 37.6 %all-to-all-start.1 = ((bf16[64,8,896]{2,1,0:T(8,128)(2,1)}), bf16[64,8,896]{2,1,0:T(8,128)(2,1)}, u32[]{:S(2)}, u32[]{:S(2)}) async-start(bf16[64,8,896]{2,1,0:T(8,128)(2,1)} %bitcast.8), calls=%async_computation.1 | async-start | bytes 1835008 | tf_op jit(solution)/shard_map/all_to_all | solution.py:297
  107.3 8.9 %collective-permute-start.15 = (bf16[8,32,512]{2,1,0:T(8,128)(2,1)}, bf16[8,32,512]{2,1,0:T(8,128)(2,1)}, u32[]{:S(2)}, u32[]{:S(2)}) collective-permute-start(bf16[8,32,512]{2,1,0:T(8,128)(2,1)} %get-tuple-element.58), channel_id=1, source_target_pairs={{0,1},{1,2},{2,3},{3,0},{4,5},{5,6},{6,7},{7,4},{8,9},{9,10},{10,1... | collective-permute-start | bytes 786440 | tf_op jit(solution)/shard_map/ppermute | solution.py:241
  108.5 13.5 %collective-permute-start.16 = (bf16[8,32,512]{2,1,0:T(8,128)(2,1)}, bf16[8,32,512]{2,1,0:T(8,128)(2,1)S(1)}, u32[]{:S(2)}, u32[]{:S(2)}) collective-permute-start(bf16[8,32,512]{2,1,0:T(8,128)(2,1)} %get-tuple-element.57), channel_id=1, source_target_pairs={{0,2},{1,3},{2,0},{3,1},{4,6},{5,7},{6,4},{7,5},{8,10},{9,11},{10,... | collective-permute-start | bytes 786440 | tf_op jit(solution)/shard_map/ppermute | solution.py:241
  111.3 12.0 %collective-permute-start.17 = (bf16[8,32,512]{2,1,0:T(8,128)(2,1)}, bf16[8,32,512]{2,1,0:T(8,128)(2,1)S(1)}, u32[]{:S(2)}, u32[]{:S(2)}) collective-permute-start(bf16[8,32,512]{2,1,0:T(8,128)(2,1)} %get-tuple-element.56), channel_id=1, source_target_pairs={{0,3},{1,0},{2,1},{3,2},{4,7},{5,4},{6,5},{7,6},{8,11},{9,8},{10,9... | collective-permute-start | bytes 786440 | tf_op jit(solution)/shard_map/ppermute | solution.py:241
  123.3 16.8 %copy-start.9 = (bf16[8,4,32,512]{3,2,1,0:T(8,128)(2,1)}, bf16[8,4,32,512]{3,2,1,0:T(8,128)(2,1)S(1)}, u32[]{:S(2)}) copy-start(bf16[8,4,32,512]{3,2,1,0:T(8,128)(2,1)S(1)} %bitcast_dynamic-update-slice_fusion) | copy-start | bytes 3145732
  133.3 2.7 %collective-permute-start.18 = (bf16[8,896]{1,0:T(8,128)(2,1)S(1)}, bf16[8,896]{1,0:T(8,128)(2,1)S(1)}, u32[]{:S(2)}, u32[]{:S(2)}) collective-permute-start(bf16[8,896]{1,0:T(8,128)(2,1)S(1)} %get-tuple-element.67), channel_id=1, source_target_pairs={{0,3},{1,0},{2,1},{3,2},{4,7},{5,4},{6,5},{7,6},{8,11},{9,8},{10,9... | collective-permute-start | bytes 43016 | tf_op jit(solution)/shard_map/ppermute | solution.py:241
  135.2 4.2 %collective-permute-start.19 = (bf16[8,896]{1,0:T(8,128)(2,1)S(1)}, bf16[8,896]{1,0:T(8,128)(2,1)S(1)}, u32[]{:S(2)}, u32[]{:S(2)}) collective-permute-start(bf16[8,896]{1,0:T(8,128)(2,1)S(1)} %get-tuple-element.66), channel_id=1, source_target_pairs={{0,2},{1,3},{2,0},{3,1},{4,6},{5,7},{6,4},{7,5},{8,10},{9,11},{10,... | collective-permute-start | bytes 43016 | tf_op jit(solution)/shard_map/ppermute | solution.py:241
  135.4 3.9 %collective-permute-start.20 = (bf16[8,896]{1,0:T(8,128)(2,1)S(1)}, bf16[8,896]{1,0:T(8,128)(2,1)S(1)}, u32[]{:S(2)}, u32[]{:S(2)}) collective-permute-start(bf16[8,896]{1,0:T(8,128)(2,1)S(1)} %get-tuple-element.64), channel_id=1, source_target_pairs={{0,1},{1,2},{2,3},{3,0},{4,5},{5,6},{6,7},{7,4},{8,9},{9,10},{10,1... | collective-permute-start | bytes 43016 | tf_op jit(solution)/shard_map/ppermute | solution.py:241
  (4 other events, 4.6 us)

commit v3 on v2

--- a/solution.py
+++ b/solution.py
@@ -39,17 +39,6 @@
     middle = rest.astype(jnp.bfloat16)
     low = (rest - middle.astype(jnp.float32)).astype(jnp.bfloat16)
     return high, middle, low
-
-
-def slot_masks(routes, experts):
-    named = jnp.any(routes[..., None] == jnp.arange(experts, dtype=jnp.int32), axis=-2)
-    rows = routes.shape[-2]
-    counts = named.astype(jnp.int32)
-    earlier = [jnp.zeros_like(counts[..., 0, :])]
-    for row in range(1, rows):
-        earlier.append(earlier[-1] + counts[..., row - 1, :])
-    earlier = jnp.stack(earlier, axis=-2)
-    return named[..., None] & (earlier[..., None] == jnp.arange(CAP, dtype=jnp.int32))
 
 
 vmem_params = pltpu.CompilerParams(vmem_limit_bytes=40 * 1024 * 1024)
@@ -91,7 +80,7 @@
         out_shape=jax.ShapeDtypeStruct((total, part), rows.dtype),
         in_specs=[whole] * 2,
         out_specs=whole,
-        compiler_params=vmem_params,
+        compiler_params=pltpu.CompilerParams(vmem_limit_bytes=58 * 1024 * 1024),
         cost_estimate=pl.CostEstimate(
             flops=2 * total * part * rows.shape[0] * shares,
             bytes_accessed=2 * total * part,
@@ -138,9 +127,31 @@
     )(*halves, order, w_gate, w_up)
 
 
+def stack_kernel(shares, *refs):
+    weights, out_ref = refs[:shares], refs[shares]
+    units = out_ref.shape[0] // shares
+    for s in range(shares):
+        out_ref[pl.ds(s * units, units), :] = weights[s][pl.ds(0, units), :]
+
+
+def stack_shares(weights, units):
+    shares, part = len(weights), weights[0].shape[1]
+    return pl.pallas_call(
+        functools.partial(stack_kernel, shares),
+        out_shape=jax.ShapeDtypeStruct((shares * units, part), jnp.bfloat16),
+        in_specs=[whole] * shares,
+        out_specs=whole,
+        compiler_params=vmem_params,
+        cost_estimate=pl.CostEstimate(
+            flops=0, bytes_accessed=4 * shares * units * part, transcendentals=0
+        ),
+    )(*weights)
+
+
 def down_early_kernel(shares, *refs):
-    early, weights, out_ref = refs[:shares], refs[shares : 2 * shares], refs[2 * shares]
+    early, weights_ref, out_ref = refs[:shares], refs[shares], refs[shares + 1]
     slots = out_ref.shape[0] // shares
+    count = early[0].shape[1]
     for block in range(shares):
         total = None
         for s in range(shares):
@@ -149,24 +160,20 @@
                 continue
             place = of_sender - (of_sender > shares // 2)
             units = early[s][pl.ds(place * slots, slots), :]
-            term = jnp.dot(
-                units, weights[s][: units.shape[1], :], preferred_element_type=jnp.float32
-            )
+            weights = weights_ref[pl.ds(s * count, count), :]
+            term = jnp.dot(units, weights, preferred_element_type=jnp.float32)
             total = term if total is None else total + term
         out_ref[pl.ds(block * slots, slots), :] = total
 
 
 def down_late_kernel(shares, *refs):
-    late, weights = refs[:shares], refs[shares : 2 * shares]
-    early_ref, order_ref, out_ref, plain = refs[2 * shares :]
-    slots = late[0].shape[0]
+    late, (weights_ref, early_ref, order_ref, out_ref, plain) = refs[:shares], refs[shares:]
+    slots, count = late[0].shape
     half = slots // 2
     for block in range(shares):
         s = (block - shares // 2) % shares
-        units = late[s][...]
-        term = jnp.dot(
-            units, weights[s][: units.shape[1], :], preferred_element_type=jnp.float32
-        )
+        weights = weights_ref[pl.ds(s * count, count), :]
+        term = jnp.dot(late[s][...], weights, preferred_element_type=jnp.float32)
         total = (early_ref[pl.ds(block * slots, slots), :] + term).astype(plain.dtype)
         plain[pl.ds(block * half, half), :] = total[:half]
         plain[pl.ds((shares + block) * half, half), :] = total[half:]
@@ -178,39 +185,130 @@
 
 
 def down_early(early, weights):
-    shares = len(weights)
-    units, part = weights[0].shape
+    shares = len(early)
+    units, part = early[0].shape[1], weights.shape[1]
     rows = early[0].shape[0] // (shares - 1) * shares
     return pl.pallas_call(
         functools.partial(down_early_kernel, shares),
         out_shape=jax.ShapeDtypeStruct((rows, part), jnp.float32),
-        in_specs=[whole] * (2 * shares),
+        in_specs=[whole] * (shares + 1),
         out_specs=whole,
         compiler_params=vmem_params,
         cost_estimate=pl.CostEstimate(
             flops=2 * rows * part * (shares - 1) * units,
-            bytes_accessed=4 * rows * part + 4 * units * part * shares,
+            bytes_accessed=4 * rows * part + 2 * units * part * shares,
             transcendentals=0,
         ),
-    )(*early, *weights)
+    )(*early, weights)
 
 
 def down_late(late, weights, early, order):
-    shares = len(weights)
+    shares = len(late)
     rows, part = early.shape
     return pl.pallas_call(
         functools.partial(down_late_kernel, shares),
         out_shape=jax.ShapeDtypeStruct((rows, part), jnp.bfloat16),
-        in_specs=[whole] * (2 * shares + 2),
+        in_specs=[whole] * (shares + 3),
         out_specs=whole,
         scratch_shapes=[pltpu.VMEM((rows, part), jnp.bfloat16)],
         compiler_params=vmem_params,
         cost_estimate=pl.CostEstimate(
-            flops=2 * rows * part * (weights[0].shape[0] + rows),
+            flops=2 * rows * part * (late[0].shape[1] + rows),
             bytes_accessed=6 * rows * part,
             transcendentals=0,
         ),
-    )(*late, *weights, early, order)
+    )(*late, weights, early, order)
+
+
+def place_kernel(shares, first_ref, *refs):
+    pieces, out_ref = refs[:shares], refs[shares]
+    part = pieces[0].shape[1]
+    for d in range(shares):
+        quarter = lax.rem(first_ref[0] + d, shares)
+        place = pl.ds(pl.multiple_of(quarter * part, 128), part)
+        out_ref[:, place] = pieces[d][...]
+
+
+def place_quarters(first, pieces):
+    shares = len(pieces)
+    rows, part = pieces[0].shape
+    return pl.pallas_call(
+        functools.partial(place_kernel, shares),
+        out_shape=jax.ShapeDtypeStruct((rows, shares * part), pieces[0].dtype),
+        in_specs=[pl.BlockSpec(memory_space=pltpu.SMEM)] + [whole] * shares,
+        out_specs=whole,
+        compiler_params=vmem_params,
+        cost_estimate=pl.CostEstimate(
+            flops=0, bytes_accessed=4 * rows * shares * part, transcendentals=0
+        ),
+    )(first.reshape(1), *pieces)
+
+
+def gates_kernel(shares, chosen, *refs):
+    f32 = jnp.float32
+    infos, out_ref = refs[:shares], refs[shares]
+    rows = out_ref.shape[0] // (3 * shares)
+    lane = lax.broadcasted_iota(jnp.int32, (rows, out_ref.shape[1]), 1)
+    chunk = shares * CAP
+    expert, slot, block = lane // chunk, lane % CAP, lane % chunk // CAP
+    expert, slot = expert.astype(f32), slot.astype(f32)
+    before = lax.broadcasted_iota(jnp.int32, (rows, rows), 0) > lax.broadcasted_iota(
+        jnp.int32, (rows, rows), 1
+    )
+    parts = []
+    for d in range(shares):
+        info = infos[d][...].astype(f32)[:rows]
+        named = jnp.zeros(lane.shape, f32)
+        gate = jnp.zeros(lane.shape, f32)
+        for k in range(chosen):
+            here = info[:, k : k + 1] == expert
+            value = (info[:, chosen + k : chosen + k + 1] + info[:, 2 * chosen + k : 2 * chosen + k + 1]) + info[
+                :, 3 * chosen + k : 3 * chosen + k + 1
+            ]
+            named = jnp.where(here, 1.0, named)
+            gate = jnp.where(here, value, gate)
+        earlier = jnp.dot(before.astype(f32), named, preferred_element_type=f32)
+        taken = (earlier == slot) & (block == d)
+        parts.append(jnp.where(taken, gate, 0.0))
+    out_ref[...] = jnp.concatenate(split3(jnp.concatenate(parts, axis=0)), axis=0)
+
+
+def gates_of_slots(infos, units, rows, chosen, experts):
+    shares = len(infos)
+    slots = experts * shares * CAP
+    below = pl.BlockSpec((INFO, 128), lambda n: (units // INFO, 0))
+    return pl.pallas_call(
+        functools.partial(gates_kernel, shares, chosen),
+        grid=(1,),
+        out_shape=jax.ShapeDtypeStruct((3 * shares * rows, slots), jnp.bfloat16),
+        in_specs=[below] * shares,
+        out_specs=pl.BlockSpec((3 * shares * rows, slots), lambda n: (0, 0)),
+        compiler_params=vmem_params,
+        cost_estimate=pl.CostEstimate(flops=0, bytes_accessed=6 * shares * rows * slots, transcendentals=0),
+    )(*infos)
+
+
+def combine_kernel(shares, gates_ref, values_ref, *outs):
+    sums = jnp.dot(gates_ref[...], values_ref[...], preferred_element_type=jnp.float32)
+    count = sums.shape[0] // 3
+    sums = sums[2 * count :] + sums[count : 2 * count] + sums[:count]
+    rows = count // shares
+    for d in range(shares):
+        outs[d][...] = sums[d * rows : (d + 1) * rows].astype(outs[d].dtype)
+
+
+def combine_slots(gates, values, shares):
+    rows, part = gates.shape[0] // (3 * shares), values.shape[1]
+    return pl.pallas_call(
+        functools.partial(combine_kernel, shares),
+        out_shape=(jax.ShapeDtypeStruct((rows, part), jnp.bfloat16),) * shares,
+        in_specs=[whole] * 2,
+        out_specs=(whole,) * shares,
+        compiler_params=vmem_params,
+        cost_estimate=pl.CostEstimate(
+            flops=2 * gates.size * part, bytes_accessed=2 * values.size, transcendentals=0
+        ),
+    )(gates, values)
 
 
 def per_device(
@@ -284,12 +382,14 @@
     high1, low3 = shift(high, 1), shift(low, 3)
     low2, high2 = shift(low1, 1), shift(high3, 3)
     hidden13 = hidden_of(low1, high1, low3, high3)
+    hidden13, down = lax.optimization_barrier((hidden13, down))
+    stacked = stack_shares(down, units)
     early = jnp.concatenate([hidden0, hidden13], axis=0)
     early = [early] + [shift(early, by) for by in range(1, shares)]
     late = hidden_of(low2, high2)
     late = [late] + [shift(late, by) for by in range(1, shares)]
 
-    expert_out = down_late(late, down, down_early(early, down), sort.T)
+    expert_out = down_late(late, stacked, down_early(early, stacked), sort.T)
     expert_out, local_context, down = lax.optimization_barrier(
         (expert_out, local_context, down)
     )
@@ -317,27 +417,11 @@
             context, context_parts[by][:, None], (0, (me - by) % shares, 0, 0)
         )
 
-    info = jnp.stack([d[units : units + rows, : 4 * chosen] for d in down]).astype(f32)
-    group_routes = info[:, :, :chosen].astype(jnp.int32)
-    group_gates = (info[:, :, chosen : 2 * chosen] + info[:, :, 2 * chosen : 3 * chosen]) + info[
-        :, :, 3 * chosen :
-    ]
-    group_mask = slot_masks(group_routes, experts)
-    match = group_routes[..., None] == jnp.arange(experts, dtype=jnp.int32)
-    gates = jnp.sum(jnp.where(match, group_gates[..., None], 0.0), axis=2)
-    weight = jnp.where(group_mask, gates[..., None], 0.0)
-    same = jnp.arange(shares)[:, None] == jnp.arange(shares)[None, :]
-    combine = jnp.where(same[:, None, None, :, None], weight[:, :, :, None, :], 0.0)
-    combine = combine.reshape(shares * rows, experts * shares * CAP)
+    combine = gates_of_slots(down, units, rows, chosen, experts)
     returned, context, combine = lax.optimization_barrier((returned, context, combine))
-    sums = jnp.dot(
-        jnp.concatenate(split3(combine), axis=0), returned, preferred_element_type=f32
-    ).reshape(3, shares, rows, part)
-    sums = (sums[2] + sums[1] + sums[0]).astype(bf16)
+    sums = combine_slots(combine, returned, shares)
     pieces = [sums[0]] + [shift(sums[d], shares - d) for d in range(1, shares)]
-    wide = jnp.concatenate(pieces + pieces, axis=1)
-    moe_output = lax.dynamic_slice(wide, (0, ((shares - me) % shares) * part), (rows, width))
-
+    moe_output = place_quarters(me, pieces)
     return (context.reshape(rows, shares * heads, latent), moe_output)
 
 

time: 141 us -> 132 us (0.936)
  other arithmetic: 8.13 us -> 3.24 us
  waiting for transfers between devices: 41.5 us -> 45.6 us
  local copies, waits for them, and re-layouts: 11.3 us -> 7.81 us
    pallas_call x0 -> x4, Pallas kernels: none -> 3.32 us  [the longest x1 1.46 us: stack_shares(): pl.pallas_call(functools.partial(stack_kernel, shares), out_shape=jax.Sha...]
    pallas_call x3, Pallas kernels: 5.95 us -> 3.55 us  [hidden_units(): pl.pallas_call(functools.partial(hidden_kernel, count, shares), out_shape...]
    unnamed x32 -> x19, local copies, waits for them, and re-layouts: 4.69 us -> 2.35 us
    ppermute x21, waiting for transfers between devices: 28.9 us -> 30.9 us  [shift(): return lax.ppermute(value, 'tensor', pairs)]
    dynamic_update_slice x5, local copies, waits for them, and re-layouts: 1.14 us -> 2.82 us  [per_device(): lax.dynamic_update_slice(context, context_parts[by][:, None], (0, (me - b...]
    pallas_call x1, Pallas kernels: 2.65 us -> 0.99 us  [down_early(): pl.pallas_call(functools.partial(down_early_kernel, shares), out_shape=ja...]
    dot_general x1 -> x0, matrix products: 1.63 us -> none  [per_device(): jnp.dot(jnp.concatenate(split3(combine), axis=0), returned, preferred_ele...]
    another operation x5 -> x0, local copies, waits for them, and re-layouts: 1.52 us -> none  [the longest x2 1.37 us: per_device(): jnp.stack([d[units:units + rows, :4 * chosen] for d in down]).astype(f32)]
  transfers between devices with their start and end apart: 23 -> 23, of which waited for: 11 -> 12; matrix products, arithmetic and copies ran while one was open for 16% -> 15% of each run, Pallas kernels for 6% -> 5%
where the time goes in v3:
time: 132 us
  starting transfers between devices  51.6 us (39%)
  waiting for transfers between devices  45.6 us (35%)
  Pallas kernels  12.2 us (9%)
  matrix products  10.5 us (8%)
  local copies, waits for them, and re-layouts  7.81 us (6%)
  other arithmetic  3.24 us (2%)
    ppermute x21, waiting for transfers between devices, shift(): return lax.ppermute(value, 'tensor', pairs)  30.9 us
    ppermute x21, starting transfers between devices, shift(): return lax.ppermute(value, 'tensor', pairs)  27.8 us
    all_to_all x1, starting transfers between devices, per_device(): lax.all_to_all(packed.reshape(experts, shares * CAP, part), 'expert', spl...  13.2 us
    all_to_all x1, starting transfers between devices, per_device(): lax.all_to_all(expert_out.reshape(experts, shares * CAP, part), 'expert',...  10.6 us
    all_to_all x1, waiting for transfers between devices, per_device(): lax.all_to_all(expert_out.reshape(experts, shares * CAP, part), 'expert',...  9.03 us
    all_to_all x1, waiting for transfers between devices, per_device(): lax.all_to_all(packed.reshape(experts, shares * CAP, part), 'expert', spl...  5.71 us
    dot_general x1, matrix products, attend(): jnp.einsum('rhp,rpl->rhl', weights, cache_latent, preferred_element_type=...  5.52 us
    dot_general x1, matrix products, attend(): jnp.einsum('rhl,rpl->rhp', query_latent, cache_latent, preferred_element_...  3.73 us
  transfers between devices with their start and end apart: 23, of which 12 were waited for; matrix products, arithmetic and copies ran while one was open for 15% of the time, Pallas kernels for 5%

profile of v3, /device:TPU:1, one launch (start us, length us, event | category | flops | bytes accessed | tf_op | source)
XLA Modules:
  0.0 131.9 jit_solution(12467879140417286069)
XLA Ops:
  0.7 2.6 %shard_map.122 = bf16[512,896]{1,0:T(8,128)(2,1)} custom-call(s32[8,8]{1,0:T(8,128)} %routes_ref.1, bf16[8,3584]{1,0:T(8,128)(2,1)} %rows_ref.1), custom_call_target="tpu_custom_call" | custom-call | flops 29360128 | bytes 917504 | tf_op jit(solution)/shard_map/pallas_call | solution.py:78
  3.2 13.2 %all-to-all-start = ((bf16[64,8,896]{2,1,0:T(8,128)(2,1)}), bf16[64,8,896]{2,1,0:T(8,128)(2,1)}, u32[]{:S(2)}, u32[]{:S(2)}) async-start(bf16[64,8,896]{2,1,0:T(8,128)(2,1)} %bitcast.40), calls=%async_computation | async-start | bytes 1835008 | tf_op jit(solution)/shard_map/all_to_all | solution.py:345
  18.1 1.2 pad_maximum_fusion
  19.3 1.3 collective-permute-start.7
  20.6 2.6 %collective-permute-start.8 = (bf16[272,896]{1,0:T(8,128)(2,1)}, bf16[272,896]{1,0:T(8,128)(2,1)}, u32[]{:S(2)}, u32[]{:S(2)}) collective-permute-start(bf16[272,896]{1,0:T(8,128)(2,1)} %get-tuple-element.75), channel_id=1, source_target_pairs={{0,2},{1,3},{2,0},{3,1},{4,6},{5,7},{6,4},{7,5},{8,10},{9,11},{10,... | collective-permute-start | bytes 1462280 | tf_op jit(solution)/shard_map/ppermute | solution.py:339
  24.7 1.3 fusion.30
  26.0 3.7 %fusion.4 = f32[32,32,128]{2,1,0:T(8,128)S(1)} fusion(f32[32,32,128]{2,1,0:T(8,128)S(1)} %fusion.30, bf16[32,32,512]{2,1,0:T(8,128)(2,1)S(1)} %copy-done, bf16[32,128,512]{2,1,0:T(8,128)(2,1)} %param.13, pred[32,128]{1,0:T(8,128)(4,1)S(1)} %iota_compare_fusion.4), kind=kOutput, calls=%fused_computation.6 | convolution fusion | flops 134610944 | bytes 6295552 | tf_op jit(solution)/shard_map/rhl,rpl->rhp/dot_general | solution.py:20
  30.9 5.5 %convolution_convert_fusion = bf16[32,32,512]{2,1,0:T(8,128)(2,1)} fusion(bf16[32,128,512]{2,1,0:T(8,128)(2,1)} %param.13, f32[32,32]{1,0:T(8,128)S(1)} %fusion.29, f32[32,32,128]{2,1,0:T(8,128)} %copy-done.5), kind=kOutput, calls=%fused_computation.1 | convolution fusion | flops 135136384 | bytes 5771264 | tf_op jit(solution)/shard_map/rhp,rpl->rhl/dot_general | solution.py:32
  36.4 5.7 %all-to-all-done = bf16[64,8,896]{2,1,0:T(8,128)(2,1)} async-done(((bf16[64,8,896]{2,1,0:T(8,128)(2,1)}), bf16[64,8,896]{2,1,0:T(8,128)(2,1)}, u32[]{:S(2)}, u32[]{:S(2)}) %all-to-all-start) | async-done | bytes 917536 | tf_op jit(solution)/shard_map/all_to_all | solution.py:345
  42.1 1.2 fusion.27
  43.3 1.4 %collective-permute-start = (bf16[256,896]{1,0:T(8,128)(2,1)S(1)}, bf16[256,896]{1,0:T(8,128)(2,1)S(1)}, u32[]{:S(2)}, u32[]{:S(2)}) collective-permute-start(bf16[256,896]{1,0:T(8,128)(2,1)S(1)} %get-tuple-element.39.refs_0_), channel_id=1, source_target_pairs={{0,1},{1,2},{2,3},{3,0},{4,5},{5,6},{6,7},{7,4},{8,9},{9,10},{10,1... | collective-permute-start | bytes 1376264 | tf_op jit(solution)/shard_map/ppermute | solution.py:339
  44.7 1.5 %collective-permute-start.2 = (bf16[256,896]{1,0:T(8,128)(2,1)S(1)}, bf16[256,896]{1,0:T(8,128)(2,1)S(1)}, u32[]{:S(2)}, u32[]{:S(2)}) collective-permute-start(bf16[256,896]{1,0:T(8,128)(2,1)S(1)} %get-tuple-element.38.refs_1_), channel_id=1, source_target_pairs={{0,3},{1,0},{2,1},{3,2},{4,7},{5,4},{6,5},{7,6},{8,11},{9,8},{10,9... | collective-permute-start | bytes 1376264 | tf_op jit(solution)/shard_map/ppermute | solution.py:339
  46.4 1.5 %copy-done.2 = bf16[1,3584,256]{2,1,0:T(8,128)(2,1)S(1)} copy-done((bf16[1,3584,256]{2,1,0:T(8,128)(2,1)S(1)}, bf16[1,3584,256]{2,1,0:T(8,128)(2,1)}, u32[]{:S(2)}) %copy-start.2) | copy-done | bytes 1835032
  48.9 2.7 %collective-permute-start.11 = (bf16[256,896]{1,0:T(8,128)(2,1)S(1)}, bf16[256,896]{1,0:T(8,128)(2,1)S(1)}, u32[]{:S(2)}, u32[]{:S(2)}) collective-permute-start(bf16[256,896]{1,0:T(8,128)(2,1)S(1)} %get-tuple-element.39.refs_0_), channel_id=1, source_target_pairs={{0,3},{1,0},{2,1},{3,2},{4,7},{5,4},{6,5},{7,6},{8,11},{9,8},{10,9... | collective-permute-start | bytes 1376264 | tf_op jit(solution)/shard_map/ppermute | solution.py:339
  51.6 4.9 %collective-permute-done.refs_0_ = bf16[256,896]{1,0:T(8,128)(2,1)S(1)} collective-permute-done((bf16[256,896]{1,0:T(8,128)(2,1)S(1)}, bf16[256,896]{1,0:T(8,128)(2,1)S(1)}, u32[]{:S(2)}, u32[]{:S(2)}) %collective-permute-start) | collective-permute-done | bytes 458784 | tf_op jit(solution)/shard_map/ppermute | solution.py:339
  56.5 2.7 %collective-permute-start.3 = (bf16[256,896]{1,0:T(8,128)(2,1)S(1)}, bf16[256,896]{1,0:T(8,128)(2,1)S(1)}, u32[]{:S(2)}, u32[]{:S(2)}) collective-permute-start(bf16[256,896]{1,0:T(8,128)(2,1)S(1)} %collective-permute-done.2.refs_3_), channel_id=1, source_target_pairs={{0,3},{1,0},{2,1},{3,2},{4,7},{5,4},{6,5},{7,6},{8,11},{9,8},{10,9... | collective-permute-start | bytes 1376264 | tf_op jit(solution)/shard_map/ppermute | solution.py:339
  59.2 7.1 %collective-permute-done.10.refs_1_ = bf16[256,896]{1,0:T(8,128)(2,1)S(1)} collective-permute-done((bf16[256,896]{1,0:T(8,128)(2,1)S(1)}, bf16[256,896]{1,0:T(8,128)(2,1)S(1)}, u32[]{:S(2)}, u32[]{:S(2)}) %collective-permute-start.10) | collective-permute-done | bytes 458784 | tf_op jit(solution)/shard_map/ppermute | solution.py:339
  66.4 1.7 %shard_map.125 = bf16[256,256]{1,0:T(8,128)(2,1)S(1)} custom-call(bf16[256,896]{1,0:T(8,128)(2,1)S(1)} %collective-permute-done.refs_0_, bf16[256,896]{1,0:T(8,128)(2,1)S(1)} %collective-permute-done.10.refs_1_, bf16[256,896]{1,0:T(8,128)(2,1)S(1)} %collective-permute-done.11.refs_2_, bf16[256,896]{1,0:T(8,128)(2,1)S(1)} %collective-permute-done.2.refs_3_, ...), custom_call_target="tpu_custom_call" | custom-call | flops 939524096 | bytes 5505024 | tf_op jit(solution)/shard_map/pallas_call | solution.py:115
  69.1 2.8 %collective-permute-start.13 = (bf16[384,256]{1,0:T(8,128)(2,1)S(1)}, bf16[384,256]{1,0:T(8,128)(2,1)S(1)}, u32[]{:S(2)}, u32[]{:S(2)}) collective-permute-start(bf16[384,256]{1,0:T(8,128)(2,1)S(1)} %constant_dynamic-update-slice_fusion.refs_0_), channel_id=1, source_target_pairs={{0,2},{1,3},{2,0},{3,1},{4,6},{5,7},{6,4},{7,5},{8,10},{9,11},{10,... | collective-permute-start | bytes 589832 | tf_op jit(solution)/shard_map/ppermute | solution.py:339
  72.4 1.5 %shard_map.126.refs_4_ = bf16[1024,896]{1,0:T(8,128)(2,1)S(1)} custom-call(bf16[272,896]{1,0:T(8,128)(2,1)S(1)} %get-tuple-element.53.refs_0_, bf16[272,896]{1,0:T(8,128)(2,1)} %collective-permute-done.7.refs_1_, bf16[272,896]{1,0:T(8,128)(2,1)} %collective-permute-done.8.refs_2_, bf16[272,896]{1,0:T(8,128)(2,1)} %collective-permute-done.9.refs_3_), custom_call_target="tpu_custom_call" | custom-call | bytes 3670016 | tf_op jit(solution)/shard_map/pallas_call | solution.py:139
  73.9 2.3 %collective-permute-done.1.refs_0_ = bf16[256,896]{1,0:T(8,128)(2,1)S(1)} collective-permute-done((bf16[256,896]{1,0:T(8,128)(2,1)S(1)}, bf16[256,896]{1,0:T(8,128)(2,1)S(1)}, u32[]{:S(2)}, u32[]{:S(2)}) %collective-permute-start.1) | collective-permute-done | bytes 458784 | tf_op jit(solution)/shard_map/ppermute | solution.py:339
  78.1 3.3 %collective-permute-start.5 = (bf16[128,256]{1,0:T(8,128)(2,1)S(1)}, bf16[128,256]{1,0:T(8,128)(2,1)S(1)}, u32[]{:S(2)}, u32[]{:S(2)}) collective-permute-start(bf16[128,256]{1,0:T(8,128)(2,1)S(1)} %shard_map.123.refs_0_), channel_id=1, source_target_pairs={{0,2},{1,3},{2,0},{3,1},{4,6},{5,7},{6,4},{7,5},{8,10},{9,11},{10,... | collective-permute-start | bytes 196616 | tf_op jit(solution)/shard_map/ppermute | solution.py:339
  81.8 3.9 %collective-permute-done.13.refs_2_ = bf16[384,256]{1,0:T(8,128)(2,1)S(1)} collective-permute-done((bf16[384,256]{1,0:T(8,128)(2,1)S(1)}, bf16[384,256]{1,0:T(8,128)(2,1)S(1)}, u32[]{:S(2)}, u32[]{:S(2)}) %collective-permute-start.13) | collective-permute-done | bytes 196640 | tf_op jit(solution)/shard_map/ppermute | solution.py:339
  87.6 1.8 %shard_map.128 = bf16[512,896]{1,0:T(8,128)(2,1)} custom-call(bf16[128,256]{1,0:T(8,128)(2,1)S(1)} %shard_map.123.refs_0_, bf16[128,256]{1,0:T(8,128)(2,1)S(1)} %collective-permute-done.4.refs_1_, bf16[128,256]{1,0:T(8,128)(2,1)S(1)} %collective-permute-done.5.refs_2_, bf16[128,256]{1,0:T(8,128)(2,1)S(1)} %collective-permute-done.6.refs_3_, ...), custom_call_target="tpu_custom_call" | custom-call | flops 704643072 | bytes 2752512 | tf_op jit(solution)/shard_map/pallas_call | solution.py:208
  89.4 10.6 %all-to-all-start.1 = ((bf16[64,8,896]{2,1,0:T(8,128)(2,1)}), bf16[64,8,896]{2,1,0:T(8,128)(2,1)S(1)}, u32[]{:S(2)}, u32[]{:S(2)}) async-start(bf16[64,8,896]{2,1,0:T(8,128)(2,1)} %bitcast.8), calls=%async_computation.1 | async-start | bytes 1835008 | tf_op jit(solution)/shard_map/all_to_all | solution.py:397
  100.9 2.1 %collective-permute-start.16 = (bf16[8,32,512]{2,1,0:T(8,128)(2,1)}, bf16[8,32,512]{2,1,0:T(8,128)(2,1)S(1)}, u32[]{:S(2)}, u32[]{:S(2)}) collective-permute-start(bf16[8,32,512]{2,1,0:T(8,128)(2,1)} %get-tuple-element.69), channel_id=1, source_target_pairs={{0,2},{1,3},{2,0},{3,1},{4,6},{5,7},{6,4},{7,5},{8,10},{9,11},{10,... | collective-permute-start | bytes 786440 | tf_op jit(solution)/shard_map/ppermute | solution.py:339
  103.1 1.2 collective-permute-start.17
  105.3 5.1 %collective-permute-done.15 = bf16[8,32,512]{2,1,0:T(8,128)(2,1)} collective-permute-done((bf16[8,32,512]{2,1,0:T(8,128)(2,1)}, bf16[8,32,512]{2,1,0:T(8,128)(2,1)}, u32[]{:S(2)}, u32[]{:S(2)}) %collective-permute-start.15) | collective-permute-done | bytes 262176 | tf_op jit(solution)/shard_map/ppermute | solution.py:339
  111.4 3.5 %collective-permute-done.16 = bf16[8,32,512]{2,1,0:T(8,128)(2,1)S(1)} collective-permute-done((bf16[8,32,512]{2,1,0:T(8,128)(2,1)}, bf16[8,32,512]{2,1,0:T(8,128)(2,1)S(1)}, u32[]{:S(2)}, u32[]{:S(2)}) %collective-permute-start.16) | collective-permute-done | bytes 262176 | tf_op jit(solution)/shard_map/ppermute | solution.py:339
  114.9 1.1 copy.13
  116.7 9.0 %all-to-all-done.1 = bf16[64,8,896]{2,1,0:T(8,128)(2,1)S(1)} async-done(((bf16[64,8,896]{2,1,0:T(8,128)(2,1)}), bf16[64,8,896]{2,1,0:T(8,128)(2,1)S(1)}, u32[]{:S(2)}, u32[]{:S(2)}) %all-to-all-start.1) | async-done | bytes 917536 | tf_op jit(solution)/shard_map/all_to_all | solution.py:397
  128.7 2.4 %collective-permute-done.19.refs_2_ = bf16[8,896]{1,0:T(8,128)(2,1)S(1)} collective-permute-done((bf16[8,896]{1,0:T(8,128)(2,1)S(1)}, bf16[8,896]{1,0:T(8,128)(2,1)S(1)}, u32[]{:S(2)}, u32[]{:S(2)}) %collective-permute-start.19) | collective-permute-done | bytes 14368 | tf_op jit(solution)/shard_map/ppermute | solution.py:339
  (65 shorter events, 18.6 us)
Async XLA Ops:
  0.6 25.3 %copy-start = (bf16[32,32,512]{2,1,0:T(8,128)(2,1)S(1)}, bf16[32,32,512]{2,1,0:T(8,128)(2,1)}, u32[]{:S(2)}) copy-start(bf16[32,32,512]{2,1,0:T(8,128)(2,1)} %param.11) | copy-start | bytes 3145732
  0.6 17.3 %copy-start.6 = (bf16[1,256,3584]{2,1,0:T(8,128)(2,1)S(1)}, bf16[1,256,3584]{2,1,0:T(8,128)(2,1)}, u32[]{:S(2)}) copy-start(bf16[1,256,3584]{2,1,0:T(8,128)(2,1)} %param.21) | copy-start | bytes 5505028
  3.2 38.8 %all-to-all-start = ((bf16[64,8,896]{2,1,0:T(8,128)(2,1)}), bf16[64,8,896]{2,1,0:T(8,128)(2,1)}, u32[]{:S(2)}, u32[]{:S(2)}) async-start(bf16[64,8,896]{2,1,0:T(8,128)(2,1)} %bitcast.40), calls=%async_computation | async-start | bytes 1835008 | tf_op jit(solution)/shard_map/all_to_all | solution.py:345
  16.4 7.9 %copy-start.7 = (bf16[32,2048]{1,0:T(8,128)(2,1)S(1)}, bf16[32,2048]{1,0:T(8,128)(2,1)}, u32[]{:S(2)}) copy-start(bf16[32,2048]{1,0:T(8,128)(2,1)} %param.12) | copy-start | bytes 393220
  16.4 8.2 %copy-start.8 = (s32[32]{0:T(128)S(1)}, s32[32]{0:T(128)}, u32[]{:S(2)}) copy-start(s32[32]{0:T(128)} %param.15) | copy-start | bytes 388
  19.3 29.5 %collective-permute-start.7 = (bf16[272,896]{1,0:T(8,128)(2,1)}, bf16[272,896]{1,0:T(8,128)(2,1)}, u32[]{:S(2)}, u32[]{:S(2)}) collective-permute-start(bf16[272,896]{1,0:T(8,128)(2,1)} %get-tuple-element.74), channel_id=1, source_target_pairs={{0,1},{1,2},{2,3},{3,0},{4,5},{5,6},{6,7},{7,4},{8,9},{9,10},{10,1... | collective-permute-start | bytes 1462280 | tf_op jit(solution)/shard_map/ppermute | solution.py:339
  20.6 28.2 %collective-permute-start.8 = (bf16[272,896]{1,0:T(8,128)(2,1)}, bf16[272,896]{1,0:T(8,128)(2,1)}, u32[]{:S(2)}, u32[]{:S(2)}) collective-permute-start(bf16[272,896]{1,0:T(8,128)(2,1)} %get-tuple-element.75), channel_id=1, source_target_pairs={{0,2},{1,3},{2,0},{3,1},{4,6},{5,7},{6,4},{7,5},{8,10},{9,11},{10,... | collective-permute-start | bytes 1462280 | tf_op jit(solution)/shard_map/ppermute | solution.py:339
  23.2 25.6 %collective-permute-start.9 = (bf16[272,896]{1,0:T(8,128)(2,1)}, bf16[272,896]{1,0:T(8,128)(2,1)}, u32[]{:S(2)}, u32[]{:S(2)}) collective-permute-start(bf16[272,896]{1,0:T(8,128)(2,1)} %get-tuple-element.73), channel_id=1, source_target_pairs={{0,3},{1,0},{2,1},{3,2},{4,7},{5,4},{6,5},{7,6},{8,11},{9,8},{10,9... | collective-permute-start | bytes 1462280 | tf_op jit(solution)/shard_map/ppermute | solution.py:339
  29.7 0.8 copy-start.5
  30.5 15.8 %copy-start.1 = (bf16[1,3584,256]{2,1,0:T(8,128)(2,1)S(1)}, bf16[1,3584,256]{2,1,0:T(8,128)(2,1)}, u32[]{:S(2)}) copy-start(bf16[1,3584,256]{2,1,0:T(8,128)(2,1)} %param.19) | copy-start | bytes 5505028
  43.3 13.2 %collective-permute-start = (bf16[256,896]{1,0:T(8,128)(2,1)S(1)}, bf16[256,896]{1,0:T(8,128)(2,1)S(1)}, u32[]{:S(2)}, u32[]{:S(2)}) collective-permute-start(bf16[256,896]{1,0:T(8,128)(2,1)S(1)} %get-tuple-element.39.refs_0_), channel_id=1, source_target_pairs={{0,1},{1,2},{2,3},{3,0},{4,5},{5,6},{6,7},{7,4},{8,9},{9,10},{10,1... | collective-permute-start | bytes 1376264 | tf_op jit(solution)/shard_map/ppermute | solution.py:339
  44.7 11.8 %collective-permute-start.2 = (bf16[256,896]{1,0:T(8,128)(2,1)S(1)}, bf16[256,896]{1,0:T(8,128)(2,1)S(1)}, u32[]{:S(2)}, u32[]{:S(2)}) collective-permute-start(bf16[256,896]{1,0:T(8,128)(2,1)S(1)} %get-tuple-element.38.refs_1_), channel_id=1, source_target_pairs={{0,3},{1,0},{2,1},{3,2},{4,7},{5,4},{6,5},{7,6},{8,11},{9,8},{10,9... | collective-permute-start | bytes 1376264 | tf_op jit(solution)/shard_map/ppermute | solution.py:339
  46.3 1.5 %copy-start.2 = (bf16[1,3584,256]{2,1,0:T(8,128)(2,1)S(1)}, bf16[1,3584,256]{2,1,0:T(8,128)(2,1)}, u32[]{:S(2)}) copy-start(bf16[1,3584,256]{2,1,0:T(8,128)(2,1)} %param.20) | copy-start | bytes 5505028
  48.8 17.5 %collective-permute-start.10 = (bf16[256,896]{1,0:T(8,128)(2,1)S(1)}, bf16[256,896]{1,0:T(8,128)(2,1)S(1)}, u32[]{:S(2)}, u32[]{:S(2)}) collective-permute-start(bf16[256,896]{1,0:T(8,128)(2,1)S(1)} %get-tuple-element.38.refs_1_), channel_id=1, source_target_pairs={{0,1},{1,2},{2,3},{3,0},{4,5},{5,6},{6,7},{7,4},{8,9},{9,10},{10,1... | collective-permute-start | bytes 1376264 | tf_op jit(solution)/shard_map/ppermute | solution.py:339
  48.9 17.4 %collective-permute-start.11 = (bf16[256,896]{1,0:T(8,128)(2,1)S(1)}, bf16[256,896]{1,0:T(8,128)(2,1)S(1)}, u32[]{:S(2)}, u32[]{:S(2)}) collective-permute-start(bf16[256,896]{1,0:T(8,128)(2,1)S(1)} %get-tuple-element.39.refs_0_), channel_id=1, source_target_pairs={{0,3},{1,0},{2,1},{3,2},{4,7},{5,4},{6,5},{7,6},{8,11},{9,8},{10,9... | collective-permute-start | bytes 1376264 | tf_op jit(solution)/shard_map/ppermute | solution.py:339
  56.5 19.7 %collective-permute-start.1 = (bf16[256,896]{1,0:T(8,128)(2,1)S(1)}, bf16[256,896]{1,0:T(8,128)(2,1)S(1)}, u32[]{:S(2)}, u32[]{:S(2)}) collective-permute-start(bf16[256,896]{1,0:T(8,128)(2,1)S(1)} %collective-permute-done.refs_0_), channel_id=1, source_target_pairs={{0,1},{1,2},{2,3},{3,0},{4,5},{5,6},{6,7},{7,4},{8,9},{9,10},{10,1... | collective-permute-start | bytes 1376264 | tf_op jit(solution)/shard_map/ppermute | solution.py:339
  56.5 19.7 %collective-permute-start.3 = (bf16[256,896]{1,0:T(8,128)(2,1)S(1)}, bf16[256,896]{1,0:T(8,128)(2,1)S(1)}, u32[]{:S(2)}, u32[]{:S(2)}) collective-permute-start(bf16[256,896]{1,0:T(8,128)(2,1)S(1)} %collective-permute-done.2.refs_3_), channel_id=1, source_target_pairs={{0,3},{1,0},{2,1},{3,2},{4,7},{5,4},{6,5},{7,6},{8,11},{9,8},{10,9... | collective-permute-start | bytes 1376264 | tf_op jit(solution)/shard_map/ppermute | solution.py:339
  59.2 17.0 %copy-start.3 = (bf16[1,3584,256]{2,1,0:T(8,128)(2,1)S(1)}, bf16[1,3584,256]{2,1,0:T(8,128)(2,1)}, u32[]{:S(2)}) copy-start(bf16[1,3584,256]{2,1,0:T(8,128)(2,1)} %param.20) | copy-start | bytes 5505028
  68.1 13.4 %collective-permute-start.12 = (bf16[384,256]{1,0:T(8,128)(2,1)S(1)}, bf16[384,256]{1,0:T(8,128)(2,1)S(1)}, u32[]{:S(2)}, u32[]{:S(2)}) collective-permute-start(bf16[384,256]{1,0:T(8,128)(2,1)S(1)} %constant_dynamic-update-slice_fusion.refs_0_), channel_id=1, source_target_pairs={{0,1},{1,2},{2,3},{3,0},{4,5},{5,6},{6,7},{7,4},{8,9},{9,10},{10,1... | collective-permute-start | bytes 589832 | tf_op jit(solution)/shard_map/ppermute | solution.py:339
  69.1 16.7 %collective-permute-start.13 = (bf16[384,256]{1,0:T(8,128)(2,1)S(1)}, bf16[384,256]{1,0:T(8,128)(2,1)S(1)}, u32[]{:S(2)}, u32[]{:S(2)}) collective-permute-start(bf16[384,256]{1,0:T(8,128)(2,1)S(1)} %constant_dynamic-update-slice_fusion.refs_0_), channel_id=1, source_target_pairs={{0,2},{1,3},{2,0},{3,1},{4,6},{5,7},{6,4},{7,5},{8,10},{9,11},{10,... | collective-permute-start | bytes 589832 | tf_op jit(solution)/shard_map/ppermute | solution.py:339
  71.9 13.9 %collective-permute-start.14 = (bf16[384,256]{1,0:T(8,128)(2,1)S(1)}, bf16[384,256]{1,0:T(8,128)(2,1)S(1)}, u32[]{:S(2)}, u32[]{:S(2)}) collective-permute-start(bf16[384,256]{1,0:T(8,128)(2,1)S(1)} %constant_dynamic-update-slice_fusion.refs_0_), channel_id=1, source_target_pairs={{0,3},{1,0},{2,1},{3,2},{4,7},{5,4},{6,5},{7,6},{8,11},{9,8},{10,9... | collective-permute-start | bytes 589832 | tf_op jit(solution)/shard_map/ppermute | solution.py:339
  77.1 9.6 %collective-permute-start.4 = (bf16[128,256]{1,0:T(8,128)(2,1)S(1)}, bf16[128,256]{1,0:T(8,128)(2,1)S(1)}, u32[]{:S(2)}, u32[]{:S(2)}) collective-permute-start(bf16[128,256]{1,0:T(8,128)(2,1)S(1)} %shard_map.123.refs_0_), channel_id=1, source_target_pairs={{0,1},{1,2},{2,3},{3,0},{4,5},{5,6},{6,7},{7,4},{8,9},{9,10},{10,1... | collective-permute-start | bytes 196616 | tf_op jit(solution)/shard_map/ppermute | solution.py:339
  78.1 9.5 %collective-permute-start.5 = (bf16[128,256]{1,0:T(8,128)(2,1)S(1)}, bf16[128,256]{1,0:T(8,128)(2,1)S(1)}, u32[]{:S(2)}, u32[]{:S(2)}) collective-permute-start(bf16[128,256]{1,0:T(8,128)(2,1)S(1)} %shard_map.123.refs_0_), channel_id=1, source_target_pairs={{0,2},{1,3},{2,0},{3,1},{4,6},{5,7},{6,4},{7,5},{8,10},{9,11},{10,... | collective-permute-start | bytes 196616 | tf_op jit(solution)/shard_map/ppermute | solution.py:339
  81.4 6.2 %collective-permute-start.6 = (bf16[128,256]{1,0:T(8,128)(2,1)S(1)}, bf16[128,256]{1,0:T(8,128)(2,1)S(1)}, u32[]{:S(2)}, u32[]{:S(2)}) collective-permute-start(bf16[128,256]{1,0:T(8,128)(2,1)S(1)} %shard_map.123.refs_0_), channel_id=1, source_target_pairs={{0,3},{1,0},{2,1},{3,2},{4,7},{5,4},{6,5},{7,6},{8,11},{9,8},{10,9... | collective-permute-start | bytes 196616 | tf_op jit(solution)/shard_map/ppermute | solution.py:339
  86.7 13.3 %copy-start.4 = (bf16[32,32,512]{2,1,0:T(8,128)(2,1)S(1)}, bf16[32,32,512]{2,1,0:T(8,128)(2,1)}, u32[]{:S(2)}) copy-start(bf16[32,32,512]{2,1,0:T(8,128)(2,1)} %convolution_convert_fusion) | copy-start | bytes 3145732
  89.4 36.4 %all-to-all-start.1 = ((bf16[64,8,896]{2,1,0:T(8,128)(2,1)}), bf16[64,8,896]{2,1,0:T(8,128)(2,1)S(1)}, u32[]{:S(2)}, u32[]{:S(2)}) async-start(bf16[64,8,896]{2,1,0:T(8,128)(2,1)} %bitcast.8), calls=%async_computation.1 | async-start | bytes 1835008 | tf_op jit(solution)/shard_map/all_to_all | solution.py:397
  100.9 9.5 %collective-permute-start.15 = (bf16[8,32,512]{2,1,0:T(8,128)(2,1)}, bf16[8,32,512]{2,1,0:T(8,128)(2,1)}, u32[]{:S(2)}, u32[]{:S(2)}) collective-permute-start(bf16[8,32,512]{2,1,0:T(8,128)(2,1)} %get-tuple-element.70), channel_id=1, source_target_pairs={{0,1},{1,2},{2,3},{3,0},{4,5},{5,6},{6,7},{7,4},{8,9},{9,10},{10,1... | collective-permute-start | bytes 786440 | tf_op jit(solution)/shard_map/ppermute | solution.py:339
  100.9 14.0 %collective-permute-start.16 = (bf16[8,32,512]{2,1,0:T(8,128)(2,1)}, bf16[8,32,512]{2,1,0:T(8,128)(2,1)S(1)}, u32[]{:S(2)}, u32[]{:S(2)}) collective-permute-start(bf16[8,32,512]{2,1,0:T(8,128)(2,1)} %get-tuple-element.69), channel_id=1, source_target_pairs={{0,2},{1,3},{2,0},{3,1},{4,6},{5,7},{6,4},{7,5},{8,10},{9,11},{10,... | collective-permute-start | bytes 786440 | tf_op jit(solution)/shard_map/ppermute | solution.py:339
  103.1 12.9 %collective-permute-start.17 = (bf16[8,32,512]{2,1,0:T(8,128)(2,1)}, bf16[8,32,512]{2,1,0:T(8,128)(2,1)S(1)}, u32[]{:S(2)}, u32[]{:S(2)}) collective-permute-start(bf16[8,32,512]{2,1,0:T(8,128)(2,1)} %get-tuple-element.68), channel_id=1, source_target_pairs={{0,3},{1,0},{2,1},{3,2},{4,7},{5,4},{6,5},{7,6},{8,11},{9,8},{10,9... | collective-permute-start | bytes 786440 | tf_op jit(solution)/shard_map/ppermute | solution.py:339
  126.1 2.6 %collective-permute-start.18 = (bf16[8,896]{1,0:T(8,128)(2,1)S(1)}, bf16[8,896]{1,0:T(8,128)(2,1)S(1)}, u32[]{:S(2)}, u32[]{:S(2)}) collective-permute-start(bf16[8,896]{1,0:T(8,128)(2,1)S(1)} %get-tuple-element.61), channel_id=1, source_target_pairs={{0,3},{1,0},{2,1},{3,2},{4,7},{5,4},{6,5},{7,6},{8,11},{9,8},{10,9... | collective-permute-start | bytes 43016 | tf_op jit(solution)/shard_map/ppermute | solution.py:339
  127.1 4.1 %collective-permute-start.19 = (bf16[8,896]{1,0:T(8,128)(2,1)S(1)}, bf16[8,896]{1,0:T(8,128)(2,1)S(1)}, u32[]{:S(2)}, u32[]{:S(2)}) collective-permute-start(bf16[8,896]{1,0:T(8,128)(2,1)S(1)} %get-tuple-element.62), channel_id=1, source_target_pairs={{0,2},{1,3},{2,0},{3,1},{4,6},{5,7},{6,4},{7,5},{8,10},{9,11},{10,... | collective-permute-start | bytes 43016 | tf_op jit(solution)/shard_map/ppermute | solution.py:339
  127.5 3.8 %collective-permute-start.20 = (bf16[8,896]{1,0:T(8,128)(2,1)S(1)}, bf16[8,896]{1,0:T(8,128)(2,1)S(1)}, u32[]{:S(2)}, u32[]{:S(2)}) collective-permute-start(bf16[8,896]{1,0:T(8,128)(2,1)S(1)} %get-tuple-element.63), channel_id=1, source_target_pairs={{0,1},{1,2},{2,3},{3,0},{4,5},{5,6},{6,7},{7,4},{8,9},{9,10},{10,1... | collective-permute-start | bytes 43016 | tf_op jit(solution)/shard_map/ppermute | solution.py:339

commit v4 on v3

--- a/solution.py
+++ b/solution.py
@@ -31,6 +31,19 @@
     weights = (powers / jnp.sum(powers, axis=-1, keepdims=True)).astype(jnp.bfloat16)
     mixed = jnp.einsum("rhp,rpl->rhl", weights, cache_latent, preferred_element_type=jnp.float32)
     return mixed.astype(jnp.bfloat16)
+
+
+def far_order(shares):
+    return [0] + sorted(range(1, shares), key=lambda by: -min(by, shares - by))
+
+
+def arranged(values):
+    return [values[by] for by in far_order(len(values))]
+
+
+def restored(values):
+    order = far_order(len(values))
+    return [values[order.index(by)] for by in range(len(values))]
 
 
 def split3(v):
@@ -128,7 +141,7 @@
 
 
 def stack_kernel(shares, *refs):
-    weights, out_ref = refs[:shares], refs[shares]
+    weights, out_ref = restored(refs[:shares]), refs[shares]
     units = out_ref.shape[0] // shares
     for s in range(shares):
         out_ref[pl.ds(s * units, units), :] = weights[s][pl.ds(0, units), :]
@@ -145,11 +158,11 @@
         cost_estimate=pl.CostEstimate(
             flops=0, bytes_accessed=4 * shares * units * part, transcendentals=0
         ),
-    )(*weights)
+    )(*arranged(weights))
 
 
 def down_early_kernel(shares, *refs):
-    early, weights_ref, out_ref = refs[:shares], refs[shares], refs[shares + 1]
+    early, weights_ref, out_ref = restored(refs[:shares]), refs[shares], refs[shares + 1]
     slots = out_ref.shape[0] // shares
     count = early[0].shape[1]
     for block in range(shares):
@@ -167,7 +180,8 @@
 
 
 def down_late_kernel(shares, *refs):
-    late, (weights_ref, early_ref, order_ref, out_ref, plain) = refs[:shares], refs[shares:]
+    late = restored(refs[:shares])
+    weights_ref, early_ref, order_ref, out_ref, plain = refs[shares:]
     slots, count = late[0].shape
     half = slots // 2
     for block in range(shares):
@@ -199,7 +213,7 @@
             bytes_accessed=4 * rows * part + 2 * units * part * shares,
             transcendentals=0,
         ),
-    )(*early, weights)
+    )(*arranged(early), weights)
 
 
 def down_late(late, weights, early, order):
@@ -217,11 +231,11 @@
             bytes_accessed=6 * rows * part,
             transcendentals=0,
         ),
-    )(*late, weights, early, order)
+    )(*arranged(late), weights, early, order)
 
 
 def place_kernel(shares, first_ref, *refs):
-    pieces, out_ref = refs[:shares], refs[shares]
+    pieces, out_ref = restored(refs[:shares]), refs[shares]
     part = pieces[0].shape[1]
     for d in range(shares):
         quarter = lax.rem(first_ref[0] + d, shares)
@@ -241,7 +255,7 @@
         cost_estimate=pl.CostEstimate(
             flops=0, bytes_accessed=4 * rows * shares * part, transcendentals=0
         ),
-    )(first.reshape(1), *pieces)
+    )(first.reshape(1), *arranged(pieces))
 
 
 def gates_kernel(shares, chosen, *refs):
@@ -338,6 +352,10 @@
         pairs = [(i, (i + by) % shares) for i in range(shares)]
         return lax.ppermute(value, "tensor", pairs)
 
+    def spread(values):
+        moved = {by: shift(values[by], by) for by in far_order(shares)[1:]}
+        return [values[0]] + [moved[by] for by in range(1, shares)]
+
     packed = pack_rows(routes, moe_input, shares, experts)
     packed, w_down, routes, gate_weights = lax.optimization_barrier(
         (packed, w_down, routes, gate_weights)
@@ -361,7 +379,7 @@
         )
         for by in range(shares)
     ]
-    down = [down_parts[0]] + [shift(down_parts[by], by) for by in range(1, shares)]
+    down = spread(down_parts)
     local_context = attend(query_latent, query_rope, cache_latent, cache_rope, cache_len)
     heads, latent = local_context.shape[1:]
     received, local_context = lax.optimization_barrier((received, local_context))
@@ -378,16 +396,17 @@
 
     low1, high3 = shift(low, 1), shift(high, 3)
     hidden0 = hidden_of(low, high)
-    low, high, hidden0, down = lax.optimization_barrier((low, high, hidden0, down))
+    low, high, hidden0, down = lax.optimization_barrier((low, high, hidden0, arranged(down)))
     high1, low3 = shift(high, 1), shift(low, 3)
     low2, high2 = shift(low1, 1), shift(high3, 3)
     hidden13 = hidden_of(low1, high1, low3, high3)
     hidden13, down = lax.optimization_barrier((hidden13, down))
+    down = restored(down)
     stacked = stack_shares(down, units)
     early = jnp.concatenate([hidden0, hidden13], axis=0)
-    early = [early] + [shift(early, by) for by in range(1, shares)]
+    early = spread([early] * shares)
     late = hidden_of(low2, high2)
-    late = [late] + [shift(late, by) for by in range(1, shares)]
+    late = spread([late] * shares)
 
     expert_out = down_late(late, stacked, down_early(early, stacked), sort.T)
     expert_out, local_context, down = lax.optimization_barrier(
@@ -407,9 +426,7 @@
         )
         for by in range(shares)
     ]
-    context_parts = [context_parts[0]] + [
-        shift(context_parts[by], by) for by in range(1, shares)
-    ]
+    context_parts = spread(context_parts)
 
     context = jnp.zeros((rows, shares, heads, latent), bf16)
     for by in range(shares):
@@ -420,7 +437,8 @@
     combine = gates_of_slots(down, units, rows, chosen, experts)
     returned, context, combine = lax.optimization_barrier((returned, context, combine))
     sums = combine_slots(combine, returned, shares)
-    pieces = [sums[0]] + [shift(sums[d], shares - d) for d in range(1, shares)]
+    pieces = {by: shift(sums[shares - by], by) for by in far_order(shares)[1:]}
+    pieces = [sums[0]] + [pieces[shares - d] for d in range(1, shares)]
     moe_output = place_quarters(me, pieces)
     return (context.reshape(rows, shares * heads, latent), moe_output)
 

time: 132 us -> 133 us (level)
  no operation moved by 1% of the time
where the time goes in v4:
time: 133 us; the launch traced here: 132 us
  starting transfers between devices  52.8 us (40%)
  waiting for transfers between devices  44.6 us (34%)
  Pallas kernels  12.2 us (9%)
  matrix products  10.5 us (8%)
  local copies, waits for them, and re-layouts  7.81 us (6%)
  other arithmetic  3.24 us (2%)
    ppermute x21, waiting for transfers between devices, shift(): return lax.ppermute(value, 'tensor', pairs)  31.2 us
    ppermute x21, starting transfers between devices, shift(): return lax.ppermute(value, 'tensor', pairs)  28.8 us
    all_to_all x1, starting transfers between devices, per_device(): lax.all_to_all(packed.reshape(experts, shares * CAP, part), 'expert', spl...  13.2 us
    all_to_all x1, starting transfers between devices, per_device(): lax.all_to_all(expert_out.reshape(experts, shares * CAP, part), 'expert',...  10.9 us
    all_to_all x1, waiting for transfers between devices, per_device(): lax.all_to_all(expert_out.reshape(experts, shares * CAP, part), 'expert',...  8.31 us
    dot_general x1, matrix products, attend(): jnp.einsum('rhp,rpl->rhl', weights, cache_latent, preferred_element_type=...  5.52 us
    all_to_all x1, waiting for transfers between devices, per_device(): lax.all_to_all(packed.reshape(experts, shares * CAP, part), 'expert', spl...  5.1 us
    dot_general x1, matrix products, attend(): jnp.einsum('rhl,rpl->rhp', query_latent, cache_latent, preferred_element_...  3.73 us
  transfers between devices with their start and end apart: 23, of which 12 were waited for; matrix products, arithmetic and copies ran while one was open for 15% of the time, Pallas kernels for 5%

profile of v4, /device:TPU:1, one launch (start us, length us, event | category | flops | bytes accessed | tf_op | source)
XLA Modules:
  0.0 132.2 jit_solution(17848601977040439726)
XLA Ops:
  0.7 2.6 %shard_map.122 = bf16[512,896]{1,0:T(8,128)(2,1)} custom-call(s32[8,8]{1,0:T(8,128)} %routes_ref.1, bf16[8,3584]{1,0:T(8,128)(2,1)} %rows_ref.1), custom_call_target="tpu_custom_call" | custom-call | flops 29360128 | bytes 917504 | tf_op jit(solution)/shard_map/pallas_call | solution.py:91
  3.2 13.2 %all-to-all-start = ((bf16[64,8,896]{2,1,0:T(8,128)(2,1)}), bf16[64,8,896]{2,1,0:T(8,128)(2,1)}, u32[]{:S(2)}, u32[]{:S(2)}) async-start(bf16[64,8,896]{2,1,0:T(8,128)(2,1)} %bitcast.40), calls=%async_computation | async-start | bytes 1835008 | tf_op jit(solution)/shard_map/all_to_all | solution.py:363
  19.3 2.9 %collective-permute-start.7 = (bf16[272,896]{1,0:T(8,128)(2,1)}, bf16[272,896]{1,0:T(8,128)(2,1)}, u32[]{:S(2)}, u32[]{:S(2)}) collective-permute-start(bf16[272,896]{1,0:T(8,128)(2,1)} %get-tuple-element.74), channel_id=1, source_target_pairs={{0,2},{1,3},{2,0},{3,1},{4,6},{5,7},{6,4},{7,5},{8,10},{9,11},{10,... | collective-permute-start | bytes 1462280 | tf_op jit(solution)/shard_map/ppermute | solution.py:353
  22.6 2.3 %collective-permute-start.9 = (bf16[272,896]{1,0:T(8,128)(2,1)}, bf16[272,896]{1,0:T(8,128)(2,1)}, u32[]{:S(2)}, u32[]{:S(2)}) collective-permute-start(bf16[272,896]{1,0:T(8,128)(2,1)} %get-tuple-element.73), channel_id=1, source_target_pairs={{0,3},{1,0},{2,1},{3,2},{4,7},{5,4},{6,5},{7,6},{8,11},{9,8},{10,9... | collective-permute-start | bytes 1462280 | tf_op jit(solution)/shard_map/ppermute | solution.py:353
  25.3 1.3 fusion.30
  26.6 3.7 %fusion.4 = f32[32,32,128]{2,1,0:T(8,128)S(1)} fusion(f32[32,32,128]{2,1,0:T(8,128)S(1)} %fusion.30, bf16[32,32,512]{2,1,0:T(8,128)(2,1)S(1)} %copy-done, bf16[32,128,512]{2,1,0:T(8,128)(2,1)} %param.13, pred[32,128]{1,0:T(8,128)(4,1)S(1)} %iota_compare_fusion.4), kind=kOutput, calls=%fused_computation.6 | convolution fusion | flops 134610944 | bytes 6295552 | tf_op jit(solution)/shard_map/rhl,rpl->rhp/dot_general | solution.py:20
  31.5 5.5 %convolution_convert_fusion = bf16[32,32,512]{2,1,0:T(8,128)(2,1)} fusion(bf16[32,128,512]{2,1,0:T(8,128)(2,1)} %param.13, f32[32,32]{1,0:T(8,128)S(1)} %fusion.29, f32[32,32,128]{2,1,0:T(8,128)} %copy-done.5), kind=kOutput, calls=%fused_computation.1 | convolution fusion | flops 135136384 | bytes 5771264 | tf_op jit(solution)/shard_map/rhp,rpl->rhl/dot_general | solution.py:32
  37.0 5.1 %all-to-all-done = bf16[64,8,896]{2,1,0:T(8,128)(2,1)} async-done(((bf16[64,8,896]{2,1,0:T(8,128)(2,1)}), bf16[64,8,896]{2,1,0:T(8,128)(2,1)}, u32[]{:S(2)}, u32[]{:S(2)}) %all-to-all-start) | async-done | bytes 917536 | tf_op jit(solution)/shard_map/all_to_all | solution.py:363
  43.3 1.4 %collective-permute-start = (bf16[256,896]{1,0:T(8,128)(2,1)S(1)}, bf16[256,896]{1,0:T(8,128)(2,1)S(1)}, u32[]{:S(2)}, u32[]{:S(2)}) collective-permute-start(bf16[256,896]{1,0:T(8,128)(2,1)S(1)} %get-tuple-element.39.refs_0_), channel_id=1, source_target_pairs={{0,1},{1,2},{2,3},{3,0},{4,5},{5,6},{6,7},{7,4},{8,9},{9,10},{10,1... | collective-permute-start | bytes 1376264 | tf_op jit(solution)/shard_map/ppermute | solution.py:353
  44.7 1.5 %collective-permute-start.2 = (bf16[256,896]{1,0:T(8,128)(2,1)S(1)}, bf16[256,896]{1,0:T(8,128)(2,1)S(1)}, u32[]{:S(2)}, u32[]{:S(2)}) collective-permute-start(bf16[256,896]{1,0:T(8,128)(2,1)S(1)} %get-tuple-element.38.refs_1_), channel_id=1, source_target_pairs={{0,3},{1,0},{2,1},{3,2},{4,7},{5,4},{6,5},{7,6},{8,11},{9,8},{10,9... | collective-permute-start | bytes 1376264 | tf_op jit(solution)/shard_map/ppermute | solution.py:353
  46.4 1.5 %copy-done.2 = bf16[1,3584,256]{2,1,0:T(8,128)(2,1)S(1)} copy-done((bf16[1,3584,256]{2,1,0:T(8,128)(2,1)S(1)}, bf16[1,3584,256]{2,1,0:T(8,128)(2,1)}, u32[]{:S(2)}) %copy-start.2) | copy-done | bytes 1835032
  48.9 2.7 %collective-permute-start.11 = (bf16[256,896]{1,0:T(8,128)(2,1)S(1)}, bf16[256,896]{1,0:T(8,128)(2,1)S(1)}, u32[]{:S(2)}, u32[]{:S(2)}) collective-permute-start(bf16[256,896]{1,0:T(8,128)(2,1)S(1)} %get-tuple-element.39.refs_0_), channel_id=1, source_target_pairs={{0,3},{1,0},{2,1},{3,2},{4,7},{5,4},{6,5},{7,6},{8,11},{9,8},{10,9... | collective-permute-start | bytes 1376264 | tf_op jit(solution)/shard_map/ppermute | solution.py:353
  51.6 4.9 %collective-permute-done.refs_0_ = bf16[256,896]{1,0:T(8,128)(2,1)S(1)} collective-permute-done((bf16[256,896]{1,0:T(8,128)(2,1)S(1)}, bf16[256,896]{1,0:T(8,128)(2,1)S(1)}, u32[]{:S(2)}, u32[]{:S(2)}) %collective-permute-start) | collective-permute-done | bytes 458784 | tf_op jit(solution)/shard_map/ppermute | solution.py:353
  56.5 2.7 %collective-permute-start.3 = (bf16[256,896]{1,0:T(8,128)(2,1)S(1)}, bf16[256,896]{1,0:T(8,128)(2,1)S(1)}, u32[]{:S(2)}, u32[]{:S(2)}) collective-permute-start(bf16[256,896]{1,0:T(8,128)(2,1)S(1)} %collective-permute-done.2.refs_3_), channel_id=1, source_target_pairs={{0,3},{1,0},{2,1},{3,2},{4,7},{5,4},{6,5},{7,6},{8,11},{9,8},{10,9... | collective-permute-start | bytes 1376264 | tf_op jit(solution)/shard_map/ppermute | solution.py:353
  59.2 7.1 %collective-permute-done.10.refs_1_ = bf16[256,896]{1,0:T(8,128)(2,1)S(1)} collective-permute-done((bf16[256,896]{1,0:T(8,128)(2,1)S(1)}, bf16[256,896]{1,0:T(8,128)(2,1)S(1)}, u32[]{:S(2)}, u32[]{:S(2)}) %collective-permute-start.10) | collective-permute-done | bytes 458784 | tf_op jit(solution)/shard_map/ppermute | solution.py:353
  66.4 1.7 %shard_map.125 = bf16[256,256]{1,0:T(8,128)(2,1)S(1)} custom-call(bf16[256,896]{1,0:T(8,128)(2,1)S(1)} %collective-permute-done.refs_0_, bf16[256,896]{1,0:T(8,128)(2,1)S(1)} %collective-permute-done.10.refs_1_, bf16[256,896]{1,0:T(8,128)(2,1)S(1)} %collective-permute-done.11.refs_2_, bf16[256,896]{1,0:T(8,128)(2,1)S(1)} %collective-permute-done.2.refs_3_, ...), custom_call_target="tpu_custom_call" | custom-call | flops 939524096 | bytes 5505024 | tf_op jit(solution)/shard_map/pallas_call | solution.py:128
  68.1 2.3 %collective-permute-start.12 = (bf16[384,256]{1,0:T(8,128)(2,1)S(1)}, bf16[384,256]{1,0:T(8,128)(2,1)S(1)}, u32[]{:S(2)}, u32[]{:S(2)}) collective-permute-start(bf16[384,256]{1,0:T(8,128)(2,1)S(1)} %constant_dynamic-update-slice_fusion.refs_0_), channel_id=1, source_target_pairs={{0,2},{1,3},{2,0},{3,1},{4,6},{5,7},{6,4},{7,5},{8,10},{9,11},{10,... | collective-permute-start | bytes 589832 | tf_op jit(solution)/shard_map/ppermute | solution.py:353
  71.3 1.8 %collective-permute-start.14 = (bf16[384,256]{1,0:T(8,128)(2,1)S(1)}, bf16[384,256]{1,0:T(8,128)(2,1)S(1)}, u32[]{:S(2)}, u32[]{:S(2)}) collective-permute-start(bf16[384,256]{1,0:T(8,128)(2,1)S(1)} %constant_dynamic-update-slice_fusion.refs_0_), channel_id=1, source_target_pairs={{0,3},{1,0},{2,1},{3,2},{4,7},{5,4},{6,5},{7,6},{8,11},{9,8},{10,9... | collective-permute-start | bytes 589832 | tf_op jit(solution)/shard_map/ppermute | solution.py:353
  73.1 1.5 %shard_map.126.refs_4_ = bf16[1024,896]{1,0:T(8,128)(2,1)S(1)} custom-call(bf16[272,896]{1,0:T(8,128)(2,1)S(1)} %get-tuple-element.53.refs_0_, bf16[272,896]{1,0:T(8,128)(2,1)} %collective-permute-done.7.refs_1_.refs_2_, bf16[272,896]{1,0:T(8,128)(2,1)} %collective-permute-done.8.refs_2_.refs_1_, bf16[272,896]{1,0:T(8,128)(2,1)} %collective-permute-done.9.refs_3_), custom_call_target="tpu_custom_call" | custom-call | bytes 3670016 | tf_op jit(solution)/shard_map/pallas_call | solution.py:152
  74.5 1.7 %collective-permute-done.1.refs_0_ = bf16[256,896]{1,0:T(8,128)(2,1)S(1)} collective-permute-done((bf16[256,896]{1,0:T(8,128)(2,1)S(1)}, bf16[256,896]{1,0:T(8,128)(2,1)S(1)}, u32[]{:S(2)}, u32[]{:S(2)}) %collective-permute-start.1) | collective-permute-done | bytes 458784 | tf_op jit(solution)/shard_map/ppermute | solution.py:353
  77.1 2.3 %collective-permute-start.4 = (bf16[128,256]{1,0:T(8,128)(2,1)S(1)}, bf16[128,256]{1,0:T(8,128)(2,1)S(1)}, u32[]{:S(2)}, u32[]{:S(2)}) collective-permute-start(bf16[128,256]{1,0:T(8,128)(2,1)S(1)} %shard_map.123.refs_0_), channel_id=1, source_target_pairs={{0,2},{1,3},{2,0},{3,1},{4,6},{5,7},{6,4},{7,5},{8,10},{9,11},{10,... | collective-permute-start | bytes 196616 | tf_op jit(solution)/shard_map/ppermute | solution.py:353
  79.5 1.4 %collective-permute-start.5 = (bf16[128,256]{1,0:T(8,128)(2,1)S(1)}, bf16[128,256]{1,0:T(8,128)(2,1)S(1)}, u32[]{:S(2)}, u32[]{:S(2)}) collective-permute-start(bf16[128,256]{1,0:T(8,128)(2,1)S(1)} %shard_map.123.refs_0_), channel_id=1, source_target_pairs={{0,1},{1,2},{2,3},{3,0},{4,5},{5,6},{6,7},{7,4},{8,9},{9,10},{10,1... | collective-permute-start | bytes 196616 | tf_op jit(solution)/shard_map/ppermute | solution.py:353
  82.5 2.1 %collective-permute-done.13.refs_2_ = bf16[384,256]{1,0:T(8,128)(2,1)S(1)} collective-permute-done((bf16[384,256]{1,0:T(8,128)(2,1)S(1)}, bf16[384,256]{1,0:T(8,128)(2,1)S(1)}, u32[]{:S(2)}, u32[]{:S(2)}) %collective-permute-start.13) | collective-permute-done | bytes 196640 | tf_op jit(solution)/shard_map/ppermute | solution.py:353
  86.9 1.8 %shard_map.128 = bf16[512,896]{1,0:T(8,128)(2,1)} custom-call(bf16[128,256]{1,0:T(8,128)(2,1)S(1)} %shard_map.123.refs_0_, bf16[128,256]{1,0:T(8,128)(2,1)S(1)} %collective-permute-done.4.refs_1_, bf16[128,256]{1,0:T(8,128)(2,1)S(1)} %collective-permute-done.5.refs_2_, bf16[128,256]{1,0:T(8,128)(2,1)S(1)} %collective-permute-done.6.refs_3_, ...), custom_call_target="tpu_custom_call" | custom-call | flops 704643072 | bytes 2752512 | tf_op jit(solution)/shard_map/pallas_call | solution.py:222
  88.6 10.9 %all-to-all-start.1 = ((bf16[64,8,896]{2,1,0:T(8,128)(2,1)}), bf16[64,8,896]{2,1,0:T(8,128)(2,1)S(1)}, u32[]{:S(2)}, u32[]{:S(2)}) async-start(bf16[64,8,896]{2,1,0:T(8,128)(2,1)} %bitcast.8), calls=%async_computation.1 | async-start | bytes 1835008 | tf_op jit(solution)/shard_map/all_to_all | solution.py:416
  100.5 2.9 %collective-permute-start.16 = (bf16[8,32,512]{2,1,0:T(8,128)(2,1)}, bf16[8,32,512]{2,1,0:T(8,128)(2,1)S(1)}, u32[]{:S(2)}, u32[]{:S(2)}) collective-permute-start(bf16[8,32,512]{2,1,0:T(8,128)(2,1)} %get-tuple-element.69), channel_id=1, source_target_pairs={{0,2},{1,3},{2,0},{3,1},{4,6},{5,7},{6,4},{7,5},{8,10},{9,11},{10,... | collective-permute-start | bytes 786440 | tf_op jit(solution)/shard_map/ppermute | solution.py:353
  104.4 5.0 %collective-permute-done.15 = bf16[8,32,512]{2,1,0:T(8,128)(2,1)} collective-permute-done((bf16[8,32,512]{2,1,0:T(8,128)(2,1)}, bf16[8,32,512]{2,1,0:T(8,128)(2,1)}, u32[]{:S(2)}, u32[]{:S(2)}) %collective-permute-start.15) | collective-permute-done | bytes 262176 | tf_op jit(solution)/shard_map/ppermute | solution.py:353
  110.4 4.8 %collective-permute-done.16 = bf16[8,32,512]{2,1,0:T(8,128)(2,1)S(1)} collective-permute-done((bf16[8,32,512]{2,1,0:T(8,128)(2,1)}, bf16[8,32,512]{2,1,0:T(8,128)(2,1)S(1)}, u32[]{:S(2)}, u32[]{:S(2)}) %collective-permute-start.16) | collective-permute-done | bytes 262176 | tf_op jit(solution)/shard_map/ppermute | solution.py:353
  117.0 8.3 %all-to-all-done.1 = bf16[64,8,896]{2,1,0:T(8,128)(2,1)S(1)} async-done(((bf16[64,8,896]{2,1,0:T(8,128)(2,1)}), bf16[64,8,896]{2,1,0:T(8,128)(2,1)S(1)}, u32[]{:S(2)}, u32[]{:S(2)}) %all-to-all-start.1) | async-done | bytes 917536 | tf_op jit(solution)/shard_map/all_to_all | solution.py:416
  126.4 1.3 %collective-permute-start.19 = (bf16[8,896]{1,0:T(8,128)(2,1)S(1)}, bf16[8,896]{1,0:T(8,128)(2,1)S(1)}, u32[]{:S(2)}, u32[]{:S(2)}) collective-permute-start(bf16[8,896]{1,0:T(8,128)(2,1)S(1)} %get-tuple-element.62), channel_id=1, source_target_pairs={{0,3},{1,0},{2,1},{3,2},{4,7},{5,4},{6,5},{7,6},{8,11},{9,8},{10,9... | collective-permute-start | bytes 43016 | tf_op jit(solution)/shard_map/ppermute | solution.py:353
  127.9 1.8 %collective-permute-done.18.refs_1_ = bf16[8,896]{1,0:T(8,128)(2,1)S(1)} collective-permute-done((bf16[8,896]{1,0:T(8,128)(2,1)S(1)}, bf16[8,896]{1,0:T(8,128)(2,1)S(1)}, u32[]{:S(2)}, u32[]{:S(2)}) %collective-permute-start.18) | collective-permute-done | bytes 14368 | tf_op jit(solution)/shard_map/ppermute | solution.py:353
  129.7 1.8 %collective-permute-done.20.refs_3_ = bf16[8,896]{1,0:T(8,128)(2,1)S(1)} collective-permute-done((bf16[8,896]{1,0:T(8,128)(2,1)S(1)}, bf16[8,896]{1,0:T(8,128)(2,1)S(1)}, u32[]{:S(2)}, u32[]{:S(2)}) %collective-permute-start.20) | collective-permute-done | bytes 14368 | tf_op jit(solution)/shard_map/ppermute | solution.py:353
  (65 shorter events, 19.6 us)
Async XLA Ops:
  0.6 25.9 %copy-start = (bf16[32,32,512]{2,1,0:T(8,128)(2,1)S(1)}, bf16[32,32,512]{2,1,0:T(8,128)(2,1)}, u32[]{:S(2)}) copy-start(bf16[32,32,512]{2,1,0:T(8,128)(2,1)} %param.11) | copy-start | bytes 3145732
  0.6 17.3 %copy-start.6 = (bf16[1,256,3584]{2,1,0:T(8,128)(2,1)S(1)}, bf16[1,256,3584]{2,1,0:T(8,128)(2,1)}, u32[]{:S(2)}) copy-start(bf16[1,256,3584]{2,1,0:T(8,128)(2,1)} %param.21) | copy-start | bytes 5505028
  3.2 38.8 %all-to-all-start = ((bf16[64,8,896]{2,1,0:T(8,128)(2,1)}), bf16[64,8,896]{2,1,0:T(8,128)(2,1)}, u32[]{:S(2)}, u32[]{:S(2)}) async-start(bf16[64,8,896]{2,1,0:T(8,128)(2,1)} %bitcast.40), calls=%async_computation | async-start | bytes 1835008 | tf_op jit(solution)/shard_map/all_to_all | solution.py:363
  16.4 8.5 %copy-start.7 = (bf16[32,2048]{1,0:T(8,128)(2,1)S(1)}, bf16[32,2048]{1,0:T(8,128)(2,1)}, u32[]{:S(2)}) copy-start(bf16[32,2048]{1,0:T(8,128)(2,1)} %param.12) | copy-start | bytes 393220
  16.4 8.8 %copy-start.8 = (s32[32]{0:T(128)S(1)}, s32[32]{0:T(128)}, u32[]{:S(2)}) copy-start(s32[32]{0:T(128)} %param.15) | copy-start | bytes 388
  19.3 29.5 %collective-permute-start.7 = (bf16[272,896]{1,0:T(8,128)(2,1)}, bf16[272,896]{1,0:T(8,128)(2,1)}, u32[]{:S(2)}, u32[]{:S(2)}) collective-permute-start(bf16[272,896]{1,0:T(8,128)(2,1)} %get-tuple-element.74), channel_id=1, source_target_pairs={{0,2},{1,3},{2,0},{3,1},{4,6},{5,7},{6,4},{7,5},{8,10},{9,11},{10,... | collective-permute-start | bytes 1462280 | tf_op jit(solution)/shard_map/ppermute | solution.py:353
  22.2 26.6 %collective-permute-start.8 = (bf16[272,896]{1,0:T(8,128)(2,1)}, bf16[272,896]{1,0:T(8,128)(2,1)}, u32[]{:S(2)}, u32[]{:S(2)}) collective-permute-start(bf16[272,896]{1,0:T(8,128)(2,1)} %get-tuple-element.75), channel_id=1, source_target_pairs={{0,1},{1,2},{2,3},{3,0},{4,5},{5,6},{6,7},{7,4},{8,9},{9,10},{10,1... | collective-permute-start | bytes 1462280 | tf_op jit(solution)/shard_map/ppermute | solution.py:353
  22.6 26.2 %collective-permute-start.9 = (bf16[272,896]{1,0:T(8,128)(2,1)}, bf16[272,896]{1,0:T(8,128)(2,1)}, u32[]{:S(2)}, u32[]{:S(2)}) collective-permute-start(bf16[272,896]{1,0:T(8,128)(2,1)} %get-tuple-element.73), channel_id=1, source_target_pairs={{0,3},{1,0},{2,1},{3,2},{4,7},{5,4},{6,5},{7,6},{8,11},{9,8},{10,9... | collective-permute-start | bytes 1462280 | tf_op jit(solution)/shard_map/ppermute | solution.py:353
  30.3 0.8 copy-start.5
  31.1 15.2 %copy-start.1 = (bf16[1,3584,256]{2,1,0:T(8,128)(2,1)S(1)}, bf16[1,3584,256]{2,1,0:T(8,128)(2,1)}, u32[]{:S(2)}) copy-start(bf16[1,3584,256]{2,1,0:T(8,128)(2,1)} %param.19) | copy-start | bytes 5505028
  43.3 13.2 %collective-permute-start = (bf16[256,896]{1,0:T(8,128)(2,1)S(1)}, bf16[256,896]{1,0:T(8,128)(2,1)S(1)}, u32[]{:S(2)}, u32[]{:S(2)}) collective-permute-start(bf16[256,896]{1,0:T(8,128)(2,1)S(1)} %get-tuple-element.39.refs_0_), channel_id=1, source_target_pairs={{0,1},{1,2},{2,3},{3,0},{4,5},{5,6},{6,7},{7,4},{8,9},{9,10},{10,1... | collective-permute-start | bytes 1376264 | tf_op jit(solution)/shard_map/ppermute | solution.py:353
  44.7 11.8 %collective-permute-start.2 = (bf16[256,896]{1,0:T(8,128)(2,1)S(1)}, bf16[256,896]{1,0:T(8,128)(2,1)S(1)}, u32[]{:S(2)}, u32[]{:S(2)}) collective-permute-start(bf16[256,896]{1,0:T(8,128)(2,1)S(1)} %get-tuple-element.38.refs_1_), channel_id=1, source_target_pairs={{0,3},{1,0},{2,1},{3,2},{4,7},{5,4},{6,5},{7,6},{8,11},{9,8},{10,9... | collective-permute-start | bytes 1376264 | tf_op jit(solution)/shard_map/ppermute | solution.py:353
  46.3 1.5 %copy-start.2 = (bf16[1,3584,256]{2,1,0:T(8,128)(2,1)S(1)}, bf16[1,3584,256]{2,1,0:T(8,128)(2,1)}, u32[]{:S(2)}) copy-start(bf16[1,3584,256]{2,1,0:T(8,128)(2,1)} %param.20) | copy-start | bytes 5505028
  48.8 17.5 %collective-permute-start.10 = (bf16[256,896]{1,0:T(8,128)(2,1)S(1)}, bf16[256,896]{1,0:T(8,128)(2,1)S(1)}, u32[]{:S(2)}, u32[]{:S(2)}) collective-permute-start(bf16[256,896]{1,0:T(8,128)(2,1)S(1)} %get-tuple-element.38.refs_1_), channel_id=1, source_target_pairs={{0,1},{1,2},{2,3},{3,0},{4,5},{5,6},{6,7},{7,4},{8,9},{9,10},{10,1... | collective-permute-start | bytes 1376264 | tf_op jit(solution)/shard_map/ppermute | solution.py:353
  48.9 17.4 %collective-permute-start.11 = (bf16[256,896]{1,0:T(8,128)(2,1)S(1)}, bf16[256,896]{1,0:T(8,128)(2,1)S(1)}, u32[]{:S(2)}, u32[]{:S(2)}) collective-permute-start(bf16[256,896]{1,0:T(8,128)(2,1)S(1)} %get-tuple-element.39.refs_0_), channel_id=1, source_target_pairs={{0,3},{1,0},{2,1},{3,2},{4,7},{5,4},{6,5},{7,6},{8,11},{9,8},{10,9... | collective-permute-start | bytes 1376264 | tf_op jit(solution)/shard_map/ppermute | solution.py:353
  56.5 19.7 %collective-permute-start.1 = (bf16[256,896]{1,0:T(8,128)(2,1)S(1)}, bf16[256,896]{1,0:T(8,128)(2,1)S(1)}, u32[]{:S(2)}, u32[]{:S(2)}) collective-permute-start(bf16[256,896]{1,0:T(8,128)(2,1)S(1)} %collective-permute-done.refs_0_), channel_id=1, source_target_pairs={{0,1},{1,2},{2,3},{3,0},{4,5},{5,6},{6,7},{7,4},{8,9},{9,10},{10,1... | collective-permute-start | bytes 1376264 | tf_op jit(solution)/shard_map/ppermute | solution.py:353
  56.5 19.7 %collective-permute-start.3 = (bf16[256,896]{1,0:T(8,128)(2,1)S(1)}, bf16[256,896]{1,0:T(8,128)(2,1)S(1)}, u32[]{:S(2)}, u32[]{:S(2)}) collective-permute-start(bf16[256,896]{1,0:T(8,128)(2,1)S(1)} %collective-permute-done.2.refs_3_), channel_id=1, source_target_pairs={{0,3},{1,0},{2,1},{3,2},{4,7},{5,4},{6,5},{7,6},{8,11},{9,8},{10,9... | collective-permute-start | bytes 1376264 | tf_op jit(solution)/shard_map/ppermute | solution.py:353
  59.2 17.0 %copy-start.3 = (bf16[1,3584,256]{2,1,0:T(8,128)(2,1)S(1)}, bf16[1,3584,256]{2,1,0:T(8,128)(2,1)}, u32[]{:S(2)}) copy-start(bf16[1,3584,256]{2,1,0:T(8,128)(2,1)} %param.20) | copy-start | bytes 5505028
  68.1 13.5 %collective-permute-start.12 = (bf16[384,256]{1,0:T(8,128)(2,1)S(1)}, bf16[384,256]{1,0:T(8,128)(2,1)S(1)}, u32[]{:S(2)}, u32[]{:S(2)}) collective-permute-start(bf16[384,256]{1,0:T(8,128)(2,1)S(1)} %constant_dynamic-update-slice_fusion.refs_0_), channel_id=1, source_target_pairs={{0,2},{1,3},{2,0},{3,1},{4,6},{5,7},{6,4},{7,5},{8,10},{9,11},{10,... | collective-permute-start | bytes 589832 | tf_op jit(solution)/shard_map/ppermute | solution.py:353
  70.4 14.2 %collective-permute-start.13 = (bf16[384,256]{1,0:T(8,128)(2,1)S(1)}, bf16[384,256]{1,0:T(8,128)(2,1)S(1)}, u32[]{:S(2)}, u32[]{:S(2)}) collective-permute-start(bf16[384,256]{1,0:T(8,128)(2,1)S(1)} %constant_dynamic-update-slice_fusion.refs_0_), channel_id=1, source_target_pairs={{0,1},{1,2},{2,3},{3,0},{4,5},{5,6},{6,7},{7,4},{8,9},{9,10},{10,1... | collective-permute-start | bytes 589832 | tf_op jit(solution)/shard_map/ppermute | solution.py:353
  71.3 13.4 %collective-permute-start.14 = (bf16[384,256]{1,0:T(8,128)(2,1)S(1)}, bf16[384,256]{1,0:T(8,128)(2,1)S(1)}, u32[]{:S(2)}, u32[]{:S(2)}) collective-permute-start(bf16[384,256]{1,0:T(8,128)(2,1)S(1)} %constant_dynamic-update-slice_fusion.refs_0_), channel_id=1, source_target_pairs={{0,3},{1,0},{2,1},{3,2},{4,7},{5,4},{6,5},{7,6},{8,11},{9,8},{10,9... | collective-permute-start | bytes 589832 | tf_op jit(solution)/shard_map/ppermute | solution.py:353
  77.1 9.7 %collective-permute-start.4 = (bf16[128,256]{1,0:T(8,128)(2,1)S(1)}, bf16[128,256]{1,0:T(8,128)(2,1)S(1)}, u32[]{:S(2)}, u32[]{:S(2)}) collective-permute-start(bf16[128,256]{1,0:T(8,128)(2,1)S(1)} %shard_map.123.refs_0_), channel_id=1, source_target_pairs={{0,2},{1,3},{2,0},{3,1},{4,6},{5,7},{6,4},{7,5},{8,10},{9,11},{10,... | collective-permute-start | bytes 196616 | tf_op jit(solution)/shard_map/ppermute | solution.py:353
  79.5 7.4 %collective-permute-start.5 = (bf16[128,256]{1,0:T(8,128)(2,1)S(1)}, bf16[128,256]{1,0:T(8,128)(2,1)S(1)}, u32[]{:S(2)}, u32[]{:S(2)}) collective-permute-start(bf16[128,256]{1,0:T(8,128)(2,1)S(1)} %shard_map.123.refs_0_), channel_id=1, source_target_pairs={{0,1},{1,2},{2,3},{3,0},{4,5},{5,6},{6,7},{7,4},{8,9},{9,10},{10,1... | collective-permute-start | bytes 196616 | tf_op jit(solution)/shard_map/ppermute | solution.py:353
  81.5 5.3 %collective-permute-start.6 = (bf16[128,256]{1,0:T(8,128)(2,1)S(1)}, bf16[128,256]{1,0:T(8,128)(2,1)S(1)}, u32[]{:S(2)}, u32[]{:S(2)}) collective-permute-start(bf16[128,256]{1,0:T(8,128)(2,1)S(1)} %shard_map.123.refs_0_), channel_id=1, source_target_pairs={{0,3},{1,0},{2,1},{3,2},{4,7},{5,4},{6,5},{7,6},{8,11},{9,8},{10,9... | collective-permute-start | bytes 196616 | tf_op jit(solution)/shard_map/ppermute | solution.py:353
  85.6 13.9 %copy-start.4 = (bf16[32,32,512]{2,1,0:T(8,128)(2,1)S(1)}, bf16[32,32,512]{2,1,0:T(8,128)(2,1)}, u32[]{:S(2)}) copy-start(bf16[32,32,512]{2,1,0:T(8,128)(2,1)} %convolution_convert_fusion) | copy-start | bytes 3145732
  88.6 36.6 %all-to-all-start.1 = ((bf16[64,8,896]{2,1,0:T(8,128)(2,1)}), bf16[64,8,896]{2,1,0:T(8,128)(2,1)S(1)}, u32[]{:S(2)}, u32[]{:S(2)}) async-start(bf16[64,8,896]{2,1,0:T(8,128)(2,1)} %bitcast.8), calls=%async_computation.1 | async-start | bytes 1835008 | tf_op jit(solution)/shard_map/all_to_all | solution.py:416
  100.5 9.0 %collective-permute-start.15 = (bf16[8,32,512]{2,1,0:T(8,128)(2,1)}, bf16[8,32,512]{2,1,0:T(8,128)(2,1)}, u32[]{:S(2)}, u32[]{:S(2)}) collective-permute-start(bf16[8,32,512]{2,1,0:T(8,128)(2,1)} %get-tuple-element.70), channel_id=1, source_target_pairs={{0,1},{1,2},{2,3},{3,0},{4,5},{5,6},{6,7},{7,4},{8,9},{9,10},{10,1... | collective-permute-start | bytes 786440 | tf_op jit(solution)/shard_map/ppermute | solution.py:353
  100.5 14.7 %collective-permute-start.16 = (bf16[8,32,512]{2,1,0:T(8,128)(2,1)}, bf16[8,32,512]{2,1,0:T(8,128)(2,1)S(1)}, u32[]{:S(2)}, u32[]{:S(2)}) collective-permute-start(bf16[8,32,512]{2,1,0:T(8,128)(2,1)} %get-tuple-element.69), channel_id=1, source_target_pairs={{0,2},{1,3},{2,0},{3,1},{4,6},{5,7},{6,4},{7,5},{8,10},{9,11},{10,... | collective-permute-start | bytes 786440 | tf_op jit(solution)/shard_map/ppermute | solution.py:353
  103.3 12.9 %collective-permute-start.17 = (bf16[8,32,512]{2,1,0:T(8,128)(2,1)}, bf16[8,32,512]{2,1,0:T(8,128)(2,1)S(1)}, u32[]{:S(2)}, u32[]{:S(2)}) collective-permute-start(bf16[8,32,512]{2,1,0:T(8,128)(2,1)} %get-tuple-element.68), channel_id=1, source_target_pairs={{0,3},{1,0},{2,1},{3,2},{4,7},{5,4},{6,5},{7,6},{8,11},{9,8},{10,9... | collective-permute-start | bytes 786440 | tf_op jit(solution)/shard_map/ppermute | solution.py:353
  125.6 4.2 %collective-permute-start.18 = (bf16[8,896]{1,0:T(8,128)(2,1)S(1)}, bf16[8,896]{1,0:T(8,128)(2,1)S(1)}, u32[]{:S(2)}, u32[]{:S(2)}) collective-permute-start(bf16[8,896]{1,0:T(8,128)(2,1)S(1)} %get-tuple-element.61), channel_id=1, source_target_pairs={{0,2},{1,3},{2,0},{3,1},{4,6},{5,7},{6,4},{7,5},{8,10},{9,11},{10,... | collective-permute-start | bytes 43016 | tf_op jit(solution)/shard_map/ppermute | solution.py:353
  126.4 3.3 %collective-permute-start.19 = (bf16[8,896]{1,0:T(8,128)(2,1)S(1)}, bf16[8,896]{1,0:T(8,128)(2,1)S(1)}, u32[]{:S(2)}, u32[]{:S(2)}) collective-permute-start(bf16[8,896]{1,0:T(8,128)(2,1)S(1)} %get-tuple-element.62), channel_id=1, source_target_pairs={{0,3},{1,0},{2,1},{3,2},{4,7},{5,4},{6,5},{7,6},{8,11},{9,8},{10,9... | collective-permute-start | bytes 43016 | tf_op jit(solution)/shard_map/ppermute | solution.py:353
  127.8 3.8 %collective-permute-start.20 = (bf16[8,896]{1,0:T(8,128)(2,1)S(1)}, bf16[8,896]{1,0:T(8,128)(2,1)S(1)}, u32[]{:S(2)}, u32[]{:S(2)}) collective-permute-start(bf16[8,896]{1,0:T(8,128)(2,1)S(1)} %get-tuple-element.63), channel_id=1, source_target_pairs={{0,1},{1,2},{2,3},{3,0},{4,5},{5,6},{6,7},{7,4},{8,9},{9,10},{10,1... | collective-permute-start | bytes 43016 | tf_op jit(solution)/shard_map/ppermute | solution.py:353

commit v5 on v3

--- a/solution.py
+++ b/solution.py
@@ -45,7 +45,7 @@
 whole = pl.BlockSpec(memory_space=pltpu.VMEM)
 
 
-def pack_kernel(shares, experts, routes_ref, rows_ref, out_ref):
+def pack_kernel(shares, experts, routes_ref, rows_ref, out_ref, held, sems):
     f32, bf16 = jnp.float32, jnp.bfloat16
     rows, width = rows_ref.shape
     part = width // shares
@@ -67,9 +67,18 @@
     values = jnp.concatenate(
         [values[:, q * part : (q + 1) * part] for q in range(shares)], axis=0
     )
-    out_ref[...] = jnp.dot(
-        select.T.astype(bf16), values.astype(bf16), preferred_element_type=f32
-    ).astype(bf16)
+    select, values = select.T.astype(bf16), values.astype(bf16)
+    step = held.shape[0] // sems.shape[0]
+    copies = []
+    for n in range(sems.shape[0]):
+        place = pl.ds(n * step, step)
+        held[place, :] = jnp.dot(
+            select[n * step : (n + 1) * step], values, preferred_element_type=f32
+        ).astype(bf16)
+        copies.append(pltpu.make_async_copy(held.at[place], out_ref.at[place], sems.at[n]))
+        copies[-1].start()
+    for copy in copies:
+        copy.wait()
 
 
 def pack_rows(routes, rows, shares, experts):
@@ -79,7 +88,11 @@
         functools.partial(pack_kernel, shares, experts),
         out_shape=jax.ShapeDtypeStruct((total, part), rows.dtype),
         in_specs=[whole] * 2,
-        out_specs=whole,
+        out_specs=pl.BlockSpec(memory_space=pl.ANY),
+        scratch_shapes=[
+            pltpu.VMEM((total, part), rows.dtype),
+            pltpu.SemaphoreType.DMA((4,)),
+        ],
         compiler_params=pltpu.CompilerParams(vmem_limit_bytes=58 * 1024 * 1024),
         cost_estimate=pl.CostEstimate(
             flops=2 * total * part * rows.shape[0] * shares,
@@ -167,7 +180,10 @@
 
 
 def down_late_kernel(shares, *refs):
-    late, (weights_ref, early_ref, order_ref, out_ref, plain) = refs[:shares], refs[shares:]
+    late, (weights_ref, early_ref, order_ref, out_ref, plain, held, sems) = (
+        refs[:shares],
+        refs[shares:],
+    )
     slots, count = late[0].shape
     half = slots // 2
     for block in range(shares):
@@ -177,11 +193,16 @@
         total = (early_ref[pl.ds(block * slots, slots), :] + term).astype(plain.dtype)
         plain[pl.ds(block * half, half), :] = total[:half]
         plain[pl.ds((shares + block) * half, half), :] = total[half:]
+    copies = []
     for h in range(2):
         place = pl.ds(h * shares * half, shares * half)
-        out_ref[place, :] = jnp.dot(
+        held[place, :] = jnp.dot(
             order_ref[...], plain[place, :], preferred_element_type=jnp.float32
-        ).astype(out_ref.dtype)
+        ).astype(held.dtype)
+        copies.append(pltpu.make_async_copy(held.at[place], out_ref.at[place], sems.at[h]))
+        copies[-1].start()
+    for copy in copies:
+        copy.wait()
 
 
 def down_early(early, weights):
@@ -209,8 +230,12 @@
         functools.partial(down_late_kernel, shares),
         out_shape=jax.ShapeDtypeStruct((rows, part), jnp.bfloat16),
         in_specs=[whole] * (shares + 3),
-        out_specs=whole,
-        scratch_shapes=[pltpu.VMEM((rows, part), jnp.bfloat16)],
+        out_specs=pl.BlockSpec(memory_space=pl.ANY),
+        scratch_shapes=[
+            pltpu.VMEM((rows, part), jnp.bfloat16),
+            pltpu.VMEM((rows, part), jnp.bfloat16),
+            pltpu.SemaphoreType.DMA((2,)),
+        ],
         compiler_params=vmem_params,
         cost_estimate=pl.CostEstimate(
             flops=2 * rows * part * (late[0].shape[1] + rows),

time: 132 us -> 132 us (level)
  no operation moved by 1% of the time
where the time goes in v5:
time: 132 us
  starting transfers between devices  51.6 us (39%)
  waiting for transfers between devices  45.6 us (35%)
  Pallas kernels  11.9 us (9%)
  matrix products  10.5 us (8%)
  local copies, waits for them, and re-layouts  7.81 us (6%)
  other arithmetic  3.24 us (2%)
    ppermute x21, waiting for transfers between devices, shift(): return lax.ppermute(value, 'tensor', pairs)  30.9 us
    ppermute x21, starting transfers between devices, shift(): return lax.ppermute(value, 'tensor', pairs)  27.8 us
    all_to_all x1, starting transfers between devices, per_device(): lax.all_to_all(packed.reshape(experts, shares * CAP, part), 'expert', spl...  13.2 us
    all_to_all x1, starting transfers between devices, per_device(): lax.all_to_all(expert_out.reshape(experts, shares * CAP, part), 'expert',...  10.6 us
    all_to_all x1, waiting for transfers between devices, per_device(): lax.all_to_all(expert_out.reshape(experts, shares * CAP, part), 'expert',...  9.03 us
    all_to_all x1, waiting for transfers between devices, per_device(): lax.all_to_all(packed.reshape(experts, shares * CAP, part), 'expert', spl...  5.69 us
    dot_general x1, matrix products, attend(): jnp.einsum('rhp,rpl->rhl', weights, cache_latent, preferred_element_type=...  5.52 us
    dot_general x1, matrix products, attend(): jnp.einsum('rhl,rpl->rhp', query_latent, cache_latent, preferred_element_...  3.73 us
  transfers between devices with their start and end apart: 23, of which 12 were waited for; matrix products, arithmetic and copies ran while one was open for 15% of the time, Pallas kernels for 5%

profile of v5, /device:TPU:1, one launch (start us, length us, event | category | flops | bytes accessed | tf_op | source)
XLA Modules:
  0.0 131.7 jit_solution(11759850168754334870)
XLA Ops:
  0.7 2.4 %shard_map.122 = bf16[512,896]{1,0:T(8,128)(2,1)} custom-call(s32[8,8]{1,0:T(8,128)} %routes_ref.1, bf16[8,3584]{1,0:T(8,128)(2,1)} %rows_ref.1), custom_call_target="tpu_custom_call" | custom-call | flops 29360128 | bytes 917504 | tf_op jit(solution)/shard_map/pallas_call | solution.py:87
  3.1 13.2 %all-to-all-start = ((bf16[64,8,896]{2,1,0:T(8,128)(2,1)}), bf16[64,8,896]{2,1,0:T(8,128)(2,1)}, u32[]{:S(2)}, u32[]{:S(2)}) async-start(bf16[64,8,896]{2,1,0:T(8,128)(2,1)} %bitcast.40), calls=%async_computation | async-start | bytes 1835008 | tf_op jit(solution)/shard_map/all_to_all | solution.py:370
  18.0 1.2 pad_maximum_fusion
  19.2 1.3 collective-permute-start.7
  20.5 2.6 %collective-permute-start.8 = (bf16[272,896]{1,0:T(8,128)(2,1)}, bf16[272,896]{1,0:T(8,128)(2,1)}, u32[]{:S(2)}, u32[]{:S(2)}) collective-permute-start(bf16[272,896]{1,0:T(8,128)(2,1)} %get-tuple-element.75), channel_id=1, source_target_pairs={{0,2},{1,3},{2,0},{3,1},{4,6},{5,7},{6,4},{7,5},{8,10},{9,11},{10,... | collective-permute-start | bytes 1462280 | tf_op jit(solution)/shard_map/ppermute | solution.py:364
  24.5 1.3 fusion.30
  25.8 3.7 %fusion.4 = f32[32,32,128]{2,1,0:T(8,128)S(1)} fusion(f32[32,32,128]{2,1,0:T(8,128)S(1)} %fusion.30, bf16[32,32,512]{2,1,0:T(8,128)(2,1)S(1)} %copy-done, bf16[32,128,512]{2,1,0:T(8,128)(2,1)} %param.13, pred[32,128]{1,0:T(8,128)(4,1)S(1)} %iota_compare_fusion.4), kind=kOutput, calls=%fused_computation.6 | convolution fusion | flops 134610944 | bytes 6295552 | tf_op jit(solution)/shard_map/rhl,rpl->rhp/dot_general | solution.py:20
  30.7 5.5 %convolution_convert_fusion = bf16[32,32,512]{2,1,0:T(8,128)(2,1)} fusion(bf16[32,128,512]{2,1,0:T(8,128)(2,1)} %param.13, f32[32,32]{1,0:T(8,128)S(1)} %fusion.29, f32[32,32,128]{2,1,0:T(8,128)} %copy-done.5), kind=kOutput, calls=%fused_computation.1 | convolution fusion | flops 135136384 | bytes 5771264 | tf_op jit(solution)/shard_map/rhp,rpl->rhl/dot_general | solution.py:32
  36.3 5.7 %all-to-all-done = bf16[64,8,896]{2,1,0:T(8,128)(2,1)} async-done(((bf16[64,8,896]{2,1,0:T(8,128)(2,1)}), bf16[64,8,896]{2,1,0:T(8,128)(2,1)}, u32[]{:S(2)}, u32[]{:S(2)}) %all-to-all-start) | async-done | bytes 917536 | tf_op jit(solution)/shard_map/all_to_all | solution.py:370
  42.0 1.2 fusion.27
  43.2 1.4 %collective-permute-start = (bf16[256,896]{1,0:T(8,128)(2,1)S(1)}, bf16[256,896]{1,0:T(8,128)(2,1)S(1)}, u32[]{:S(2)}, u32[]{:S(2)}) collective-permute-start(bf16[256,896]{1,0:T(8,128)(2,1)S(1)} %get-tuple-element.39.refs_0_), channel_id=1, source_target_pairs={{0,1},{1,2},{2,3},{3,0},{4,5},{5,6},{6,7},{7,4},{8,9},{9,10},{10,1... | collective-permute-start | bytes 1376264 | tf_op jit(solution)/shard_map/ppermute | solution.py:364
  44.6 1.5 %collective-permute-start.2 = (bf16[256,896]{1,0:T(8,128)(2,1)S(1)}, bf16[256,896]{1,0:T(8,128)(2,1)S(1)}, u32[]{:S(2)}, u32[]{:S(2)}) collective-permute-start(bf16[256,896]{1,0:T(8,128)(2,1)S(1)} %get-tuple-element.38.refs_1_), channel_id=1, source_target_pairs={{0,3},{1,0},{2,1},{3,2},{4,7},{5,4},{6,5},{7,6},{8,11},{9,8},{10,9... | collective-permute-start | bytes 1376264 | tf_op jit(solution)/shard_map/ppermute | solution.py:364
  46.2 1.5 %copy-done.2 = bf16[1,3584,256]{2,1,0:T(8,128)(2,1)S(1)} copy-done((bf16[1,3584,256]{2,1,0:T(8,128)(2,1)S(1)}, bf16[1,3584,256]{2,1,0:T(8,128)(2,1)}, u32[]{:S(2)}) %copy-start.2) | copy-done | bytes 1835032
  48.8 2.7 %collective-permute-start.11 = (bf16[256,896]{1,0:T(8,128)(2,1)S(1)}, bf16[256,896]{1,0:T(8,128)(2,1)S(1)}, u32[]{:S(2)}, u32[]{:S(2)}) collective-permute-start(bf16[256,896]{1,0:T(8,128)(2,1)S(1)} %get-tuple-element.39.refs_0_), channel_id=1, source_target_pairs={{0,3},{1,0},{2,1},{3,2},{4,7},{5,4},{6,5},{7,6},{8,11},{9,8},{10,9... | collective-permute-start | bytes 1376264 | tf_op jit(solution)/shard_map/ppermute | solution.py:364
  51.5 5.0 %collective-permute-done.refs_0_ = bf16[256,896]{1,0:T(8,128)(2,1)S(1)} collective-permute-done((bf16[256,896]{1,0:T(8,128)(2,1)S(1)}, bf16[256,896]{1,0:T(8,128)(2,1)S(1)}, u32[]{:S(2)}, u32[]{:S(2)}) %collective-permute-start) | collective-permute-done | bytes 458784 | tf_op jit(solution)/shard_map/ppermute | solution.py:364
  56.4 2.7 %collective-permute-start.3 = (bf16[256,896]{1,0:T(8,128)(2,1)S(1)}, bf16[256,896]{1,0:T(8,128)(2,1)S(1)}, u32[]{:S(2)}, u32[]{:S(2)}) collective-permute-start(bf16[256,896]{1,0:T(8,128)(2,1)S(1)} %collective-permute-done.2.refs_3_), channel_id=1, source_target_pairs={{0,3},{1,0},{2,1},{3,2},{4,7},{5,4},{6,5},{7,6},{8,11},{9,8},{10,9... | collective-permute-start | bytes 1376264 | tf_op jit(solution)/shard_map/ppermute | solution.py:364
  59.1 7.1 %collective-permute-done.10.refs_1_ = bf16[256,896]{1,0:T(8,128)(2,1)S(1)} collective-permute-done((bf16[256,896]{1,0:T(8,128)(2,1)S(1)}, bf16[256,896]{1,0:T(8,128)(2,1)S(1)}, u32[]{:S(2)}, u32[]{:S(2)}) %collective-permute-start.10) | collective-permute-done | bytes 458784 | tf_op jit(solution)/shard_map/ppermute | solution.py:364
  66.3 1.7 %shard_map.125 = bf16[256,256]{1,0:T(8,128)(2,1)S(1)} custom-call(bf16[256,896]{1,0:T(8,128)(2,1)S(1)} %collective-permute-done.refs_0_, bf16[256,896]{1,0:T(8,128)(2,1)S(1)} %collective-permute-done.10.refs_1_, bf16[256,896]{1,0:T(8,128)(2,1)S(1)} %collective-permute-done.11.refs_2_, bf16[256,896]{1,0:T(8,128)(2,1)S(1)} %collective-permute-done.2.refs_3_, ...), custom_call_target="tpu_custom_call" | custom-call | flops 939524096 | bytes 5505024 | tf_op jit(solution)/shard_map/pallas_call | solution.py:128
  68.9 2.8 %collective-permute-start.13 = (bf16[384,256]{1,0:T(8,128)(2,1)S(1)}, bf16[384,256]{1,0:T(8,128)(2,1)S(1)}, u32[]{:S(2)}, u32[]{:S(2)}) collective-permute-start(bf16[384,256]{1,0:T(8,128)(2,1)S(1)} %constant_dynamic-update-slice_fusion.refs_0_), channel_id=1, source_target_pairs={{0,2},{1,3},{2,0},{3,1},{4,6},{5,7},{6,4},{7,5},{8,10},{9,11},{10,... | collective-permute-start | bytes 589832 | tf_op jit(solution)/shard_map/ppermute | solution.py:364
  72.3 1.5 %shard_map.126.refs_4_ = bf16[1024,896]{1,0:T(8,128)(2,1)S(1)} custom-call(bf16[272,896]{1,0:T(8,128)(2,1)S(1)} %get-tuple-element.53.refs_0_, bf16[272,896]{1,0:T(8,128)(2,1)} %collective-permute-done.7.refs_1_, bf16[272,896]{1,0:T(8,128)(2,1)} %collective-permute-done.8.refs_2_, bf16[272,896]{1,0:T(8,128)(2,1)} %collective-permute-done.9.refs_3_), custom_call_target="tpu_custom_call" | custom-call | bytes 3670016 | tf_op jit(solution)/shard_map/pallas_call | solution.py:152
  73.8 2.3 %collective-permute-done.1.refs_0_ = bf16[256,896]{1,0:T(8,128)(2,1)S(1)} collective-permute-done((bf16[256,896]{1,0:T(8,128)(2,1)S(1)}, bf16[256,896]{1,0:T(8,128)(2,1)S(1)}, u32[]{:S(2)}, u32[]{:S(2)}) %collective-permute-start.1) | collective-permute-done | bytes 458784 | tf_op jit(solution)/shard_map/ppermute | solution.py:364
  78.0 3.3 %collective-permute-start.5 = (bf16[128,256]{1,0:T(8,128)(2,1)S(1)}, bf16[128,256]{1,0:T(8,128)(2,1)S(1)}, u32[]{:S(2)}, u32[]{:S(2)}) collective-permute-start(bf16[128,256]{1,0:T(8,128)(2,1)S(1)} %shard_map.123.refs_0_), channel_id=1, source_target_pairs={{0,2},{1,3},{2,0},{3,1},{4,6},{5,7},{6,4},{7,5},{8,10},{9,11},{10,... | collective-permute-start | bytes 196616 | tf_op jit(solution)/shard_map/ppermute | solution.py:364
  81.7 3.9 %collective-permute-done.13.refs_2_ = bf16[384,256]{1,0:T(8,128)(2,1)S(1)} collective-permute-done((bf16[384,256]{1,0:T(8,128)(2,1)S(1)}, bf16[384,256]{1,0:T(8,128)(2,1)S(1)}, u32[]{:S(2)}, u32[]{:S(2)}) %collective-permute-start.13) | collective-permute-done | bytes 196640 | tf_op jit(solution)/shard_map/ppermute | solution.py:364
  87.5 1.6 %shard_map.128 = bf16[512,896]{1,0:T(8,128)(2,1)} custom-call(bf16[128,256]{1,0:T(8,128)(2,1)S(1)} %shard_map.123.refs_0_, bf16[128,256]{1,0:T(8,128)(2,1)S(1)} %collective-permute-done.4.refs_1_, bf16[128,256]{1,0:T(8,128)(2,1)S(1)} %collective-permute-done.5.refs_2_, bf16[128,256]{1,0:T(8,128)(2,1)S(1)} %collective-permute-done.6.refs_3_, ...), custom_call_target="tpu_custom_call" | custom-call | flops 704643072 | bytes 2752512 | tf_op jit(solution)/shard_map/pallas_call | solution.py:229
  89.2 10.6 %all-to-all-start.1 = ((bf16[64,8,896]{2,1,0:T(8,128)(2,1)}), bf16[64,8,896]{2,1,0:T(8,128)(2,1)S(1)}, u32[]{:S(2)}, u32[]{:S(2)}) async-start(bf16[64,8,896]{2,1,0:T(8,128)(2,1)} %bitcast.8), calls=%async_computation.1 | async-start | bytes 1835008 | tf_op jit(solution)/shard_map/all_to_all | solution.py:422
  100.7 2.1 %collective-permute-start.16 = (bf16[8,32,512]{2,1,0:T(8,128)(2,1)}, bf16[8,32,512]{2,1,0:T(8,128)(2,1)S(1)}, u32[]{:S(2)}, u32[]{:S(2)}) collective-permute-start(bf16[8,32,512]{2,1,0:T(8,128)(2,1)} %get-tuple-element.69), channel_id=1, source_target_pairs={{0,2},{1,3},{2,0},{3,1},{4,6},{5,7},{6,4},{7,5},{8,10},{9,11},{10,... | collective-permute-start | bytes 786440 | tf_op jit(solution)/shard_map/ppermute | solution.py:364
  102.8 1.2 collective-permute-start.17
  105.1 5.1 %collective-permute-done.15 = bf16[8,32,512]{2,1,0:T(8,128)(2,1)} collective-permute-done((bf16[8,32,512]{2,1,0:T(8,128)(2,1)}, bf16[8,32,512]{2,1,0:T(8,128)(2,1)}, u32[]{:S(2)}, u32[]{:S(2)}) %collective-permute-start.15) | collective-permute-done | bytes 262176 | tf_op jit(solution)/shard_map/ppermute | solution.py:364
  111.2 3.5 %collective-permute-done.16 = bf16[8,32,512]{2,1,0:T(8,128)(2,1)S(1)} collective-permute-done((bf16[8,32,512]{2,1,0:T(8,128)(2,1)}, bf16[8,32,512]{2,1,0:T(8,128)(2,1)S(1)}, u32[]{:S(2)}, u32[]{:S(2)}) %collective-permute-start.16) | collective-permute-done | bytes 262176 | tf_op jit(solution)/shard_map/ppermute | solution.py:364
  114.7 1.1 copy.13
  116.5 9.0 %all-to-all-done.1 = bf16[64,8,896]{2,1,0:T(8,128)(2,1)S(1)} async-done(((bf16[64,8,896]{2,1,0:T(8,128)(2,1)}), bf16[64,8,896]{2,1,0:T(8,128)(2,1)S(1)}, u32[]{:S(2)}, u32[]{:S(2)}) %all-to-all-start.1) | async-done | bytes 917536 | tf_op jit(solution)/shard_map/all_to_all | solution.py:422
  128.5 2.4 %collective-permute-done.19.refs_2_ = bf16[8,896]{1,0:T(8,128)(2,1)S(1)} collective-permute-done((bf16[8,896]{1,0:T(8,128)(2,1)S(1)}, bf16[8,896]{1,0:T(8,128)(2,1)S(1)}, u32[]{:S(2)}, u32[]{:S(2)}) %collective-permute-start.19) | collective-permute-done | bytes 14368 | tf_op jit(solution)/shard_map/ppermute | solution.py:364
  (65 shorter events, 18.5 us)
Async XLA Ops:
  0.6 25.2 %copy-start = (bf16[32,32,512]{2,1,0:T(8,128)(2,1)S(1)}, bf16[32,32,512]{2,1,0:T(8,128)(2,1)}, u32[]{:S(2)}) copy-start(bf16[32,32,512]{2,1,0:T(8,128)(2,1)} %param.11) | copy-start | bytes 3145732
  0.6 17.2 %copy-start.6 = (bf16[1,256,3584]{2,1,0:T(8,128)(2,1)S(1)}, bf16[1,256,3584]{2,1,0:T(8,128)(2,1)}, u32[]{:S(2)}) copy-start(bf16[1,256,3584]{2,1,0:T(8,128)(2,1)} %param.21) | copy-start | bytes 5505028
  3.1 38.9 %all-to-all-start = ((bf16[64,8,896]{2,1,0:T(8,128)(2,1)}), bf16[64,8,896]{2,1,0:T(8,128)(2,1)}, u32[]{:S(2)}, u32[]{:S(2)}) async-start(bf16[64,8,896]{2,1,0:T(8,128)(2,1)} %bitcast.40), calls=%async_computation | async-start | bytes 1835008 | tf_op jit(solution)/shard_map/all_to_all | solution.py:370
  16.3 7.9 %copy-start.7 = (bf16[32,2048]{1,0:T(8,128)(2,1)S(1)}, bf16[32,2048]{1,0:T(8,128)(2,1)}, u32[]{:S(2)}) copy-start(bf16[32,2048]{1,0:T(8,128)(2,1)} %param.12) | copy-start | bytes 393220
  16.3 8.2 %copy-start.8 = (s32[32]{0:T(128)S(1)}, s32[32]{0:T(128)}, u32[]{:S(2)}) copy-start(s32[32]{0:T(128)} %param.15) | copy-start | bytes 388
  19.2 29.5 %collective-permute-start.7 = (bf16[272,896]{1,0:T(8,128)(2,1)}, bf16[272,896]{1,0:T(8,128)(2,1)}, u32[]{:S(2)}, u32[]{:S(2)}) collective-permute-start(bf16[272,896]{1,0:T(8,128)(2,1)} %get-tuple-element.74), channel_id=1, source_target_pairs={{0,1},{1,2},{2,3},{3,0},{4,5},{5,6},{6,7},{7,4},{8,9},{9,10},{10,1... | collective-permute-start | bytes 1462280 | tf_op jit(solution)/shard_map/ppermute | solution.py:364
  20.5 28.2 %collective-permute-start.8 = (bf16[272,896]{1,0:T(8,128)(2,1)}, bf16[272,896]{1,0:T(8,128)(2,1)}, u32[]{:S(2)}, u32[]{:S(2)}) collective-permute-start(bf16[272,896]{1,0:T(8,128)(2,1)} %get-tuple-element.75), channel_id=1, source_target_pairs={{0,2},{1,3},{2,0},{3,1},{4,6},{5,7},{6,4},{7,5},{8,10},{9,11},{10,... | collective-permute-start | bytes 1462280 | tf_op jit(solution)/shard_map/ppermute | solution.py:364
  23.1 25.6 %collective-permute-start.9 = (bf16[272,896]{1,0:T(8,128)(2,1)}, bf16[272,896]{1,0:T(8,128)(2,1)}, u32[]{:S(2)}, u32[]{:S(2)}) collective-permute-start(bf16[272,896]{1,0:T(8,128)(2,1)} %get-tuple-element.73), channel_id=1, source_target_pairs={{0,3},{1,0},{2,1},{3,2},{4,7},{5,4},{6,5},{7,6},{8,11},{9,8},{10,9... | collective-permute-start | bytes 1462280 | tf_op jit(solution)/shard_map/ppermute | solution.py:364
  29.6 0.8 copy-start.5
  30.4 15.8 %copy-start.1 = (bf16[1,3584,256]{2,1,0:T(8,128)(2,1)S(1)}, bf16[1,3584,256]{2,1,0:T(8,128)(2,1)}, u32[]{:S(2)}) copy-start(bf16[1,3584,256]{2,1,0:T(8,128)(2,1)} %param.19) | copy-start | bytes 5505028
  43.2 13.2 %collective-permute-start = (bf16[256,896]{1,0:T(8,128)(2,1)S(1)}, bf16[256,896]{1,0:T(8,128)(2,1)S(1)}, u32[]{:S(2)}, u32[]{:S(2)}) collective-permute-start(bf16[256,896]{1,0:T(8,128)(2,1)S(1)} %get-tuple-element.39.refs_0_), channel_id=1, source_target_pairs={{0,1},{1,2},{2,3},{3,0},{4,5},{5,6},{6,7},{7,4},{8,9},{9,10},{10,1... | collective-permute-start | bytes 1376264 | tf_op jit(solution)/shard_map/ppermute | solution.py:364
  44.6 11.9 %collective-permute-start.2 = (bf16[256,896]{1,0:T(8,128)(2,1)S(1)}, bf16[256,896]{1,0:T(8,128)(2,1)S(1)}, u32[]{:S(2)}, u32[]{:S(2)}) collective-permute-start(bf16[256,896]{1,0:T(8,128)(2,1)S(1)} %get-tuple-element.38.refs_1_), channel_id=1, source_target_pairs={{0,3},{1,0},{2,1},{3,2},{4,7},{5,4},{6,5},{7,6},{8,11},{9,8},{10,9... | collective-permute-start | bytes 1376264 | tf_op jit(solution)/shard_map/ppermute | solution.py:364
  46.2 1.5 %copy-start.2 = (bf16[1,3584,256]{2,1,0:T(8,128)(2,1)S(1)}, bf16[1,3584,256]{2,1,0:T(8,128)(2,1)}, u32[]{:S(2)}) copy-start(bf16[1,3584,256]{2,1,0:T(8,128)(2,1)} %param.20) | copy-start | bytes 5505028
  48.7 17.5 %collective-permute-start.10 = (bf16[256,896]{1,0:T(8,128)(2,1)S(1)}, bf16[256,896]{1,0:T(8,128)(2,1)S(1)}, u32[]{:S(2)}, u32[]{:S(2)}) collective-permute-start(bf16[256,896]{1,0:T(8,128)(2,1)S(1)} %get-tuple-element.38.refs_1_), channel_id=1, source_target_pairs={{0,1},{1,2},{2,3},{3,0},{4,5},{5,6},{6,7},{7,4},{8,9},{9,10},{10,1... | collective-permute-start | bytes 1376264 | tf_op jit(solution)/shard_map/ppermute | solution.py:364
  48.8 17.5 %collective-permute-start.11 = (bf16[256,896]{1,0:T(8,128)(2,1)S(1)}, bf16[256,896]{1,0:T(8,128)(2,1)S(1)}, u32[]{:S(2)}, u32[]{:S(2)}) collective-permute-start(bf16[256,896]{1,0:T(8,128)(2,1)S(1)} %get-tuple-element.39.refs_0_), channel_id=1, source_target_pairs={{0,3},{1,0},{2,1},{3,2},{4,7},{5,4},{6,5},{7,6},{8,11},{9,8},{10,9... | collective-permute-start | bytes 1376264 | tf_op jit(solution)/shard_map/ppermute | solution.py:364
  56.4 19.7 %collective-permute-start.1 = (bf16[256,896]{1,0:T(8,128)(2,1)S(1)}, bf16[256,896]{1,0:T(8,128)(2,1)S(1)}, u32[]{:S(2)}, u32[]{:S(2)}) collective-permute-start(bf16[256,896]{1,0:T(8,128)(2,1)S(1)} %collective-permute-done.refs_0_), channel_id=1, source_target_pairs={{0,1},{1,2},{2,3},{3,0},{4,5},{5,6},{6,7},{7,4},{8,9},{9,10},{10,1... | collective-permute-start | bytes 1376264 | tf_op jit(solution)/shard_map/ppermute | solution.py:364
  56.4 19.7 %collective-permute-start.3 = (bf16[256,896]{1,0:T(8,128)(2,1)S(1)}, bf16[256,896]{1,0:T(8,128)(2,1)S(1)}, u32[]{:S(2)}, u32[]{:S(2)}) collective-permute-start(bf16[256,896]{1,0:T(8,128)(2,1)S(1)} %collective-permute-done.2.refs_3_), channel_id=1, source_target_pairs={{0,3},{1,0},{2,1},{3,2},{4,7},{5,4},{6,5},{7,6},{8,11},{9,8},{10,9... | collective-permute-start | bytes 1376264 | tf_op jit(solution)/shard_map/ppermute | solution.py:364
  59.1 17.0 %copy-start.3 = (bf16[1,3584,256]{2,1,0:T(8,128)(2,1)S(1)}, bf16[1,3584,256]{2,1,0:T(8,128)(2,1)}, u32[]{:S(2)}) copy-start(bf16[1,3584,256]{2,1,0:T(8,128)(2,1)} %param.20) | copy-start | bytes 5505028
  68.0 13.4 %collective-permute-start.12 = (bf16[384,256]{1,0:T(8,128)(2,1)S(1)}, bf16[384,256]{1,0:T(8,128)(2,1)S(1)}, u32[]{:S(2)}, u32[]{:S(2)}) collective-permute-start(bf16[384,256]{1,0:T(8,128)(2,1)S(1)} %constant_dynamic-update-slice_fusion.refs_0_), channel_id=1, source_target_pairs={{0,1},{1,2},{2,3},{3,0},{4,5},{5,6},{6,7},{7,4},{8,9},{9,10},{10,1... | collective-permute-start | bytes 589832 | tf_op jit(solution)/shard_map/ppermute | solution.py:364
  68.9 16.7 %collective-permute-start.13 = (bf16[384,256]{1,0:T(8,128)(2,1)S(1)}, bf16[384,256]{1,0:T(8,128)(2,1)S(1)}, u32[]{:S(2)}, u32[]{:S(2)}) collective-permute-start(bf16[384,256]{1,0:T(8,128)(2,1)S(1)} %constant_dynamic-update-slice_fusion.refs_0_), channel_id=1, source_target_pairs={{0,2},{1,3},{2,0},{3,1},{4,6},{5,7},{6,4},{7,5},{8,10},{9,11},{10,... | collective-permute-start | bytes 589832 | tf_op jit(solution)/shard_map/ppermute | solution.py:364
  71.8 13.9 %collective-permute-start.14 = (bf16[384,256]{1,0:T(8,128)(2,1)S(1)}, bf16[384,256]{1,0:T(8,128)(2,1)S(1)}, u32[]{:S(2)}, u32[]{:S(2)}) collective-permute-start(bf16[384,256]{1,0:T(8,128)(2,1)S(1)} %constant_dynamic-update-slice_fusion.refs_0_), channel_id=1, source_target_pairs={{0,3},{1,0},{2,1},{3,2},{4,7},{5,4},{6,5},{7,6},{8,11},{9,8},{10,9... | collective-permute-start | bytes 589832 | tf_op jit(solution)/shard_map/ppermute | solution.py:364
  77.0 9.6 %collective-permute-start.4 = (bf16[128,256]{1,0:T(8,128)(2,1)S(1)}, bf16[128,256]{1,0:T(8,128)(2,1)S(1)}, u32[]{:S(2)}, u32[]{:S(2)}) collective-permute-start(bf16[128,256]{1,0:T(8,128)(2,1)S(1)} %shard_map.123.refs_0_), channel_id=1, source_target_pairs={{0,1},{1,2},{2,3},{3,0},{4,5},{5,6},{6,7},{7,4},{8,9},{9,10},{10,1... | collective-permute-start | bytes 196616 | tf_op jit(solution)/shard_map/ppermute | solution.py:364
  78.0 9.5 %collective-permute-start.5 = (bf16[128,256]{1,0:T(8,128)(2,1)S(1)}, bf16[128,256]{1,0:T(8,128)(2,1)S(1)}, u32[]{:S(2)}, u32[]{:S(2)}) collective-permute-start(bf16[128,256]{1,0:T(8,128)(2,1)S(1)} %shard_map.123.refs_0_), channel_id=1, source_target_pairs={{0,2},{1,3},{2,0},{3,1},{4,6},{5,7},{6,4},{7,5},{8,10},{9,11},{10,... | collective-permute-start | bytes 196616 | tf_op jit(solution)/shard_map/ppermute | solution.py:364
  81.4 6.1 %collective-permute-start.6 = (bf16[128,256]{1,0:T(8,128)(2,1)S(1)}, bf16[128,256]{1,0:T(8,128)(2,1)S(1)}, u32[]{:S(2)}, u32[]{:S(2)}) collective-permute-start(bf16[128,256]{1,0:T(8,128)(2,1)S(1)} %shard_map.123.refs_0_), channel_id=1, source_target_pairs={{0,3},{1,0},{2,1},{3,2},{4,7},{5,4},{6,5},{7,6},{8,11},{9,8},{10,9... | collective-permute-start | bytes 196616 | tf_op jit(solution)/shard_map/ppermute | solution.py:364
  86.6 13.2 %copy-start.4 = (bf16[32,32,512]{2,1,0:T(8,128)(2,1)S(1)}, bf16[32,32,512]{2,1,0:T(8,128)(2,1)}, u32[]{:S(2)}) copy-start(bf16[32,32,512]{2,1,0:T(8,128)(2,1)} %convolution_convert_fusion) | copy-start | bytes 3145732
  89.2 36.4 %all-to-all-start.1 = ((bf16[64,8,896]{2,1,0:T(8,128)(2,1)}), bf16[64,8,896]{2,1,0:T(8,128)(2,1)S(1)}, u32[]{:S(2)}, u32[]{:S(2)}) async-start(bf16[64,8,896]{2,1,0:T(8,128)(2,1)} %bitcast.8), calls=%async_computation.1 | async-start | bytes 1835008 | tf_op jit(solution)/shard_map/all_to_all | solution.py:422
  100.7 9.5 %collective-permute-start.15 = (bf16[8,32,512]{2,1,0:T(8,128)(2,1)}, bf16[8,32,512]{2,1,0:T(8,128)(2,1)}, u32[]{:S(2)}, u32[]{:S(2)}) collective-permute-start(bf16[8,32,512]{2,1,0:T(8,128)(2,1)} %get-tuple-element.70), channel_id=1, source_target_pairs={{0,1},{1,2},{2,3},{3,0},{4,5},{5,6},{6,7},{7,4},{8,9},{9,10},{10,1... | collective-permute-start | bytes 786440 | tf_op jit(solution)/shard_map/ppermute | solution.py:364
  100.7 14.0 %collective-permute-start.16 = (bf16[8,32,512]{2,1,0:T(8,128)(2,1)}, bf16[8,32,512]{2,1,0:T(8,128)(2,1)S(1)}, u32[]{:S(2)}, u32[]{:S(2)}) collective-permute-start(bf16[8,32,512]{2,1,0:T(8,128)(2,1)} %get-tuple-element.69), channel_id=1, source_target_pairs={{0,2},{1,3},{2,0},{3,1},{4,6},{5,7},{6,4},{7,5},{8,10},{9,11},{10,... | collective-permute-start | bytes 786440 | tf_op jit(solution)/shard_map/ppermute | solution.py:364
  102.8 12.9 %collective-permute-start.17 = (bf16[8,32,512]{2,1,0:T(8,128)(2,1)}, bf16[8,32,512]{2,1,0:T(8,128)(2,1)S(1)}, u32[]{:S(2)}, u32[]{:S(2)}) collective-permute-start(bf16[8,32,512]{2,1,0:T(8,128)(2,1)} %get-tuple-element.68), channel_id=1, source_target_pairs={{0,3},{1,0},{2,1},{3,2},{4,7},{5,4},{6,5},{7,6},{8,11},{9,8},{10,9... | collective-permute-start | bytes 786440 | tf_op jit(solution)/shard_map/ppermute | solution.py:364
  125.8 2.6 %collective-permute-start.18 = (bf16[8,896]{1,0:T(8,128)(2,1)S(1)}, bf16[8,896]{1,0:T(8,128)(2,1)S(1)}, u32[]{:S(2)}, u32[]{:S(2)}) collective-permute-start(bf16[8,896]{1,0:T(8,128)(2,1)S(1)} %get-tuple-element.61), channel_id=1, source_target_pairs={{0,3},{1,0},{2,1},{3,2},{4,7},{5,4},{6,5},{7,6},{8,11},{9,8},{10,9... | collective-permute-start | bytes 43016 | tf_op jit(solution)/shard_map/ppermute | solution.py:364
  126.8 4.1 %collective-permute-start.19 = (bf16[8,896]{1,0:T(8,128)(2,1)S(1)}, bf16[8,896]{1,0:T(8,128)(2,1)S(1)}, u32[]{:S(2)}, u32[]{:S(2)}) collective-permute-start(bf16[8,896]{1,0:T(8,128)(2,1)S(1)} %get-tuple-element.62), channel_id=1, source_target_pairs={{0,2},{1,3},{2,0},{3,1},{4,6},{5,7},{6,4},{7,5},{8,10},{9,11},{10,... | collective-permute-start | bytes 43016 | tf_op jit(solution)/shard_map/ppermute | solution.py:364
  127.2 3.8 %collective-permute-start.20 = (bf16[8,896]{1,0:T(8,128)(2,1)S(1)}, bf16[8,896]{1,0:T(8,128)(2,1)S(1)}, u32[]{:S(2)}, u32[]{:S(2)}) collective-permute-start(bf16[8,896]{1,0:T(8,128)(2,1)S(1)} %get-tuple-element.63), channel_id=1, source_target_pairs={{0,1},{1,2},{2,3},{3,0},{4,5},{5,6},{6,7},{7,4},{8,9},{9,10},{10,1... | collective-permute-start | bytes 43016 | tf_op jit(solution)/shard_map/ppermute | solution.py:364

commit v6 on v5

--- a/solution.py
+++ b/solution.py
@@ -103,7 +103,12 @@
 
 
 def hidden_kernel(count, shares, *refs):
-    halves, (order_ref, gate_ref, up_ref, out_ref, wide) = refs[:count], refs[count:]
+    halves, (order_ref, gate_ref, up_ref), ahead = refs[:count], refs[count : count + 3], refs[count + 3 : -2]
+    out_ref, wide = refs[-2:]
+    first = 0
+    for ref in ahead:
+        first = ref.shape[0]
+        out_ref[pl.ds(0, first), :] = ref[...]
     rows, part = halves[0].shape
     slots = rows // shares
     for h in range(count):
@@ -116,10 +121,12 @@
             ]
     gate = jnp.dot(wide[...], gate_ref[...], preferred_element_type=jnp.float32)
     upper = jnp.dot(wide[...], up_ref[...], preferred_element_type=jnp.float32)
-    out_ref[...] = (gate / (1.0 + jnp.exp(-gate)) * upper).astype(out_ref.dtype)
-
-
-def hidden_units(halves, order, w_gate, w_up):
+    out_ref[pl.ds(first, wide.shape[0]), :] = (gate / (1.0 + jnp.exp(-gate)) * upper).astype(
+        out_ref.dtype
+    )
+
+
+def hidden_units(halves, order, w_gate, w_up, ahead):
     count = len(halves)
     rows, part = halves[0].shape
     width, units = w_gate.shape
@@ -127,8 +134,10 @@
     total = count * rows // shares
     return pl.pallas_call(
         functools.partial(hidden_kernel, count, shares),
-        out_shape=jax.ShapeDtypeStruct((total, units), jnp.bfloat16),
-        in_specs=[whole] * (count + 3),
+        out_shape=jax.ShapeDtypeStruct(
+            (total + sum(v.shape[0] for v in ahead), units), jnp.bfloat16
+        ),
+        in_specs=[whole] * (count + 3 + len(ahead)),
         out_specs=whole,
         scratch_shapes=[pltpu.VMEM((total, width), jnp.bfloat16)],
         compiler_params=vmem_params,
@@ -137,7 +146,7 @@
             bytes_accessed=4 * width * units + 2 * total * width,
             transcendentals=total * units,
         ),
-    )(*halves, order, w_gate, w_up)
+    )(*halves, order, w_gate, w_up, *ahead)
 
 
 def stack_kernel(shares, *refs):
@@ -398,18 +407,17 @@
     source = by_quarter[1] // CAP * (shares * CAP) + by_quarter[0] * CAP + by_quarter[1] % CAP
     sort = (source[:, None] == place[None, :]).astype(bf16)
 
-    def hidden_of(*halves):
-        return hidden_units(halves, sort, w_gate[0], w_up[0])
+    def hidden_of(*halves, ahead=()):
+        return hidden_units(halves, sort, w_gate[0], w_up[0], ahead)
 
     low1, high3 = shift(low, 1), shift(high, 3)
     hidden0 = hidden_of(low, high)
     low, high, hidden0, down = lax.optimization_barrier((low, high, hidden0, down))
     high1, low3 = shift(high, 1), shift(low, 3)
     low2, high2 = shift(low1, 1), shift(high3, 3)
-    hidden13 = hidden_of(low1, high1, low3, high3)
-    hidden13, down = lax.optimization_barrier((hidden13, down))
+    early = hidden_of(low1, high1, low3, high3, ahead=(hidden0,))
+    early, down = lax.optimization_barrier((early, down))
     stacked = stack_shares(down, units)
-    early = jnp.concatenate([hidden0, hidden13], axis=0)
     early = [early] + [shift(early, by) for by in range(1, shares)]
     late = hidden_of(low2, high2)
     late = [late] + [shift(late, by) for by in range(1, shares)]

time: 132 us -> 132 us (level)
  no operation moved by 1% of the time
where the time goes in v6:
time: 132 us
  starting transfers between devices  51.6 us (39%)
  waiting for transfers between devices  45.6 us (35%)
  Pallas kernels  11.9 us (9%)
  matrix products  10.5 us (8%)
  local copies, waits for them, and re-layouts  7.8 us (6%)
  other arithmetic  3.24 us (2%)
    ppermute x21, waiting for transfers between devices, shift(): return lax.ppermute(value, 'tensor', pairs)  30.9 us
    ppermute x21, starting transfers between devices, shift(): return lax.ppermute(value, 'tensor', pairs)  27.8 us
    all_to_all x1, starting transfers between devices, per_device(): lax.all_to_all(packed.reshape(experts, shares * CAP, part), 'expert', spl...  13.2 us
    all_to_all x1, starting transfers between devices, per_device(): lax.all_to_all(expert_out.reshape(experts, shares * CAP, part), 'expert',...  10.6 us
    all_to_all x1, waiting for transfers between devices, per_device(): lax.all_to_all(expert_out.reshape(experts, shares * CAP, part), 'expert',...  9.03 us
    all_to_all x1, waiting for transfers between devices, per_device(): lax.all_to_all(packed.reshape(experts, shares * CAP, part), 'expert', spl...  5.69 us
    dot_general x1, matrix products, attend(): jnp.einsum('rhp,rpl->rhl', weights, cache_latent, preferred_element_type=...  5.52 us
    dot_general x1, matrix products, attend(): jnp.einsum('rhl,rpl->rhp', query_latent, cache_latent, preferred_element_...  3.73 us
  transfers between devices with their start and end apart: 23, of which 12 were waited for; matrix products, arithmetic and copies ran while one was open for 15% of the time, Pallas kernels for 5%

profile of v6, /device:TPU:1, one launch (start us, length us, event | category | flops | bytes accessed | tf_op | source)
XLA Modules:
  0.0 131.7 jit_solution(11155776886389882008)
XLA Ops:
  0.7 2.4 %shard_map.122 = bf16[512,896]{1,0:T(8,128)(2,1)} custom-call(s32[8,8]{1,0:T(8,128)} %routes_ref.1, bf16[8,3584]{1,0:T(8,128)(2,1)} %rows_ref.1), custom_call_target="tpu_custom_call" | custom-call | flops 29360128 | bytes 917504 | tf_op jit(solution)/shard_map/pallas_call | solution.py:87
  3.1 13.2 %all-to-all-start = ((bf16[64,8,896]{2,1,0:T(8,128)(2,1)}), bf16[64,8,896]{2,1,0:T(8,128)(2,1)}, u32[]{:S(2)}, u32[]{:S(2)}) async-start(bf16[64,8,896]{2,1,0:T(8,128)(2,1)} %bitcast.40), calls=%async_computation | async-start | bytes 1835008 | tf_op jit(solution)/shard_map/all_to_all | solution.py:379
  18.0 1.2 pad_maximum_fusion
  19.2 1.3 collective-permute-start.7
  20.5 2.6 %collective-permute-start.8 = (bf16[272,896]{1,0:T(8,128)(2,1)}, bf16[272,896]{1,0:T(8,128)(2,1)}, u32[]{:S(2)}, u32[]{:S(2)}) collective-permute-start(bf16[272,896]{1,0:T(8,128)(2,1)} %get-tuple-element.75), channel_id=1, source_target_pairs={{0,2},{1,3},{2,0},{3,1},{4,6},{5,7},{6,4},{7,5},{8,10},{9,11},{10,... | collective-permute-start | bytes 1462280 | tf_op jit(solution)/shard_map/ppermute | solution.py:373
  24.5 1.3 fusion.30
  25.8 3.7 %fusion.4 = f32[32,32,128]{2,1,0:T(8,128)S(1)} fusion(f32[32,32,128]{2,1,0:T(8,128)S(1)} %fusion.30, bf16[32,32,512]{2,1,0:T(8,128)(2,1)S(1)} %copy-done, bf16[32,128,512]{2,1,0:T(8,128)(2,1)} %param.13, pred[32,128]{1,0:T(8,128)(4,1)S(1)} %iota_compare_fusion.4), kind=kOutput, calls=%fused_computation.6 | convolution fusion | flops 134610944 | bytes 6295552 | tf_op jit(solution)/shard_map/rhl,rpl->rhp/dot_general | solution.py:20
  30.7 5.5 %convolution_convert_fusion = bf16[32,32,512]{2,1,0:T(8,128)(2,1)} fusion(bf16[32,128,512]{2,1,0:T(8,128)(2,1)} %param.13, f32[32,32]{1,0:T(8,128)S(1)} %fusion.29, f32[32,32,128]{2,1,0:T(8,128)} %copy-done.5), kind=kOutput, calls=%fused_computation.1 | convolution fusion | flops 135136384 | bytes 5771264 | tf_op jit(solution)/shard_map/rhp,rpl->rhl/dot_general | solution.py:32
  36.3 5.7 %all-to-all-done = bf16[64,8,896]{2,1,0:T(8,128)(2,1)} async-done(((bf16[64,8,896]{2,1,0:T(8,128)(2,1)}), bf16[64,8,896]{2,1,0:T(8,128)(2,1)}, u32[]{:S(2)}, u32[]{:S(2)}) %all-to-all-start) | async-done | bytes 917536 | tf_op jit(solution)/shard_map/all_to_all | solution.py:379
  42.0 1.2 fusion.27
  43.2 1.4 %collective-permute-start = (bf16[256,896]{1,0:T(8,128)(2,1)S(1)}, bf16[256,896]{1,0:T(8,128)(2,1)S(1)}, u32[]{:S(2)}, u32[]{:S(2)}) collective-permute-start(bf16[256,896]{1,0:T(8,128)(2,1)S(1)} %get-tuple-element.39.refs_0_), channel_id=1, source_target_pairs={{0,1},{1,2},{2,3},{3,0},{4,5},{5,6},{6,7},{7,4},{8,9},{9,10},{10,1... | collective-permute-start | bytes 1376264 | tf_op jit(solution)/shard_map/ppermute | solution.py:373
  44.6 1.5 %collective-permute-start.2 = (bf16[256,896]{1,0:T(8,128)(2,1)S(1)}, bf16[256,896]{1,0:T(8,128)(2,1)S(1)}, u32[]{:S(2)}, u32[]{:S(2)}) collective-permute-start(bf16[256,896]{1,0:T(8,128)(2,1)S(1)} %get-tuple-element.38.refs_1_), channel_id=1, source_target_pairs={{0,3},{1,0},{2,1},{3,2},{4,7},{5,4},{6,5},{7,6},{8,11},{9,8},{10,9... | collective-permute-start | bytes 1376264 | tf_op jit(solution)/shard_map/ppermute | solution.py:373
  46.2 1.5 %copy-done.2 = bf16[1,3584,256]{2,1,0:T(8,128)(2,1)S(1)} copy-done((bf16[1,3584,256]{2,1,0:T(8,128)(2,1)S(1)}, bf16[1,3584,256]{2,1,0:T(8,128)(2,1)}, u32[]{:S(2)}) %copy-start.2) | copy-done | bytes 1835032
  48.8 2.7 %collective-permute-start.11 = (bf16[256,896]{1,0:T(8,128)(2,1)S(1)}, bf16[256,896]{1,0:T(8,128)(2,1)S(1)}, u32[]{:S(2)}, u32[]{:S(2)}) collective-permute-start(bf16[256,896]{1,0:T(8,128)(2,1)S(1)} %get-tuple-element.39.refs_0_), channel_id=1, source_target_pairs={{0,3},{1,0},{2,1},{3,2},{4,7},{5,4},{6,5},{7,6},{8,11},{9,8},{10,9... | collective-permute-start | bytes 1376264 | tf_op jit(solution)/shard_map/ppermute | solution.py:373
  51.5 4.9 %collective-permute-done.refs_0_ = bf16[256,896]{1,0:T(8,128)(2,1)S(1)} collective-permute-done((bf16[256,896]{1,0:T(8,128)(2,1)S(1)}, bf16[256,896]{1,0:T(8,128)(2,1)S(1)}, u32[]{:S(2)}, u32[]{:S(2)}) %collective-permute-start) | collective-permute-done | bytes 458784 | tf_op jit(solution)/shard_map/ppermute | solution.py:373
  56.4 2.7 %collective-permute-start.3 = (bf16[256,896]{1,0:T(8,128)(2,1)S(1)}, bf16[256,896]{1,0:T(8,128)(2,1)S(1)}, u32[]{:S(2)}, u32[]{:S(2)}) collective-permute-start(bf16[256,896]{1,0:T(8,128)(2,1)S(1)} %collective-permute-done.2.refs_3_), channel_id=1, source_target_pairs={{0,3},{1,0},{2,1},{3,2},{4,7},{5,4},{6,5},{7,6},{8,11},{9,8},{10,9... | collective-permute-start | bytes 1376264 | tf_op jit(solution)/shard_map/ppermute | solution.py:373
  59.1 7.1 %collective-permute-done.10.refs_1_ = bf16[256,896]{1,0:T(8,128)(2,1)S(1)} collective-permute-done((bf16[256,896]{1,0:T(8,128)(2,1)S(1)}, bf16[256,896]{1,0:T(8,128)(2,1)S(1)}, u32[]{:S(2)}, u32[]{:S(2)}) %collective-permute-start.10) | collective-permute-done | bytes 458784 | tf_op jit(solution)/shard_map/ppermute | solution.py:373
  66.3 1.7 %shard_map.125.refs_0_ = bf16[384,256]{1,0:T(8,128)(2,1)S(1)} custom-call(bf16[256,896]{1,0:T(8,128)(2,1)S(1)} %collective-permute-done.refs_0_, bf16[256,896]{1,0:T(8,128)(2,1)S(1)} %collective-permute-done.10.refs_1_, bf16[256,896]{1,0:T(8,128)(2,1)S(1)} %collective-permute-done.11.refs_2_, bf16[256,896]{1,0:T(8,128)(2,1)S(1)} %collective-permute-done.2.refs_3_, ...), custom_call_target="tpu_custom_call" | custom-call | flops 939524096 | bytes 5505024 | tf_op jit(solution)/shard_map/pallas_call | solution.py:135
  68.9 2.8 %collective-permute-start.13 = (bf16[384,256]{1,0:T(8,128)(2,1)S(1)}, bf16[384,256]{1,0:T(8,128)(2,1)S(1)}, u32[]{:S(2)}, u32[]{:S(2)}) collective-permute-start(bf16[384,256]{1,0:T(8,128)(2,1)S(1)} %shard_map.125.refs_0_), channel_id=1, source_target_pairs={{0,2},{1,3},{2,0},{3,1},{4,6},{5,7},{6,4},{7,5},{8,10},{9,11},{10,... | collective-permute-start | bytes 589832 | tf_op jit(solution)/shard_map/ppermute | solution.py:373
  72.3 1.5 %shard_map.126.refs_4_ = bf16[1024,896]{1,0:T(8,128)(2,1)S(1)} custom-call(bf16[272,896]{1,0:T(8,128)(2,1)S(1)} %get-tuple-element.53.refs_0_, bf16[272,896]{1,0:T(8,128)(2,1)} %collective-permute-done.7.refs_1_, bf16[272,896]{1,0:T(8,128)(2,1)} %collective-permute-done.8.refs_2_, bf16[272,896]{1,0:T(8,128)(2,1)} %collective-permute-done.9.refs_3_), custom_call_target="tpu_custom_call" | custom-call | bytes 3670016 | tf_op jit(solution)/shard_map/pallas_call | solution.py:161
  73.8 2.3 %collective-permute-done.1.refs_0_ = bf16[256,896]{1,0:T(8,128)(2,1)S(1)} collective-permute-done((bf16[256,896]{1,0:T(8,128)(2,1)S(1)}, bf16[256,896]{1,0:T(8,128)(2,1)S(1)}, u32[]{:S(2)}, u32[]{:S(2)}) %collective-permute-start.1) | collective-permute-done | bytes 458784 | tf_op jit(solution)/shard_map/ppermute | solution.py:373
  78.0 3.3 %collective-permute-start.5 = (bf16[128,256]{1,0:T(8,128)(2,1)S(1)}, bf16[128,256]{1,0:T(8,128)(2,1)S(1)}, u32[]{:S(2)}, u32[]{:S(2)}) collective-permute-start(bf16[128,256]{1,0:T(8,128)(2,1)S(1)} %shard_map.123.refs_0_), channel_id=1, source_target_pairs={{0,2},{1,3},{2,0},{3,1},{4,6},{5,7},{6,4},{7,5},{8,10},{9,11},{10,... | collective-permute-start | bytes 196616 | tf_op jit(solution)/shard_map/ppermute | solution.py:373
  81.7 3.9 %collective-permute-done.13.refs_2_ = bf16[384,256]{1,0:T(8,128)(2,1)S(1)} collective-permute-done((bf16[384,256]{1,0:T(8,128)(2,1)S(1)}, bf16[384,256]{1,0:T(8,128)(2,1)S(1)}, u32[]{:S(2)}, u32[]{:S(2)}) %collective-permute-start.13) | collective-permute-done | bytes 196640 | tf_op jit(solution)/shard_map/ppermute | solution.py:373
  87.5 1.6 %shard_map.128 = bf16[512,896]{1,0:T(8,128)(2,1)} custom-call(bf16[128,256]{1,0:T(8,128)(2,1)S(1)} %shard_map.123.refs_0_, bf16[128,256]{1,0:T(8,128)(2,1)S(1)} %collective-permute-done.4.refs_1_, bf16[128,256]{1,0:T(8,128)(2,1)S(1)} %collective-permute-done.5.refs_2_, bf16[128,256]{1,0:T(8,128)(2,1)S(1)} %collective-permute-done.6.refs_3_, ...), custom_call_target="tpu_custom_call" | custom-call | flops 704643072 | bytes 2752512 | tf_op jit(solution)/shard_map/pallas_call | solution.py:238
  89.2 10.6 %all-to-all-start.1 = ((bf16[64,8,896]{2,1,0:T(8,128)(2,1)}), bf16[64,8,896]{2,1,0:T(8,128)(2,1)S(1)}, u32[]{:S(2)}, u32[]{:S(2)}) async-start(bf16[64,8,896]{2,1,0:T(8,128)(2,1)} %bitcast.8), calls=%async_computation.1 | async-start | bytes 1835008 | tf_op jit(solution)/shard_map/all_to_all | solution.py:430
  100.7 2.1 %collective-permute-start.16 = (bf16[8,32,512]{2,1,0:T(8,128)(2,1)}, bf16[8,32,512]{2,1,0:T(8,128)(2,1)S(1)}, u32[]{:S(2)}, u32[]{:S(2)}) collective-permute-start(bf16[8,32,512]{2,1,0:T(8,128)(2,1)} %get-tuple-element.69), channel_id=1, source_target_pairs={{0,2},{1,3},{2,0},{3,1},{4,6},{5,7},{6,4},{7,5},{8,10},{9,11},{10,... | collective-permute-start | bytes 786440 | tf_op jit(solution)/shard_map/ppermute | solution.py:373
  102.8 1.2 collective-permute-start.17
  105.1 5.1 %collective-permute-done.15 = bf16[8,32,512]{2,1,0:T(8,128)(2,1)} collective-permute-done((bf16[8,32,512]{2,1,0:T(8,128)(2,1)}, bf16[8,32,512]{2,1,0:T(8,128)(2,1)}, u32[]{:S(2)}, u32[]{:S(2)}) %collective-permute-start.15) | collective-permute-done | bytes 262176 | tf_op jit(solution)/shard_map/ppermute | solution.py:373
  111.2 3.5 %collective-permute-done.16 = bf16[8,32,512]{2,1,0:T(8,128)(2,1)S(1)} collective-permute-done((bf16[8,32,512]{2,1,0:T(8,128)(2,1)}, bf16[8,32,512]{2,1,0:T(8,128)(2,1)S(1)}, u32[]{:S(2)}, u32[]{:S(2)}) %collective-permute-start.16) | collective-permute-done | bytes 262176 | tf_op jit(solution)/shard_map/ppermute | solution.py:373
  114.7 1.1 copy.13
  116.5 9.0 %all-to-all-done.1 = bf16[64,8,896]{2,1,0:T(8,128)(2,1)S(1)} async-done(((bf16[64,8,896]{2,1,0:T(8,128)(2,1)}), bf16[64,8,896]{2,1,0:T(8,128)(2,1)S(1)}, u32[]{:S(2)}, u32[]{:S(2)}) %all-to-all-start.1) | async-done | bytes 917536 | tf_op jit(solution)/shard_map/all_to_all | solution.py:430
  128.5 2.4 %collective-permute-done.19.refs_2_ = bf16[8,896]{1,0:T(8,128)(2,1)S(1)} collective-permute-done((bf16[8,896]{1,0:T(8,128)(2,1)S(1)}, bf16[8,896]{1,0:T(8,128)(2,1)S(1)}, u32[]{:S(2)}, u32[]{:S(2)}) %collective-permute-start.19) | collective-permute-done | bytes 14368 | tf_op jit(solution)/shard_map/ppermute | solution.py:373
  (63 shorter events, 18.5 us)
Async XLA Ops:
  0.6 25.2 %copy-start = (bf16[32,32,512]{2,1,0:T(8,128)(2,1)S(1)}, bf16[32,32,512]{2,1,0:T(8,128)(2,1)}, u32[]{:S(2)}) copy-start(bf16[32,32,512]{2,1,0:T(8,128)(2,1)} %param.11) | copy-start | bytes 3145732
  0.6 17.2 %copy-start.6 = (bf16[1,256,3584]{2,1,0:T(8,128)(2,1)S(1)}, bf16[1,256,3584]{2,1,0:T(8,128)(2,1)}, u32[]{:S(2)}) copy-start(bf16[1,256,3584]{2,1,0:T(8,128)(2,1)} %param.21) | copy-start | bytes 5505028
  3.1 38.9 %all-to-all-start = ((bf16[64,8,896]{2,1,0:T(8,128)(2,1)}), bf16[64,8,896]{2,1,0:T(8,128)(2,1)}, u32[]{:S(2)}, u32[]{:S(2)}) async-start(bf16[64,8,896]{2,1,0:T(8,128)(2,1)} %bitcast.40), calls=%async_computation | async-start | bytes 1835008 | tf_op jit(solution)/shard_map/all_to_all | solution.py:379
  16.3 7.9 %copy-start.7 = (bf16[32,2048]{1,0:T(8,128)(2,1)S(1)}, bf16[32,2048]{1,0:T(8,128)(2,1)}, u32[]{:S(2)}) copy-start(bf16[32,2048]{1,0:T(8,128)(2,1)} %param.12) | copy-start | bytes 393220
  16.3 8.2 %copy-start.8 = (s32[32]{0:T(128)S(1)}, s32[32]{0:T(128)}, u32[]{:S(2)}) copy-start(s32[32]{0:T(128)} %param.15) | copy-start | bytes 388
  19.2 29.5 %collective-permute-start.7 = (bf16[272,896]{1,0:T(8,128)(2,1)}, bf16[272,896]{1,0:T(8,128)(2,1)}, u32[]{:S(2)}, u32[]{:S(2)}) collective-permute-start(bf16[272,896]{1,0:T(8,128)(2,1)} %get-tuple-element.74), channel_id=1, source_target_pairs={{0,1},{1,2},{2,3},{3,0},{4,5},{5,6},{6,7},{7,4},{8,9},{9,10},{10,1... | collective-permute-start | bytes 1462280 | tf_op jit(solution)/shard_map/ppermute | solution.py:373
  20.5 28.2 %collective-permute-start.8 = (bf16[272,896]{1,0:T(8,128)(2,1)}, bf16[272,896]{1,0:T(8,128)(2,1)}, u32[]{:S(2)}, u32[]{:S(2)}) collective-permute-start(bf16[272,896]{1,0:T(8,128)(2,1)} %get-tuple-element.75), channel_id=1, source_target_pairs={{0,2},{1,3},{2,0},{3,1},{4,6},{5,7},{6,4},{7,5},{8,10},{9,11},{10,... | collective-permute-start | bytes 1462280 | tf_op jit(solution)/shard_map/ppermute | solution.py:373
  23.1 25.6 %collective-permute-start.9 = (bf16[272,896]{1,0:T(8,128)(2,1)}, bf16[272,896]{1,0:T(8,128)(2,1)}, u32[]{:S(2)}, u32[]{:S(2)}) collective-permute-start(bf16[272,896]{1,0:T(8,128)(2,1)} %get-tuple-element.73), channel_id=1, source_target_pairs={{0,3},{1,0},{2,1},{3,2},{4,7},{5,4},{6,5},{7,6},{8,11},{9,8},{10,9... | collective-permute-start | bytes 1462280 | tf_op jit(solution)/shard_map/ppermute | solution.py:373
  29.6 0.8 copy-start.5
  30.4 15.8 %copy-start.1 = (bf16[1,3584,256]{2,1,0:T(8,128)(2,1)S(1)}, bf16[1,3584,256]{2,1,0:T(8,128)(2,1)}, u32[]{:S(2)}) copy-start(bf16[1,3584,256]{2,1,0:T(8,128)(2,1)} %param.19) | copy-start | bytes 5505028
  43.2 13.2 %collective-permute-start = (bf16[256,896]{1,0:T(8,128)(2,1)S(1)}, bf16[256,896]{1,0:T(8,128)(2,1)S(1)}, u32[]{:S(2)}, u32[]{:S(2)}) collective-permute-start(bf16[256,896]{1,0:T(8,128)(2,1)S(1)} %get-tuple-element.39.refs_0_), channel_id=1, source_target_pairs={{0,1},{1,2},{2,3},{3,0},{4,5},{5,6},{6,7},{7,4},{8,9},{9,10},{10,1... | collective-permute-start | bytes 1376264 | tf_op jit(solution)/shard_map/ppermute | solution.py:373
  44.6 11.9 %collective-permute-start.2 = (bf16[256,896]{1,0:T(8,128)(2,1)S(1)}, bf16[256,896]{1,0:T(8,128)(2,1)S(1)}, u32[]{:S(2)}, u32[]{:S(2)}) collective-permute-start(bf16[256,896]{1,0:T(8,128)(2,1)S(1)} %get-tuple-element.38.refs_1_), channel_id=1, source_target_pairs={{0,3},{1,0},{2,1},{3,2},{4,7},{5,4},{6,5},{7,6},{8,11},{9,8},{10,9... | collective-permute-start | bytes 1376264 | tf_op jit(solution)/shard_map/ppermute | solution.py:373
  46.2 1.5 %copy-start.2 = (bf16[1,3584,256]{2,1,0:T(8,128)(2,1)S(1)}, bf16[1,3584,256]{2,1,0:T(8,128)(2,1)}, u32[]{:S(2)}) copy-start(bf16[1,3584,256]{2,1,0:T(8,128)(2,1)} %param.20) | copy-start | bytes 5505028
  48.7 27.4 %copy-start.3 = (bf16[1,3584,256]{2,1,0:T(8,128)(2,1)S(1)}, bf16[1,3584,256]{2,1,0:T(8,128)(2,1)}, u32[]{:S(2)}) copy-start(bf16[1,3584,256]{2,1,0:T(8,128)(2,1)} %param.20) | copy-start | bytes 5505028
  48.7 17.5 %collective-permute-start.10 = (bf16[256,896]{1,0:T(8,128)(2,1)S(1)}, bf16[256,896]{1,0:T(8,128)(2,1)S(1)}, u32[]{:S(2)}, u32[]{:S(2)}) collective-permute-start(bf16[256,896]{1,0:T(8,128)(2,1)S(1)} %get-tuple-element.38.refs_1_), channel_id=1, source_target_pairs={{0,1},{1,2},{2,3},{3,0},{4,5},{5,6},{6,7},{7,4},{8,9},{9,10},{10,1... | collective-permute-start | bytes 1376264 | tf_op jit(solution)/shard_map/ppermute | solution.py:373
  48.8 17.4 %collective-permute-start.11 = (bf16[256,896]{1,0:T(8,128)(2,1)S(1)}, bf16[256,896]{1,0:T(8,128)(2,1)S(1)}, u32[]{:S(2)}, u32[]{:S(2)}) collective-permute-start(bf16[256,896]{1,0:T(8,128)(2,1)S(1)} %get-tuple-element.39.refs_0_), channel_id=1, source_target_pairs={{0,3},{1,0},{2,1},{3,2},{4,7},{5,4},{6,5},{7,6},{8,11},{9,8},{10,9... | collective-permute-start | bytes 1376264 | tf_op jit(solution)/shard_map/ppermute | solution.py:373
  56.4 19.7 %collective-permute-start.1 = (bf16[256,896]{1,0:T(8,128)(2,1)S(1)}, bf16[256,896]{1,0:T(8,128)(2,1)S(1)}, u32[]{:S(2)}, u32[]{:S(2)}) collective-permute-start(bf16[256,896]{1,0:T(8,128)(2,1)S(1)} %collective-permute-done.refs_0_), channel_id=1, source_target_pairs={{0,1},{1,2},{2,3},{3,0},{4,5},{5,6},{6,7},{7,4},{8,9},{9,10},{10,1... | collective-permute-start | bytes 1376264 | tf_op jit(solution)/shard_map/ppermute | solution.py:373
  56.4 19.7 %collective-permute-start.3 = (bf16[256,896]{1,0:T(8,128)(2,1)S(1)}, bf16[256,896]{1,0:T(8,128)(2,1)S(1)}, u32[]{:S(2)}, u32[]{:S(2)}) collective-permute-start(bf16[256,896]{1,0:T(8,128)(2,1)S(1)} %collective-permute-done.2.refs_3_), channel_id=1, source_target_pairs={{0,3},{1,0},{2,1},{3,2},{4,7},{5,4},{6,5},{7,6},{8,11},{9,8},{10,9... | collective-permute-start | bytes 1376264 | tf_op jit(solution)/shard_map/ppermute | solution.py:373
  67.9 13.4 %collective-permute-start.12 = (bf16[384,256]{1,0:T(8,128)(2,1)S(1)}, bf16[384,256]{1,0:T(8,128)(2,1)S(1)}, u32[]{:S(2)}, u32[]{:S(2)}) collective-permute-start(bf16[384,256]{1,0:T(8,128)(2,1)S(1)} %shard_map.125.refs_0_), channel_id=1, source_target_pairs={{0,1},{1,2},{2,3},{3,0},{4,5},{5,6},{6,7},{7,4},{8,9},{9,10},{10,1... | collective-permute-start | bytes 589832 | tf_op jit(solution)/shard_map/ppermute | solution.py:373
  68.9 16.7 %collective-permute-start.13 = (bf16[384,256]{1,0:T(8,128)(2,1)S(1)}, bf16[384,256]{1,0:T(8,128)(2,1)S(1)}, u32[]{:S(2)}, u32[]{:S(2)}) collective-permute-start(bf16[384,256]{1,0:T(8,128)(2,1)S(1)} %shard_map.125.refs_0_), channel_id=1, source_target_pairs={{0,2},{1,3},{2,0},{3,1},{4,6},{5,7},{6,4},{7,5},{8,10},{9,11},{10,... | collective-permute-start | bytes 589832 | tf_op jit(solution)/shard_map/ppermute | solution.py:373
  71.7 13.9 %collective-permute-start.14 = (bf16[384,256]{1,0:T(8,128)(2,1)S(1)}, bf16[384,256]{1,0:T(8,128)(2,1)S(1)}, u32[]{:S(2)}, u32[]{:S(2)}) collective-permute-start(bf16[384,256]{1,0:T(8,128)(2,1)S(1)} %shard_map.125.refs_0_), channel_id=1, source_target_pairs={{0,3},{1,0},{2,1},{3,2},{4,7},{5,4},{6,5},{7,6},{8,11},{9,8},{10,9... | collective-permute-start | bytes 589832 | tf_op jit(solution)/shard_map/ppermute | solution.py:373
  77.0 9.6 %collective-permute-start.4 = (bf16[128,256]{1,0:T(8,128)(2,1)S(1)}, bf16[128,256]{1,0:T(8,128)(2,1)S(1)}, u32[]{:S(2)}, u32[]{:S(2)}) collective-permute-start(bf16[128,256]{1,0:T(8,128)(2,1)S(1)} %shard_map.123.refs_0_), channel_id=1, source_target_pairs={{0,1},{1,2},{2,3},{3,0},{4,5},{5,6},{6,7},{7,4},{8,9},{9,10},{10,1... | collective-permute-start | bytes 196616 | tf_op jit(solution)/shard_map/ppermute | solution.py:373
  78.0 9.5 %collective-permute-start.5 = (bf16[128,256]{1,0:T(8,128)(2,1)S(1)}, bf16[128,256]{1,0:T(8,128)(2,1)S(1)}, u32[]{:S(2)}, u32[]{:S(2)}) collective-permute-start(bf16[128,256]{1,0:T(8,128)(2,1)S(1)} %shard_map.123.refs_0_), channel_id=1, source_target_pairs={{0,2},{1,3},{2,0},{3,1},{4,6},{5,7},{6,4},{7,5},{8,10},{9,11},{10,... | collective-permute-start | bytes 196616 | tf_op jit(solution)/shard_map/ppermute | solution.py:373
  81.4 6.1 %collective-permute-start.6 = (bf16[128,256]{1,0:T(8,128)(2,1)S(1)}, bf16[128,256]{1,0:T(8,128)(2,1)S(1)}, u32[]{:S(2)}, u32[]{:S(2)}) collective-permute-start(bf16[128,256]{1,0:T(8,128)(2,1)S(1)} %shard_map.123.refs_0_), channel_id=1, source_target_pairs={{0,3},{1,0},{2,1},{3,2},{4,7},{5,4},{6,5},{7,6},{8,11},{9,8},{10,9... | collective-permute-start | bytes 196616 | tf_op jit(solution)/shard_map/ppermute | solution.py:373
  86.6 13.2 %copy-start.4 = (bf16[32,32,512]{2,1,0:T(8,128)(2,1)S(1)}, bf16[32,32,512]{2,1,0:T(8,128)(2,1)}, u32[]{:S(2)}) copy-start(bf16[32,32,512]{2,1,0:T(8,128)(2,1)} %convolution_convert_fusion) | copy-start | bytes 3145732
  89.2 36.4 %all-to-all-start.1 = ((bf16[64,8,896]{2,1,0:T(8,128)(2,1)}), bf16[64,8,896]{2,1,0:T(8,128)(2,1)S(1)}, u32[]{:S(2)}, u32[]{:S(2)}) async-start(bf16[64,8,896]{2,1,0:T(8,128)(2,1)} %bitcast.8), calls=%async_computation.1 | async-start | bytes 1835008 | tf_op jit(solution)/shard_map/all_to_all | solution.py:430
  100.7 9.5 %collective-permute-start.15 = (bf16[8,32,512]{2,1,0:T(8,128)(2,1)}, bf16[8,32,512]{2,1,0:T(8,128)(2,1)}, u32[]{:S(2)}, u32[]{:S(2)}) collective-permute-start(bf16[8,32,512]{2,1,0:T(8,128)(2,1)} %get-tuple-element.70), channel_id=1, source_target_pairs={{0,1},{1,2},{2,3},{3,0},{4,5},{5,6},{6,7},{7,4},{8,9},{9,10},{10,1... | collective-permute-start | bytes 786440 | tf_op jit(solution)/shard_map/ppermute | solution.py:373
  100.7 14.0 %collective-permute-start.16 = (bf16[8,32,512]{2,1,0:T(8,128)(2,1)}, bf16[8,32,512]{2,1,0:T(8,128)(2,1)S(1)}, u32[]{:S(2)}, u32[]{:S(2)}) collective-permute-start(bf16[8,32,512]{2,1,0:T(8,128)(2,1)} %get-tuple-element.69), channel_id=1, source_target_pairs={{0,2},{1,3},{2,0},{3,1},{4,6},{5,7},{6,4},{7,5},{8,10},{9,11},{10,... | collective-permute-start | bytes 786440 | tf_op jit(solution)/shard_map/ppermute | solution.py:373
  102.8 12.9 %collective-permute-start.17 = (bf16[8,32,512]{2,1,0:T(8,128)(2,1)}, bf16[8,32,512]{2,1,0:T(8,128)(2,1)S(1)}, u32[]{:S(2)}, u32[]{:S(2)}) collective-permute-start(bf16[8,32,512]{2,1,0:T(8,128)(2,1)} %get-tuple-element.68), channel_id=1, source_target_pairs={{0,3},{1,0},{2,1},{3,2},{4,7},{5,4},{6,5},{7,6},{8,11},{9,8},{10,9... | collective-permute-start | bytes 786440 | tf_op jit(solution)/shard_map/ppermute | solution.py:373
  125.8 2.6 %collective-permute-start.18 = (bf16[8,896]{1,0:T(8,128)(2,1)S(1)}, bf16[8,896]{1,0:T(8,128)(2,1)S(1)}, u32[]{:S(2)}, u32[]{:S(2)}) collective-permute-start(bf16[8,896]{1,0:T(8,128)(2,1)S(1)} %get-tuple-element.61), channel_id=1, source_target_pairs={{0,3},{1,0},{2,1},{3,2},{4,7},{5,4},{6,5},{7,6},{8,11},{9,8},{10,9... | collective-permute-start | bytes 43016 | tf_op jit(solution)/shard_map/ppermute | solution.py:373
  126.8 4.1 %collective-permute-start.19 = (bf16[8,896]{1,0:T(8,128)(2,1)S(1)}, bf16[8,896]{1,0:T(8,128)(2,1)S(1)}, u32[]{:S(2)}, u32[]{:S(2)}) collective-permute-start(bf16[8,896]{1,0:T(8,128)(2,1)S(1)} %get-tuple-element.62), channel_id=1, source_target_pairs={{0,2},{1,3},{2,0},{3,1},{4,6},{5,7},{6,4},{7,5},{8,10},{9,11},{10,... | collective-permute-start | bytes 43016 | tf_op jit(solution)/shard_map/ppermute | solution.py:373
  127.2 3.8 %collective-permute-start.20 = (bf16[8,896]{1,0:T(8,128)(2,1)S(1)}, bf16[8,896]{1,0:T(8,128)(2,1)S(1)}, u32[]{:S(2)}, u32[]{:S(2)}) collective-permute-start(bf16[8,896]{1,0:T(8,128)(2,1)S(1)} %get-tuple-element.63), channel_id=1, source_target_pairs={{0,1},{1,2},{2,3},{3,0},{4,5},{5,6},{6,7},{7,4},{8,9},{9,10},{10,1... | collective-permute-start | bytes 43016 | tf_op jit(solution)/shard_map/ppermute | solution.py:373
